TPU v7x, 128 devices: a whole 4x4x4 slice. The times are simulated.
128 devices in a mesh: row: 8 (over x, core), col: 16 (over z, y).
Axes of the slice: x: 4, y: 4, z: 4, core: 2. Of those that a mesh axis runs over, the one named last changes fastest.
Arguments:
- object_field: float32 [2, 4096, 8192], P(None, 'row', 'col'), may hold values from -5 to 5
- probe: float32 [4, 2, 256, 256], replicated, may hold values from -4 to 4
- measured: float32 [384, 256, 256], P(('row', 'col')), may hold values from 0.2 to 4
- offsets: int32 [128, 2], replicated, may hold values from 0 to 7936, as said below
- owner: int32 [128], replicated, may hold values from 0 to 15, as said below
Outputs:
- new_object: float32 [2, 4096, 8192], P(None, 'row', 'col')
- new_probe: float32 [4, 2, 256, 256], replicated
Inputs may be any that keep to these rules, and one draw needn't show every extreme that they name: `offsets`: position p's patch corner lies in the tile of device p (numbered row-major over row, col; tiles of 512 x 512 pixels), and the whole 256 x 256 patch lies inside the object. owner[p] names a device in the same mesh row as p's tile. Each device holds at most 3 positions' measurements in its first slots, in order of position; in every mesh row one device holds exactly 3. Other slots are unused.
All inputs are finite; a program needn't handle non-finite values.
Results may differ from a plain program's by a relative error of at most 0.0001.
Values sent between devices are 32-bit elements; how exact they have to be, the bound alone decides.
No kernel may reach another device: no remote copies, remote signals or barrier semaphores. Data moves between devices by JAX's collectives and lax.ppermute only.
A program may use at most 128 MiB of HBM per device.

v0:
```python
import math

import jax
import jax.numpy as jnp
from jax import lax
from jax.sharding import PartitionSpec as P


def passed_along(block, axis, distance):
    devices = range(lax.axis_size(axis))
    route = [(i - distance, i) for i in devices if i - distance in devices]
    return lax.ppermute(block, axis, route)


def right_mult(field, table):
    return jnp.matmul(field, table, precision=lax.Precision.HIGHEST)


def left_mult(table, field):
    return jnp.einsum("ab,...bc->...ac", table, field, precision=lax.Precision.HIGHEST)


def spectrum(real_part, imag_part, cos_table, sin_table):
    half_re = right_mult(real_part, cos_table) + right_mult(imag_part, sin_table)
    half_im = right_mult(imag_part, cos_table) - right_mult(real_part, sin_table)
    full_re = left_mult(cos_table, half_re) + left_mult(sin_table, half_im)
    full_im = left_mult(cos_table, half_im) - left_mult(sin_table, half_re)
    return (full_re, full_im)


def position_work(patches, amps, probe, cos_table, sin_table):
    probe_re = probe[None, :, 0]
    probe_im = probe[None, :, 1]
    patch_re = patches[:, None, 0]
    patch_im = patches[:, None, 1]
    exit_re = probe_re * patch_re - probe_im * patch_im
    exit_im = probe_re * patch_im + probe_im * patch_re
    far_re, far_im = spectrum(exit_re, exit_im, cos_table, sin_table)
    inten = jnp.sum(far_re * far_re + far_im * far_im, axis=1)
    factor = (amps / jnp.maximum(jnp.sqrt(inten), 0.5) - 1.0)[:, None]
    back_re, back_im = spectrum(far_re * factor, far_im * factor, cos_table, -sin_table)
    grad_re = jnp.sum(probe_re * back_re + probe_im * back_im, axis=1)
    grad_im = jnp.sum(probe_re * back_im - probe_im * back_re, axis=1)
    pgrad_re = jnp.sum(patch_re * back_re + patch_im * back_im, axis=0)
    pgrad_im = jnp.sum(patch_re * back_im - patch_im * back_re, axis=0)
    return (jnp.stack([grad_re, grad_im], axis=1), jnp.stack([pgrad_re, pgrad_im], axis=1))


def shards(object_field, probe, measured, offsets, owner):
    size = probe.shape[-1]
    tile = object_field.shape[-1]
    ncols = lax.axis_size("col")
    nrows = lax.axis_size("row")
    my_row = lax.axis_index("row")
    my_col = lax.axis_index("col")
    pos_dev = offsets.shape[0] // (nrows * ncols)
    slots = measured.shape[0]
    per_row = ncols * pos_dev
    highest = lax.Precision.HIGHEST
    index = jnp.arange(size)
    angle = 2.0 * math.pi / size * (index[:, None] * index[None, :] % size).astype(jnp.float32)
    cos_table = jnp.cos(angle) / math.sqrt(size)
    sin_table = jnp.sin(angle) / math.sqrt(size)
    right = passed_along(object_field[:, :, :size], "col", -1)
    widened = jnp.concatenate([object_field, right], axis=2)
    below = passed_along(widened[:, :size, :], "row", -1)
    extended = jnp.concatenate([widened, below], axis=1)
    device = my_row * ncols + my_col
    home_spots = lax.dynamic_slice_in_dim(offsets, device * pos_dev, pos_dev, 0)
    local_row = home_spots[:, 0] - my_row * tile
    local_col = home_spots[:, 1] - my_col * tile
    zero_index = jnp.zeros((), jnp.int32)

    def cut_patch(row_at, col_at):
        return lax.dynamic_slice(extended, (zero_index, row_at, col_at), (2, size, size))

    home_patches = jax.vmap(cut_patch)(local_row, local_col)
    row_owner = lax.dynamic_slice_in_dim(owner, my_row * per_row, per_row, 0)
    mine = (row_owner == my_col).astype(jnp.int32)
    rank = jnp.cumsum(mine) - 1
    slot_of = jnp.where(mine > 0, rank, -1)
    select = (slot_of[None, :] == jnp.arange(slots)[:, None]).astype(jnp.float32)
    part = select
    slot_patches = jnp.einsum(
        "kj,jabc->kabc",
        part,
        lax.all_gather(home_patches, "col", axis=0, tiled=True),
        precision=highest,
    )
    slot_grads, probe_part = position_work(slot_patches, measured, probe, cos_table, sin_table)
    part = select
    home_grads = lax.psum_scatter(
        jnp.einsum("kj,kabc->jabc", part, slot_grads, precision=highest),
        "col",
        scatter_dimension=0,
        tiled=True,
    )
    probe_total = lax.psum(probe_part, ("row", "col"))
    gathered = jnp.zeros((2, tile + size, tile + size), jnp.float32)
    spot = (zero_index, local_row[0], local_col[0])
    gathered = lax.dynamic_update_slice(gathered, home_grads[0], spot)
    from_above = passed_along(gathered[:, tile:, :], "row", 1)
    gathered = gathered.at[:, :size, :].add(from_above)
    from_left = passed_along(gathered[:, :tile, tile:], "col", 1)
    gathered = gathered.at[:, :tile, :size].add(from_left)
    scale = 1.0 / (jnp.max(jnp.sum(probe * probe, axis=(0, 1))) + 1e-05)
    new_object = object_field + gathered[:, :tile, :tile] * scale
    new_probe = probe + probe_total / offsets.shape[0]
    return (new_object, new_probe)


def solution(mesh):
    placed = (P(None, "row", "col"), P(), P(("row", "col"), None, None), P(), P())
    return jax.shard_map(
        shards, mesh=mesh, in_specs=placed, out_specs=(P(None, "row", "col"), P()), check_vma=False
    )
```

profile of v0, /device:TPU:1, one launch (start us, length us, event | category | flops | bytes accessed | tf_op | source)
XLA Modules:
  0.0 550.6 jit_solution(9092885332117091368)
XLA Ops:
  10.2 25.0 %collective-permute-done = f32[2,512,256]{2,1,0:T(8,128)S(1)} collective-permute-done((f32[2,512,256]{2,1,0:T(8,128)S(1)}, f32[2,512,256]{2,1,0:T(8,128)S(1)}, u32[]{:S(2)}, u32[]{:S(2)}) %collective-permute-start) | collective-permute-done | bytes 1048608 | tf_op jit(solution)/shard_map/ppermute | solution.py:12
  43.8 17.7 %collective-permute-done.1 = f32[2,256,768]{2,1,0:T(8,128)} collective-permute-done((f32[2,256,768]{2,1,0:T(8,128)}, f32[2,256,768]{2,1,0:T(8,128)}, u32[]{:S(2)}, u32[]{:S(2)}) %collective-permute-start.1) | collective-permute-done | bytes 1572896 | tf_op jit(solution)/shard_map/ppermute | solution.py:12
  69.7 68.5 %all-gather.3.cloned.1.call-done = f32[32,256,256]{2,1,0:T(8,128)} async-done(((f32[2,256,256]{2,1,0:T(8,128)}), f32[32,256,256]{2,1,0:T(8,128)}) %all-gather.3.cloned.1.call-update) | async-done | bytes 8388624 | tf_op jit(solution)/shard_map/all_gather | solution.py:87
  138.2 10.7 %fusion = f32[3,2,256,256]{3,0,2,1:T(4,128)S(1)} fusion(f32[16,2,256,256]{3,2,1,0:T(8,128)} %bitcast.138, s32[16]{0:T(128)S(1)} %compare_select_fusion), kind=kOutput, calls=%fused_computation | convolution fusion | flops 75497520 | bytes 9961536 | tf_op jit(solution)/shard_map/kj,jabc->kabc/dot_general | solution.py:84
  154.4 8.0 %fusion.12 = f32[3,4,256,256]{3,2,1,0:T(8,128)S(1)} fusion(f32[3,256,256]{1,2,0:T(8,128)} %copy.85, f32[4,256,256]{1,2,0:T(8,128)S(1)} %copy.84, f32[3,256,256]{1,2,0:T(8,128)S(1)} %copy.83, f32[4,256,256]{1,2,0:T(8,128)S(1)} %copy.81), kind=kOutput, calls=%fused_computation.27 | convolution fusion | flops 2419261440 | bytes 6815744 | tf_op jit(solution)/shard_map/dot_general | solution.py:16
  162.4 6.4 %fusion.13 = f32[3,4,256,256]{3,2,1,0:T(8,128)S(1)} fusion(f32[3,256,256]{1,2,0:T(8,128)S(1)} %copy-done.2, f32[4,256,256]{1,2,0:T(8,128)S(1)} %copy.84, f32[3,256,256]{1,2,0:T(8,128)S(1)} %copy.83, f32[4,256,256]{1,2,0:T(8,128)S(1)} %copy.81), kind=kOutput, calls=%fused_computation.28 | convolution fusion | flops 2419261440 | bytes 6815744 | tf_op jit(solution)/shard_map/dot_general | solution.py:16
  168.8 6.6 %fusion.28 = f32[3,4,256,256]{3,2,1,0:T(8,128)S(1)} fusion(f32[3,4,256,256]{3,2,1,0:T(8,128)S(1)} %fusion.12, f32[3,256,256]{1,2,0:T(8,128)S(1)} %copy-done.2, f32[4,256,256]{1,2,0:T(8,128)S(1)} %copy.84, f32[3,256,256]{1,2,0:T(8,128)S(1)} %copy.83, f32[4,256,256]{1,2,0:T(8,128)S(1)} %copy.81), kind=kOutput, calls=%fused_computation.52 | convolution fusion | flops 2420047872 | bytes 9961472 | tf_op jit(solution)/shard_map/dot_general | solution.py:16
  175.4 6.4 %fusion.27 = f32[3,4,256,256]{3,2,1,0:T(8,128)S(1)} fusion(f32[3,4,256,256]{3,2,1,0:T(8,128)S(1)} %fusion.13, f32[3,256,256]{1,2,0:T(8,128)S(1)} %copy-done.2, f32[4,256,256]{1,2,0:T(8,128)S(1)} %copy.84, f32[3,256,256]{1,2,0:T(8,128)S(1)} %copy.83, f32[4,256,256]{1,2,0:T(8,128)S(1)} %copy.81), kind=kOutput, calls=%fused_computation.51 | convolution fusion | flops 2420047872 | bytes 9961472 | tf_op jit(solution)/shard_map/dot_general | solution.py:16
  181.8 6.6 %fusion.72 = f32[3,4,256,256]{3,2,1,0:T(8,128)S(1)} fusion(f32[3,4,256,256]{3,2,1,0:T(8,128)S(1)} %fusion.27), kind=kOutput, calls=%fused_computation.106 | convolution fusion | flops 2416902144 | bytes 6291456 | tf_op jit(solution)/shard_map/ab,...bc->...ac/dot_general | solution.py:20
  188.5 6.2 %fusion.69 = f32[3,4,256,256]{3,2,1,0:T(8,128)S(1)} fusion(f32[3,4,256,256]{3,2,1,0:T(8,128)S(1)} %fusion.28), kind=kOutput, calls=%fused_computation.103 | convolution fusion | flops 2416902144 | bytes 6291456 | tf_op jit(solution)/shard_map/ab,...bc->...ac/dot_general | solution.py:20
  194.6 6.7 %convolution_add_fusion.1 = f32[3,4,256,256]{3,2,1,0:T(8,128)S(1)} fusion(f32[3,4,256,256]{3,2,1,0:T(8,128)S(1)} %fusion.72, f32[3,4,256,256]{3,2,1,0:T(8,128)S(1)} %fusion.28), kind=kOutput, calls=%fused_computation.50 | convolution fusion | flops 2417688576 | bytes 9437184 | tf_op jit(solution)/shard_map/ab,...bc->...ac/dot_general | solution.py:20
  201.3 6.5 %fusion.11 = (f32[3,256,256]{1,2,0:T(8,128)S(1)}, f32[3,4,256,256]{3,2,1,0:T(8,128)S(1)}) fusion(f32[3,4,256,256]{3,2,1,0:T(8,128)S(1)} %convolution_add_fusion.1, f32[3,4,256,256]{3,2,1,0:T(8,128)S(1)} %fusion.69, f32[3,4,256,256]{3,2,1,0:T(8,128)S(1)} %fusion.27), kind=kOutput, calls=%fused_computation.23 | convolution fusion | flops 2420637696 | bytes 13369344 | tf_op jit(solution)/shard_map/ab,...bc->...ac/dot_general | solution.py:20
  208.2 6.4 %fusion.16 = f32[3,4,256,256]{3,2,1,0:T(8,128)S(1)} fusion(f32[3,4,256,256]{3,2,1,0:T(8,128)S(1)} %convolution_add_fusion.1, f32[3,256,256]{1,2,0:T(8,128)S(1)} %divide_add_fusion), kind=kOutput, calls=%fused_computation.32 | convolution fusion | flops 2417754112 | bytes 7077888 | tf_op jit(solution)/shard_map/dot_general | solution.py:16
  214.6 6.2 %fusion.17 = f32[3,4,256,256]{3,2,1,0:T(8,128)S(1)} fusion(f32[3,4,256,256]{3,2,1,0:T(8,128)S(1)} %convolution_add_fusion.1, f32[3,256,256]{1,2,0:T(8,128)S(1)} %divide_add_fusion), kind=kOutput, calls=%fused_computation.33 | convolution fusion | flops 2417688576 | bytes 7077888 | tf_op jit(solution)/shard_map/dot_general | solution.py:16
  220.8 6.5 %fusion.26 = f32[3,4,256,256]{3,2,1,0:T(8,128)S(1)} fusion(f32[3,4,256,256]{3,2,1,0:T(8,128)S(1)} %fusion.16, f32[3,4,256,256]{3,2,1,0:T(8,128)S(1)} %get-tuple-element.54, f32[3,256,256]{1,2,0:T(8,128)S(1)} %divide_add_fusion), kind=kOutput, calls=%fused_computation.46 | convolution fusion | flops 2418475008 | bytes 10223616 | tf_op jit(solution)/shard_map/dot_general | solution.py:16
  227.3 6.3 %fusion.25 = f32[3,4,256,256]{3,2,1,0:T(8,128)S(1)} fusion(f32[3,4,256,256]{3,2,1,0:T(8,128)S(1)} %fusion.17, f32[3,4,256,256]{3,2,1,0:T(8,128)S(1)} %get-tuple-element.54, f32[3,256,256]{1,2,0:T(8,128)S(1)} %divide_add_fusion), kind=kOutput, calls=%fused_computation.45 | convolution fusion | flops 2418540544 | bytes 10223616 | tf_op jit(solution)/shard_map/dot_general | solution.py:16
  233.7 6.6 %fusion.66 = f32[3,4,256,256]{3,2,1,0:T(8,128)S(1)} fusion(f32[3,4,256,256]{3,2,1,0:T(8,128)S(1)} %fusion.25), kind=kOutput, calls=%fused_computation.100 | convolution fusion | flops 2416902144 | bytes 6291456 | tf_op jit(solution)/shard_map/ab,...bc->...ac/dot_general | solution.py:20
  246.4 6.3 %convolution_add_fusion = f32[3,4,256,256]{3,2,1,0:T(8,128)S(1)} fusion(f32[3,4,256,256]{3,2,1,0:T(8,128)S(1)} %fusion.66, f32[3,4,256,256]{3,2,1,0:T(8,128)S(1)} %fusion.26), kind=kOutput, calls=%fused_computation.48 | convolution fusion | flops 2417754112 | bytes 9437184 | tf_op jit(solution)/shard_map/ab,...bc->...ac/dot_general | solution.py:20
  252.8 10.5 %fusion.7 = (f32[4,256,256]{1,2,0:T(8,128)}, f32[4,256,256]{1,2,0:T(8,128)}, f32[3,256,256]{1,2,0:T(8,128)}, f32[3,256,256]{1,2,0:T(8,128)}) fusion(f32[3,4,256,256]{3,2,1,0:T(8,128)S(1)} %convolution_add_fusion, f32[3,256,256]{1,2,0:T(8,128)S(1)} %copy-done.2, f32[3,256,256]{1,2,0:T(8,128)S(1)} %copy.83, f32[4,256,256]{1,2,0:T(8,128)S(1)} %copy.84, ...), kind=kOutput, calls=%fused_computation.13 | convolution fusion | flops 2429419520 | bytes 16777216 | tf_op jit(solution)/shard_map/ab,...bc->...ac/dot_general | solution.py:20
  270.4 8.1 %copy.105 = f32[16,2,256,256]{3,2,1,0:T(8,128)} copy(f32[16,2,256,256]{3,0,2,1:T(8,128)S(1)} %fusion.21) | data formatting | bytes 16777216 | tf_op jit(solution)/shard_map/kj,kabc->jabc/dot_general | solution.py:93
  278.8 83.4 %reduce-scatter.4.cloned.1.call-done = f32[1,2,256,256]{3,2,1,0:T(8,128)} async-done(((f32[16,2,256,256]{3,2,1,0:T(8,128)}), f32[1,2,256,256]{3,2,1,0:T(8,128)}) %reduce-scatter.4.cloned.1.call-update) | async-done | bytes 524304
  364.7 6.7 %dynamic_update_slice.3 = f32[2,768,768]{2,1,0:T(8,128)} dynamic-update-slice(f32[2,768,768]{2,1,0:T(8,128)} %broadcast_in_dim.8, f32[2,256,256]{2,1,0:T(8,128)S(1)} %bitcast.143, s32[]{:T(128)} %constant.105.clone.1, s32[]{:T(128)S(6)} %select_n.65, s32[]{:T(128)S(6)} %select_n.66) | dynamic-update-slice | bytes 1048580 | tf_op jit(solution)/shard_map/dynamic_update_slice | solution.py:101
  380.7 17.5 %collective-permute-done.2 = f32[2,256,768]{2,1,0:T(8,128)} collective-permute-done((f32[2,256,768]{2,1,0:T(8,128)}, f32[2,256,768]{2,1,0:T(8,128)}, u32[]{:S(2)}, u32[]{:S(2)}) %collective-permute-start.2) | collective-permute-done | bytes 1572896 | tf_op jit(solution)/shard_map/ppermute | solution.py:12
  410.8 119.4 %all-reduce.3.cloned.1.call-done = f32[4,2,256,256]{2,3,0,1:T(8,128)} async-done(((f32[4,2,256,256]{2,3,0,1:T(8,128)}), f32[4,2,256,256]{2,3,0,1:T(8,128)}) %all-reduce.3.cloned.1.call-update) | async-done | bytes 2097168 | tf_op jit(solution)/shard_map/psum | solution.py:98
  (74 shorter events, 74.9 us)
Async XLA Ops:
  7.2 34.7 %copy-start = (s32[128,2]{0,1:T(2,128)S(1)}, s32[128,2]{0,1:T(2,128)}, u32[]{:S(2)}) copy-start(s32[128,2]{0,1:T(2,128)} %param.12) | copy-start | bytes 3076
  7.2 2.8 copy-start.6
  7.2 131.0 %all-gather.3.cloned.1.call-start = ((), (), s32[]{:S(2)}) async-start(), calls=%async_computation.2 | async-start | bytes 8912896 | tf_op jit(solution)/shard_map/all_gather | solution.py:87
  8.7 26.5 %collective-permute-start = (f32[2,512,256]{2,1,0:T(8,128)S(1)}, f32[2,512,256]{2,1,0:T(8,128)S(1)}, u32[]{:S(2)}, u32[]{:S(2)}) collective-permute-start(f32[2,512,256]{2,1,0:T(8,128)S(1)} %slice.86), channel_id=1, source_target_pairs={{1,0},{2,1},{3,2},{4,3},{5,4},{6,5},{7,6},{8,7},{9,8},{10,9},{11,1... | collective-permute-start | bytes 3145736 | tf_op jit(solution)/shard_map/ppermute | solution.py:12
  35.3 1.7 copy-start.5
  38.2 25.7 %copy-start.12 = (s32[128]{0:T(128)S(1)}, s32[128]{0:T(128)}, u32[]{:S(2)}) copy-start(s32[128]{0:T(128)} %param.13) | copy-start | bytes 1540
  38.2 25.9 %copy-start.3 = (f32[4,2,256,256]{3,2,1,0:T(8,128)S(1)}, f32[4,2,256,256]{3,2,1,0:T(8,128)}, u32[]{:S(2)}) copy-start(f32[4,2,256,256]{3,2,1,0:T(8,128)} %param.10) | copy-start | bytes 6291460
  38.2 23.3 %collective-permute-start.1 = (f32[2,256,768]{2,1,0:T(8,128)}, f32[2,256,768]{2,1,0:T(8,128)}, u32[]{:S(2)}, u32[]{:S(2)}) collective-permute-start(f32[2,256,768]{2,1,0:T(8,128)} %slice.115), channel_id=1, source_target_pairs={{16,0},{32,16},{48,32},{64,48},{80,64},{96,80},{112,96},{17,1},{33... | collective-permute-start | bytes 4718600 | tf_op jit(solution)/shard_map/ppermute | solution.py:12
  63.8 298.4 %reduce-scatter.4.cloned.1.call-start = ((), (), s32[]{:S(2)}) async-start(), calls=%async_computation.3 | async-start | bytes 8912896
  154.4 8.0 %copy-start.2 = (f32[3,256,256]{1,2,0:T(8,128)S(1)}, f32[3,256,256]{1,2,0:T(8,128)}, u32[]{:S(2)}) copy-start(f32[3,256,256]{1,2,0:T(8,128)} %copy.85) | copy-start | bytes 2359300
  201.3 6.6 %copy-start.10 = (f32[3,256,256]{1,2,0:T(8,128)S(1)}, f32[3,256,256]{1,2,0:T(8,128)}, u32[]{:S(2)}) copy-start(f32[3,256,256]{1,2,0:T(8,128)} %copy.94) | copy-start | bytes 2359300
  278.5 251.6 %all-reduce.3.cloned.1.call-start = ((), (), s32[]{:S(2)}) async-start(), calls=%async_computation.1 | async-start | bytes 4194304 | tf_op jit(solution)/shard_map/psum | solution.py:98
  362.2 2.4 copy-start.11
  364.7 14.4 %copy-start.8 = (f32[4,256,256]{1,2,0:T(8,128)S(1)}, f32[4,256,256]{1,2,0:T(8,128)}, u32[]{:S(2)}) copy-start(f32[4,256,256]{1,2,0:T(8,128)} %get-tuple-element.43) | copy-start | bytes 3145732
  364.7 14.4 %copy-start.9 = (f32[4,256,256]{1,2,0:T(8,128)S(1)}, f32[4,256,256]{1,2,0:T(8,128)}, u32[]{:S(2)}) copy-start(f32[4,256,256]{1,2,0:T(8,128)} %get-tuple-element.44) | copy-start | bytes 3145732
  374.0 24.1 %collective-permute-start.2 = (f32[2,256,768]{2,1,0:T(8,128)}, f32[2,256,768]{2,1,0:T(8,128)}, u32[]{:S(2)}, u32[]{:S(2)}) collective-permute-start(f32[2,256,768]{2,1,0:T(8,128)} %slice.119), channel_id=1, source_target_pairs={{0,16},{16,32},{32,48},{48,64},{64,80},{80,96},{96,112},{1,17},{17... | collective-permute-start | bytes 4718600 | tf_op jit(solution)/shard_map/ppermute | solution.py:12
  380.7 26.1 %copy-start.4 = (f32[4,2,256,256]{3,2,1,0:T(8,128)S(1)}, f32[4,2,256,256]{3,2,1,0:T(8,128)}, u32[]{:S(2)}) copy-start(f32[4,2,256,256]{3,2,1,0:T(8,128)} %param.10) | copy-start | bytes 6291460
  403.7 133.3 %collective-permute-start.3 = (f32[2,512,256]{2,1,0:T(8,128)}, f32[2,512,256]{2,1,0:T(8,128)S(1)}, u32[]{:S(2)}, u32[]{:S(2)}) collective-permute-start(f32[2,512,256]{2,1,0:T(8,128)} %slice.121), channel_id=1, source_target_pairs={{0,1},{1,2},{2,3},{3,4},{4,5},{5,6},{6,7},{7,8},{8,9},{9,10},{10,1... | collective-permute-start | bytes 3145736 | tf_op jit(solution)/shard_map/ppermute | solution.py:12
  534.0 6.2 %copy-start.7 = (f32[2,512,512]{2,1,0:T(8,128)S(1)}, f32[2,512,512]{2,1,0:T(8,128)}, u32[]{:S(2)}) copy-start(f32[2,512,512]{2,1,0:T(8,128)} %param.9) | copy-start | bytes 6291460
  537.0 6.6 %copy-start.1 = (s32[128,2]{0,1:T(2,128)S(1)}, s32[128,2]{0,1:T(2,128)}, u32[]{:S(2)}) copy-start(s32[128,2]{0,1:T(2,128)} %param.12) | copy-start | bytes 3076
Sparse Core Ops, SparseCore 0:
  63.9 74.1 all-gather.2
  278.6 83.5 reduce-scatter.3
  380.8 149.3 all-reduce.2
where the time goes:
time: 561 us; the launch traced here: 551 us
  waiting for transfers between devices  331 us (59%)
  matrix products  123 us (22%)
  local copies, waits for them, and re-layouts  46.4 us (8%)
  other arithmetic  19.7 us (4%)
  between operations  16.5 us (3%)
  starting transfers between devices  13.3 us (2%)
    psum x1, waiting for transfers between devices, shards(): probe_total = lax.psum(probe_part, ('row', 'col'))  119 us
    unnamed x4, waiting for transfers between devices  83.5 us
    all_gather x1, waiting for transfers between devices, shards(): lax.all_gather(home_patches, 'col', axis=0, tiled=True)  68.5 us
    ppermute x4, waiting for transfers between devices, passed_along(): return lax.ppermute(block, axis, route)  60.2 us
    dot_general x8, matrix products, left_mult(): jnp.einsum('ab,...bc->...ac', table, field, precision=lax.Precision.HIGHEST)  55.5 us
    dot_general x8, matrix products, right_mult(): return jnp.matmul(field, table, precision=lax.Precision.HIGHEST)  52.8 us
    ppermute x4, starting transfers between devices, passed_along(): return lax.ppermute(block, axis, route)  13 us
  transfers between devices with their start and end apart: 7, of which 6 were waited for; matrix products, arithmetic and copies ran while one was open for 4% of the time, Pallas kernels for 0%

commit v1 on v0

v1 whole, which is shorter than its diff:
```python
import functools
import math

import jax
import jax.numpy as jnp
import ml_dtypes
import numpy as np
from jax import lax
from jax.experimental import pallas as pl
from jax.experimental.pallas import tpu as pltpu
from jax.sharding import Mesh
from jax.sharding import PartitionSpec as P

W = 256
HALF = 128
TILE = 512
MODES = 4
CAP = 3
NR = 8
NC = 16
ALL = ("x", "core", "z", "y")
COL = ("z", "y")
CHIPS = ("x", "z", "y")
CHUNK = W // NC
BF = jnp.bfloat16
F32 = jnp.float32


def dft_tables():
    n = np.arange(HALF)[:, None]
    q = np.arange(HALF)[None, :]
    out = []
    for k in (2 * q, 2 * q + 1):
        angle = 2.0 * math.pi * ((n * k) % W) / W
        c = np.cos(angle) / math.sqrt(W)
        s = np.sin(angle) / math.sqrt(W)
        m = np.block([[c, -s], [s, c]])
        for t in (m, m.T):
            hi = t.astype(ml_dtypes.bfloat16)
            lo = (t - hi.astype(np.float64)).astype(ml_dtypes.bfloat16)
            out += [hi, lo]
    order = np.concatenate([np.arange(0, W, 2), np.arange(1, W, 2)])
    perm = np.zeros((W, W))
    perm[np.arange(W), order] = 1.0
    out += [perm.astype(ml_dtypes.bfloat16), perm.T.astype(ml_dtypes.bfloat16)]
    return np.stack(out)


def routes():
    up, down, side_in, side_out, swap = [], [], [], [], []
    for r in range(NR):
        for c in range(NC):
            me = r * NC + c
            if r > 0:
                up.append((me, me - NC))
                down.append((me - NC, me))
            if r % 2 == 0:
                other = r * NC + (c - 1) % NC
            else:
                other = r * NC + (c + 1) % NC
            side_in.append((me, other))
            side_out.append((other, me))
            swap.append((me, (r ^ 1) * NC + c))
    return up, down, side_in, side_out, swap


UP, DOWN, SIDE_IN, SIDE_OUT, SWAP = routes()


def coords():
    core = lax.axis_index("core")
    row = lax.axis_index("x") * 2 + core
    col = lax.axis_index("z") * 4 + lax.axis_index("y")
    return row, col, core


def corner(offs, row, col):
    row = (row + NR) % NR
    col = (col + NC) % NC
    p = row * NC + col
    return offs[p, 0] - row * TILE, offs[p, 1] - col * TILE


def iota(shape, dim):
    return lax.broadcasted_iota(jnp.int32, shape, dim)


def send_up_kernel(offs, tile, first, second):
    row, col, core = coords()
    _, c = corner(offs, row - 1, col)
    b = iota((W, W), 1)
    c1 = jnp.where(core == 1, 0, c)
    c2 = jnp.where(core == 1, c, 0)
    for i in range(2):
        left = tile[i, :, :W]
        right = tile[i, :, W:]
        first[i] = jnp.where(b >= c1, left, right)
        second[i] = jnp.where(b >= c2, left, right)


def send_side_kernel(offs, tile, below, out):
    row, col, core = coords()
    _, c = corner(offs, row, col)
    r, _ = corner(offs, row, jnp.where(core == 0, col - 1, col))
    c = jnp.where(core == 0, 0, c)
    a = iota((W, W), 0)
    b = iota((W, W), 1)
    for i in range(2):
        top = jnp.where(b >= c, tile[i, :W, :W], tile[i, :W, W:])
        low = jnp.where(b >= c, tile[i, W:, :W], tile[i, W:, W:])
        out[i] = jnp.where(a >= r, top, jnp.where(a + W >= r, low, below[i]))


def split(x):
    hi = x.astype(BF)
    lo = (x - hi.astype(F32)).astype(BF)
    return hi, lo


def mm(a, b):
    return jnp.dot(a, b, preferred_element_type=F32)


def right(x, hi, lo):
    xh, xl = split(x)
    return mm(xh, hi) + mm(xh, lo) + mm(xl, hi)


def left(hi, lo, x):
    xh, xl = split(x)
    return mm(hi, xh) + mm(lo, xh) + mm(hi, xl)


def forward_kernel(offs, tile, below, side, probe, tables, far, mag, patch, scale):
    row, col, core = coords()
    r, c = corner(offs, row, jnp.where(core == 0, col, col - 1))
    c_own = jnp.where(core == 0, c, 0)
    a = iota((W, W), 0)
    b = iota((W, W), 1)
    beyond = jnp.where(c > b + W, 1, 0)
    use_side = beyond != core
    row_shift = (2 * W - r) % W
    col_shift = (2 * W - c) % W
    for i in range(2):
        top = jnp.where(b >= c_own, tile[i, :W, :W], tile[i, :W, W:])
        low = jnp.where(b >= c_own, tile[i, W:, :W], tile[i, W:, W:])
        own = jnp.where(a >= r, top, jnp.where(a + W >= r, low, below[i]))
        whole = jnp.where(use_side, side[i], own)
        patch[i] = pltpu.roll(pltpu.roll(whole, row_shift, 0), col_shift, 1)
    mag[...] = jnp.zeros((W, W), F32)
    scale[...] = jnp.zeros_like(scale)

    def mode(m, power):
        p_re = probe[m, 0]
        p_im = probe[m, 1]
        o_re = patch[0]
        o_im = patch[1]
        e_re = p_re * o_re - p_im * o_im
        e_im = p_re * o_im + p_im * o_re
        sums = jnp.concatenate([e_re[:, :HALF] + e_re[:, HALF:], e_im[:, :HALF] + e_im[:, HALF:]], axis=1)
        diff = jnp.concatenate([e_re[:, :HALF] - e_re[:, HALF:], e_im[:, :HALF] - e_im[:, HALF:]], axis=1)
        even = right(sums, tables[0], tables[1])
        odd = right(diff, tables[4], tables[5])
        h_re = jnp.concatenate([even[:, :HALF], odd[:, :HALF]], axis=1)
        h_im = jnp.concatenate([even[:, HALF:], odd[:, HALF:]], axis=1)
        sums = jnp.concatenate([h_re[:HALF] + h_re[HALF:], h_im[:HALF] + h_im[HALF:]], axis=0)
        diff = jnp.concatenate([h_re[:HALF] - h_re[HALF:], h_im[:HALF] - h_im[HALF:]], axis=0)
        even = left(tables[2], tables[3], sums)
        odd = left(tables[6], tables[7], diff)
        far[m, 0] = even
        far[m, 1] = odd
        mag[:HALF] += even[:HALF] * even[:HALF] + even[HALF:] * even[HALF:]
        mag[HALF:] += odd[:HALF] * odd[:HALF] + odd[HALF:] * odd[HALF:]
        return power + (p_re * p_re + p_im * p_im)

    power = lax.fori_loop(0, MODES, mode, jnp.zeros((W, W), F32))
    scale[...] = jnp.full(scale.shape, 1.0 / (jnp.max(power) + 1e-05), F32)


def backward_kernel(offs, far, mag, amp, patch, probe, tables, grad, give, keep, factor):
    row, col, core = coords()
    r, c = corner(offs, row, jnp.where(core == 0, col, col - 1))
    x = amp[...]
    perm = tables[8]
    perm_t = tables[9]
    for side in range(2):
        p1 = x.astype(BF)
        rest = x - p1.astype(F32)
        p2 = rest.astype(BF)
        p3 = (rest - p2.astype(F32)).astype(BF)
        if side == 0:
            x = mm(perm, p1) + mm(perm, p2) + mm(perm, p3)
        else:
            x = mm(p1, perm_t) + mm(p2, perm_t) + mm(p3, perm_t)
    factor[...] = x / jnp.maximum(jnp.sqrt(mag[...]), 0.5) - 1.0
    grad[...] = jnp.zeros_like(grad)

    def mode(t, carry):
        m = (t + 2 * (1 - core)) % MODES
        f_even = factor[:HALF]
        f_odd = factor[HALF:]
        even = far[m, 0] * jnp.concatenate([f_even, f_even], axis=0)
        odd = far[m, 1] * jnp.concatenate([f_odd, f_odd], axis=0)
        u = left(tables[0], tables[1], even)
        v = left(tables[4], tables[5], odd)
        h_re = jnp.concatenate([u[:HALF] + v[:HALF], u[:HALF] - v[:HALF]], axis=0)
        h_im = jnp.concatenate([u[HALF:] + v[HALF:], u[HALF:] - v[HALF:]], axis=0)
        u = right(jnp.concatenate([h_re[:, :HALF], h_im[:, :HALF]], axis=1), tables[2], tables[3])
        v = right(jnp.concatenate([h_re[:, HALF:], h_im[:, HALF:]], axis=1), tables[6], tables[7])
        b_re = jnp.concatenate([u[:, :HALF] + v[:, :HALF], u[:, :HALF] - v[:, :HALF]], axis=1)
        b_im = jnp.concatenate([u[:, HALF:] + v[:, HALF:], u[:, HALF:] - v[:, HALF:]], axis=1)
        p_re = probe[m, 0]
        p_im = probe[m, 1]
        o_re = patch[0]
        o_im = patch[1]
        grad[0] += p_re * b_re + p_im * b_im
        grad[1] += p_re * b_im - p_im * b_re
        g_re = o_re * b_re + o_im * b_im
        g_im = o_re * b_im - o_im * b_re

        @pl.when(t < 2)
        def _():
            give[t, 0] = g_re
            give[t, 1] = g_im

        @pl.when(t >= 2)
        def _():
            keep[t - 2, 0] = g_re
            keep[t - 2, 1] = g_im

        return carry

    lax.fori_loop(0, MODES, mode, 0)
    for i in range(2):
        grad[i] = pltpu.roll(pltpu.roll(grad[i], r % W, 0), c % W, 1)


def pick_kernel(owner, slots, out):
    row, col, core = coords()
    base = row * NC
    owners = [owner[base + i] for i in range(NC)]
    index = []
    for i in range(NC):
        rank = jnp.int32(0)
        for q in range(i):
            rank = rank + jnp.where(owners[q] == owners[i], 1, 0)
        index.append(owners[i] * CAP + rank)
    for i in range(NC):
        device = jnp.where(core == 0, i, (i + 1) % NC)
        out[device] = slots[index[i]]


def object_kernel(offs, tile, own, got, above_first, above_second, scale, out):
    row, col, core = coords()
    a = iota((W, W), 0)
    b = iota((W, W), 1)
    s = scale[0, 0]
    r_s, c_s = corner(offs, row, col)
    r_b, c_b = corner(offs, row, col - 1)
    r_as, c_as = corner(offs, row - 1, col)
    r_ab, c_ab = corner(offs, row - 1, col - 1)

    def bands(at, v):
        return [v <= at, jnp.logical_and(v > at, v <= at + W)]

    even = core == 0
    rows_s, cols_s = bands(a, r_s), bands(b, c_s)
    rows_b = bands(a, r_b)
    in_b = c_b > b + W
    cols_as = bands(b, c_as)
    low_as = r_as > a + W
    low_ab = jnp.logical_and(r_ab > a + W, c_ab > b + W)
    for i in range(2):
        g_s = jnp.where(even, own[i], got[i])
        g_b = jnp.where(even, got[i], own[i])
        d_s = jnp.where(even, above_second[i], above_first[i])
        d_b = jnp.where(even, above_first[i], above_second[i])
        for p in range(2):
            for q in range(2):
                total = jnp.where(jnp.logical_and(rows_s[p], cols_s[q]), g_s, 0.0)
                if q == 0:
                    total += jnp.where(jnp.logical_and(rows_b[p], in_b), g_b, 0.0)
                if p == 0:
                    total += jnp.where(jnp.logical_and(low_as, cols_as[q]), d_s, 0.0)
                if p == 0 and q == 0:
                    total += jnp.where(low_ab, d_b, 0.0)
                at = (i, pl.ds(p * W, W), pl.ds(q * W, W))
                out[at] = tile[at] + total * s


SMEM = pl.BlockSpec(memory_space=pltpu.SMEM)
VMEM = pl.BlockSpec(memory_space=pltpu.VMEM)


def call(kernel, outs, ins, *args, flops=0, data=0, scratch=(), mb=40):
    shapes = [jax.ShapeDtypeStruct(s, F32) for s in outs]
    return pl.pallas_call(
        kernel,
        grid=(1,),
        out_shape=shapes,
        in_specs=ins,
        out_specs=[VMEM] * len(outs),
        scratch_shapes=[pltpu.VMEM(s, F32) for s in scratch],
        compiler_params=pltpu.CompilerParams(vmem_limit_bytes=mb * 2**20),
        cost_estimate=pl.CostEstimate(flops=flops, bytes_accessed=data, transcendentals=0),
    )(*args)


def shards(tables, object_field, probe, measured, offsets, owner):
    core = lax.axis_index("core")
    piece = (2, W, W)
    top_spec = pl.BlockSpec((2, W, TILE), lambda i: (0, 0, 0))
    first, second = call(send_up_kernel, [piece, piece], [SMEM, top_spec], offsets, object_field, data=2 << 20)
    below_first = lax.ppermute(first, ALL, UP)
    below_second = lax.ppermute(second, ALL, UP)
    spread = measured.reshape(CAP, NC, CHUNK, W).transpose(1, 0, 2, 3)
    spread = lax.all_to_all(spread, COL, 0, 0, tiled=True)
    side = call(
        send_side_kernel, [piece], [SMEM, VMEM, VMEM], offsets, object_field, below_first, data=3 << 20
    )[0]
    side = lax.ppermute(side, ALL, SIDE_IN)
    picked = call(
        pick_kernel, [(NC, CHUNK, W)], [SMEM, VMEM], owner, spread.reshape(NC * CAP, CHUNK, W), data=1 << 20
    )[0]
    amp = lax.all_to_all(picked, COL, 0, 0, tiled=True).reshape(W, W)
    far, mag, patch, scale = call(
        forward_kernel,
        [(MODES, 2, W, W), (W, W), piece, (8, 128)],
        [SMEM] + [VMEM] * 5,
        offsets, object_field, below_second, side, probe, tables,
        flops=2 * 48 * W**3, data=8 << 20,
    )
    grad, give, keep = call(
        backward_kernel,
        [piece, (2, 2, W, W), (2, 2, W, W)],
        [SMEM] + [VMEM] * 6,
        offsets, far, mag, amp, patch, probe, tables,
        flops=2 * 48 * W**3, data=8 << 20, scratch=[(W, W)],
    )
    taken = lax.ppermute(give, ALL, SWAP)
    got = lax.ppermute(grad, ALL, SIDE_OUT)
    above_first = lax.ppermute(grad, ALL, DOWN)
    mine = (keep + taken).reshape(64, 16, W)
    mine = lax.all_to_all(mine, CHIPS, 0, 0, tiled=True)
    above_second = lax.ppermute(got, ALL, DOWN)
    part = jnp.sum(mine, axis=0)
    mine = lax.all_to_all(jnp.broadcast_to(part[None], (64, 16, W)), CHIPS, 0, 0, tiled=True)
    new_object = call(
        object_kernel,
        [(2, TILE, TILE)],
        [SMEM] + [VMEM] * 6,
        offsets, object_field, grad, got, above_first, above_second, scale,
        data=6 << 20,
    )[0]
    mine = mine.reshape(2, 2, W, W)
    theirs = lax.ppermute(mine, ALL, SWAP)
    total = jnp.concatenate([jnp.where(core == 0, mine, theirs), jnp.where(core == 0, theirs, mine)], axis=0)
    new_probe = probe + total / (NR * NC)
    return (new_object, new_probe)


def solution(mesh):
    inner = Mesh(mesh.devices.reshape(4, 2, 4, 4), ALL)
    tables = dft_tables()
    placed = (P(None, ("x", "core"), COL), P(), P(ALL, None, None), P(), P())

    def whole(*args):
        return shards(jnp.asarray(tables), *args)

    return jax.shard_map(
        whole, mesh=inner, in_specs=placed, out_specs=(P(None, ("x", "core"), COL), P()), check_vma=False
    )
```

time: 561 us -> 143 us (0.25); the launches traced: 551 us -> 142 us
  waiting for transfers between devices: 331 us -> 32.2 us
  matrix products: 123 us -> 0 us
  local copies, waits for them, and re-layouts: 46.4 us -> 15.1 us
  blocking collectives: 0 us -> 27.4 us
  starting transfers between devices: 13.3 us -> 39.3 us
  Pallas kernels: 0 us -> 22.2 us
  between operations: 16.5 us -> 0.86 us
  other arithmetic: 19.7 us -> 4.95 us
    dot_general x18 -> x0, matrix products: 123 us -> none  [the longest x8 55.5 us: left_mult(): jnp.einsum('ab,...bc->...ac', table, field, precision=lax.Precision.HIGHEST)]
    psum x1 -> x0, waiting for transfers between devices: 119 us -> none  [shards(): probe_total = lax.psum(probe_part, ('row', 'col'))]
    unnamed x4 -> x0, waiting for transfers between devices: 83.5 us -> none
    all_gather x1 -> x0, waiting for transfers between devices: 68.5 us -> none  [shards(): lax.all_gather(home_patches, 'col', axis=0, tiled=True)]
    ppermute x4 -> x8, waiting for transfers between devices: 60.2 us -> 9.82 us  [the longest x1 5.62 us: shards(): above_second = lax.ppermute(got, ALL, DOWN)]
    all_to_all x0 -> x1, blocking collectives: none -> 27.4 us  [shards(): mine = lax.all_to_all(mine, CHIPS, 0, 0, tiled=True)]
    all_to_all x0 -> x3, waiting for transfers between devices: none -> 22.3 us  [the longest x1 12.1 us: shards(): lax.all_to_all(jnp.broadcast_to(part[None], (64, 16, W)), CHIPS, 0, 0, ti...]
    pallas_call x0 -> x6, Pallas kernels: none -> 22.2 us  [call(): pl.pallas_call(kernel, grid=(1,), out_shape=shapes, in_specs=ins, out_spe...]
  transfers between devices with their start and end apart: 7 -> 11, of which waited for: 6 -> 5; matrix products, arithmetic and copies ran while one was open for 4% -> 1% of each run, Pallas kernels for 0% -> 10%
where the time goes in v1:
time: 143 us; the launch traced here: 142 us
  starting transfers between devices  39.3 us (27%)
  waiting for transfers between devices  32.2 us (23%)
  blocking collectives  27.4 us (19%)
  Pallas kernels  22.2 us (16%)
  local copies, waits for them, and re-layouts  15.1 us (11%)
  other arithmetic  4.95 us (3%)
    all_to_all x1, blocking collectives, shards(): mine = lax.all_to_all(mine, CHIPS, 0, 0, tiled=True)  27.4 us
    pallas_call x6, Pallas kernels, call(): pl.pallas_call(kernel, grid=(1,), out_shape=shapes, in_specs=ins, out_spe...  22.2 us
    unnamed x37, local copies, waits for them, and re-layouts  13 us
    all_to_all x1, waiting for transfers between devices, shards(): lax.all_to_all(jnp.broadcast_to(part[None], (64, 16, W)), CHIPS, 0, 0, ti...  12.1 us
    all_to_all x1, waiting for transfers between devices, shards(): spread = lax.all_to_all(spread, COL, 0, 0, tiled=True)  10.2 us
    all_to_all x1, starting transfers between devices, shards(): spread = lax.all_to_all(spread, COL, 0, 0, tiled=True)  8.03 us
    all_to_all x1, starting transfers between devices, shards(): lax.all_to_all(jnp.broadcast_to(part[None], (64, 16, W)), CHIPS, 0, 0, ti...  5.88 us
    ppermute x1, waiting for transfers between devices, shards(): above_second = lax.ppermute(got, ALL, DOWN)  5.62 us
  transfers between devices with their start and end apart: 11, of which 5 were waited for; matrix products, arithmetic and copies ran while one was open for 1% of the time, Pallas kernels for 10%

profile of v1, /device:TPU:1, one launch (start us, length us, event | category | flops | bytes accessed | tf_op | source)
XLA Modules:
  0.0 141.9 jit_solution(5018559308019085452)
XLA Ops:
  3.0 2.5 %shard_map.77 = (f32[2,256,256]{2,1,0:T(8,128)}, f32[2,256,256]{2,1,0:T(8,128)S(1)}) custom-call(s32[128,2]{1,0:T(8,128)S(1)} %copy.13.offs, f32[2,512,512]{2,1,0:T(8,128)S(1)} %copy-done), custom_call_target="tpu_custom_call" | custom-call | bytes 2097152 | tf_op jit(solution)/shard_map/pallas_call | solution.py:297
  5.5 3.6 %collective-permute-start.1 = (f32[2,256,256]{2,1,0:T(8,128)}, f32[2,256,256]{2,1,0:T(8,128)}, u32[]{:S(2)}, u32[]{:S(2)}) collective-permute-start(f32[2,256,256]{2,1,0:T(8,128)} %get-tuple-element.12), channel_id=1, source_target_pairs={{16,0},{17,1},{18,2},{19,3},{20,4},{21,5},{22,6},{23,7},{24,8},{25... | collective-permute-start | bytes 1572872 | tf_op jit(solution)/shard_map/ppermute | solution.py:314
  10.0 8.0 %all-to-all-start = ((f32[16,3,16,256]{3,2,1,0:T(8,128)}), f32[16,3,16,256]{3,2,1,0:T(8,128)}, u32[]{:S(2)}, u32[]{:S(2)}) async-start(f32[16,3,16,256]{3,2,1,0:T(8,128)} %bitcast.7), calls=%async_computation | async-start | bytes 1572864 | tf_op jit(solution)/shard_map/all_to_all | solution.py:317
  18.1 2.1 %collective-permute-start = (f32[2,256,256]{2,1,0:T(8,128)}, f32[2,256,256]{2,1,0:T(8,128)}, u32[]{:S(2)}, u32[]{:S(2)}) collective-permute-start(f32[2,256,256]{2,1,0:T(8,128)} %copy-done.16), channel_id=1, source_target_pairs={{16,0},{17,1},{18,2},{19,3},{20,4},{21,5},{22,6},{23,7},{24,8},{25... | collective-permute-start | bytes 1572872 | tf_op jit(solution)/shard_map/ppermute | solution.py:315
  20.2 2.6 %shard_map.78 = f32[2,256,256]{2,1,0:T(8,128)} custom-call(s32[128,2]{1,0:T(8,128)S(1)} %copy.13.offs, f32[2,512,512]{2,1,0:T(8,128)S(1)} %copy-done.1, f32[2,256,256]{2,1,0:T(8,128)} %collective-permute-done.1.below), custom_call_target="tpu_custom_call" | custom-call | bytes 3145728 | tf_op jit(solution)/shard_map/pallas_call | solution.py:297
  24.0 10.2 %all-to-all-done = f32[16,3,16,256]{3,2,1,0:T(8,128)} async-done(((f32[16,3,16,256]{3,2,1,0:T(8,128)}), f32[16,3,16,256]{3,2,1,0:T(8,128)}, u32[]{:S(2)}, u32[]{:S(2)}) %all-to-all-start) | async-done | bytes 786464 | tf_op jit(solution)/shard_map/all_to_all | solution.py:317
  36.3 4.2 %all-to-all-start.1 = ((f32[16,16,256]{2,1,0:T(8,128)}), f32[16,16,256]{2,1,0:T(8,128)}, u32[]{:S(2)}, u32[]{:S(2)}) async-start(f32[16,16,256]{2,1,0:T(8,128)} %copy-done.8), calls=%async_computation.1 | async-start | bytes 524288 | tf_op jit(solution)/shard_map/all_to_all | solution.py:325
  42.1 5.8 %shard_map.79 = (f32[4,2,256,256]{3,2,1,0:T(8,128)S(1)}, f32[256,256]{1,0:T(8,128)S(1)}, f32[2,256,256]{2,1,0:T(8,128)S(1)}, f32[8,128]{1,0:T(8,128)S(1)}) custom-call(s32[128,2]{1,0:T(8,128)S(1)} %copy.13.offs, f32[2,512,512]{2,1,0:T(8,128)S(1)} %copy-done.1, f32[2,256,256]{2,1,0:T(8,128)} %collective-permute-done.below, ...), custom_call_target="tpu_custom_call" | custom-call | flops 1610612736 | bytes 8388608 | tf_op jit(solution)/shard_map/pallas_call | solution.py:297
  50.8 1.6 %copy-done.3 = f32[4,2,256,256]{3,2,1,0:T(8,128)S(1)} copy-done((f32[4,2,256,256]{3,2,1,0:T(8,128)S(1)}, f32[4,2,256,256]{3,2,1,0:T(8,128)}, u32[]{:S(2)}) %copy-start.3) | copy-done | bytes 2097176
  52.4 1.6 %copy-done.7 = f32[4,2,256,256]{3,2,1,0:T(8,128)S(1)} copy-done((f32[4,2,256,256]{3,2,1,0:T(8,128)S(1)}, f32[4,2,256,256]{3,2,1,0:T(8,128)}, u32[]{:S(2)}) %copy-start.7) | copy-done | bytes 2097176
  56.0 5.9 %shard_map.81 = (f32[2,256,256]{2,1,0:T(8,128)S(1)}, f32[2,2,256,256]{3,2,1,0:T(8,128)S(1)}, f32[2,2,256,256]{3,2,1,0:T(8,128)S(1)}) custom-call(s32[128,2]{1,0:T(8,128)S(1)} %copy.13.offs, f32[4,2,256,256]{3,2,1,0:T(8,128)S(1)} %copy-done.7, f32[256,256]{1,0:T(8,128)S(1)} %copy-done.14, f32[256,256]{1,0:T(8,128)} %bitcast.3.amp, ...), custom_call_target="tpu_custom_call" | custom-call | flops 1610612736 | bytes 8388608 | tf_op jit(solution)/shard_map/pallas_call | solution.py:297
  62.6 2.3 %collective-permute-done.6 = f32[2,2,256,256]{3,2,1,0:T(8,128)S(1)} collective-permute-done((f32[2,2,256,256]{3,2,1,0:T(8,128)S(1)}, f32[2,2,256,256]{3,2,1,0:T(8,128)S(1)}, u32[]{:S(2)}, u32[]{:S(2)}) %collective-permute-start.6) | collective-permute-done | bytes 1048608 | tf_op jit(solution)/shard_map/ppermute | solution.py:340
  65.0 27.4 %all_to_all.20 = f32[64,16,256]{2,1,0:T(8,128)} all-to-all(f32[64,16,256]{2,1,0:T(8,128)S(1)} %bitcast.8), channel_id=1, replica_groups=mesh['x'=4,'core'=2,'z'=4,'y'=4] {'x','z','y'}, dimensions={0} | all-to-all | bytes 2097152 | tf_op jit(solution)/shard_map/all_to_all | solution.py:344
  94.9 5.9 %all-to-all-start.3 = ((f32[64,16,256]{2,1,0:T(8,128)}), f32[64,16,256]{2,1,0:T(8,128)}, u32[]{:S(2)}, u32[]{:S(2)}) async-start(f32[64,16,256]{2,1,0:T(8,128)} %broadcast_in_dim.2), calls=%async_computation.3 | async-start | bytes 2097152 | tf_op jit(solution)/shard_map/all_to_all | solution.py:347
  100.8 4.3 %collective-permute-start.3 = (f32[2,256,256]{2,1,0:T(8,128)S(1)}, f32[2,256,256]{2,1,0:T(8,128)S(1)}, u32[]{:S(2)}, u32[]{:S(2)}) collective-permute-start(f32[2,256,256]{2,1,0:T(8,128)S(1)} %copy-done.12), channel_id=1, source_target_pairs={{15,0},{0,1},{1,2},{2,3},{3,4},{4,5},{5,6},{6,7},{7,8},{8,9},{9,10... | collective-permute-start | bytes 1572872 | tf_op jit(solution)/shard_map/ppermute | solution.py:341
  105.1 12.1 %all-to-all-done.3 = f32[64,16,256]{2,1,0:T(8,128)} async-done(((f32[64,16,256]{2,1,0:T(8,128)}), f32[64,16,256]{2,1,0:T(8,128)}, u32[]{:S(2)}, u32[]{:S(2)}) %all-to-all-start.3) | async-done | bytes 1048608 | tf_op jit(solution)/shard_map/all_to_all | solution.py:347
  117.2 3.1 %collective-permute-start.7 = (f32[2,2,256,256]{3,2,1,0:T(8,128)}, f32[2,2,256,256]{3,2,1,0:T(8,128)}, u32[]{:S(2)}, u32[]{:S(2)}) collective-permute-start(f32[2,2,256,256]{3,2,1,0:T(8,128)} %bitcast.5), channel_id=1, source_target_pairs={{0,16},{1,17},{2,18},{3,19},{4,20},{5,21},{6,22},{7,23},{8,24},{9,... | collective-permute-start | bytes 3145736 | tf_op jit(solution)/shard_map/ppermute | solution.py:356
  120.3 1.9 %collective-permute-start.4 = (f32[2,256,256]{2,1,0:T(8,128)S(1)}, f32[2,256,256]{2,1,0:T(8,128)}, u32[]{:S(2)}, u32[]{:S(2)}) collective-permute-start(f32[2,256,256]{2,1,0:T(8,128)S(1)} %copy-done.12), channel_id=1, source_target_pairs={{0,16},{1,17},{2,18},{3,19},{4,20},{5,21},{6,22},{7,23},{8,24},{9,... | collective-permute-start | bytes 1572872 | tf_op jit(solution)/shard_map/ppermute | solution.py:342
  122.2 4.2 %collective-permute-start.5 = (f32[2,256,256]{2,1,0:T(8,128)S(1)}, f32[2,256,256]{2,1,0:T(8,128)}, u32[]{:S(2)}, u32[]{:S(2)}) collective-permute-start(f32[2,256,256]{2,1,0:T(8,128)S(1)} %collective-permute-done.3.got), channel_id=1, source_target_pairs={{0,16},{1,17},{2,18},{3,19},{4,20},{5,21},{6,22},{7,23},{8,24},{9,... | collective-permute-start | bytes 1572872 | tf_op jit(solution)/shard_map/ppermute | solution.py:345
  126.4 1.9 %collective-permute-done.4.above_first = f32[2,256,256]{2,1,0:T(8,128)} collective-permute-done((f32[2,256,256]{2,1,0:T(8,128)S(1)}, f32[2,256,256]{2,1,0:T(8,128)}, u32[]{:S(2)}, u32[]{:S(2)}) %collective-permute-start.4) | collective-permute-done | bytes 524320 | tf_op jit(solution)/shard_map/ppermute | solution.py:342
  128.3 5.6 %collective-permute-done.5.above_second = f32[2,256,256]{2,1,0:T(8,128)} collective-permute-done((f32[2,256,256]{2,1,0:T(8,128)S(1)}, f32[2,256,256]{2,1,0:T(8,128)}, u32[]{:S(2)}, u32[]{:S(2)}) %collective-permute-start.5) | collective-permute-done | bytes 524320 | tf_op jit(solution)/shard_map/ppermute | solution.py:345
  133.9 4.1 %shard_map.82 = f32[2,512,512]{2,1,0:T(8,128)} custom-call(s32[128,2]{1,0:T(8,128)S(1)} %copy.13.offs, f32[2,512,512]{2,1,0:T(8,128)S(1)} %copy-done.1, f32[2,256,256]{2,1,0:T(8,128)S(1)} %copy-done.12, f32[2,256,256]{2,1,0:T(8,128)S(1)} %collective-permute-done.3.got, f32[2,256,256]{2,1,0:T(8,128)} %collective-permute-done.4.above_first, ...), custom_call_target="tpu_custom_call" | custom-call | bytes 6291456 | tf_op jit(solution)/shard_map/pallas_call | solution.py:297
  138.1 1.8 %broadcast_select_fusion.1 = (f32[2,2,256,256]{3,2,1,0:T(8,128)S(1)}, f32[2,2,256,256]{3,2,1,0:T(8,128)S(1)}) fusion(f32[2,2,256,256]{3,2,1,0:T(8,128)} %bitcast.5, f32[2,2,256,256]{3,2,1,0:T(8,128)} %collective-permute-done.7, pred[]{:T(512)S(6)} %eq.4), kind=kLoop, calls=%fused_computation.4 | loop fusion | flops 524288 | bytes 4194305 | tf_op jit(solution)/shard_map/jit(_where)/select_n | solution.py:357
  140.3 1.6 %fusion = f32[4,2,256,256]{3,2,1,0:T(8,128)} fusion(f32[4,2,256,256]{3,2,1,0:T(8,128)S(1)} %copy-done.4, f32[2,2,256,256]{3,2,1,0:T(8,128)S(1)} %get-tuple-element.21, f32[2,2,256,256]{3,2,1,0:T(8,128)S(1)} %get-tuple-element.20), kind=kLoop, calls=%fused_computation.1 | loop fusion | flops 1572864 | bytes 6291456 | tf_op jit(solution)/shard_map/add | solution.py:358
  (48 shorter events, 16.8 us)
Async XLA Ops:
  1.4 1.6 %copy-start = (f32[2,512,512]{2,1,0:T(8,128)S(1)}, f32[2,512,512]{2,1,0:T(8,128)}, u32[]{:S(2)}) copy-start(f32[2,512,512]{2,1,0:T(8,128)} %tile.7) | copy-start | bytes 6291460
  3.0 6.1 %copy-start.17 = (f32[3,256,256]{2,1,0:T(8,128)S(1)}, f32[3,256,256]{2,1,0:T(8,128)}, u32[]{:S(2)}) copy-start(f32[3,256,256]{2,1,0:T(8,128)} %param.8) | copy-start | bytes 2359300
  5.5 4.5 %copy-start.16 = (f32[2,256,256]{2,1,0:T(8,128)}, f32[2,256,256]{2,1,0:T(8,128)S(1)}, u32[]{:S(2)}) copy-start(f32[2,256,256]{2,1,0:T(8,128)S(1)} %get-tuple-element.11) | copy-start | bytes 1572868
  5.5 14.7 %copy-start.1 = (f32[2,512,512]{2,1,0:T(8,128)S(1)}, f32[2,512,512]{2,1,0:T(8,128)}, u32[]{:S(2)}) copy-start(f32[2,512,512]{2,1,0:T(8,128)} %tile.7) | copy-start | bytes 6291460
  5.5 14.6 %collective-permute-start.1 = (f32[2,256,256]{2,1,0:T(8,128)}, f32[2,256,256]{2,1,0:T(8,128)}, u32[]{:S(2)}, u32[]{:S(2)}) collective-permute-start(f32[2,256,256]{2,1,0:T(8,128)} %get-tuple-element.12), channel_id=1, source_target_pairs={{16,0},{17,1},{18,2},{19,3},{20,4},{21,5},{22,6},{23,7},{24,8},{25... | collective-permute-start | bytes 1572872 | tf_op jit(solution)/shard_map/ppermute | solution.py:314
  10.0 24.2 %copy-start.15 = (s32[128]{0:T(128)S(1)}, s32[128]{0:T(128)}, u32[]{:S(2)}) copy-start(s32[128]{0:T(128)} %owner.1) | copy-start | bytes 1540
  10.0 24.2 %all-to-all-start = ((f32[16,3,16,256]{3,2,1,0:T(8,128)}), f32[16,3,16,256]{3,2,1,0:T(8,128)}, u32[]{:S(2)}, u32[]{:S(2)}) async-start(f32[16,3,16,256]{3,2,1,0:T(8,128)} %bitcast.7), calls=%async_computation | async-start | bytes 1572864 | tf_op jit(solution)/shard_map/all_to_all | solution.py:317
  18.1 22.5 %copy-start.5 = (bf16[10,256,256]{2,1,0:T(8,128)(2,1)S(1)}, bf16[10,256,256]{2,1,0:T(8,128)(2,1)}, u32[]{:S(2)}) copy-start(bf16[10,256,256]{2,1,0:T(8,128)(2,1)} %constant.15.clone.tables) | copy-start | bytes 3932164
  18.1 22.4 %collective-permute-start = (f32[2,256,256]{2,1,0:T(8,128)}, f32[2,256,256]{2,1,0:T(8,128)}, u32[]{:S(2)}, u32[]{:S(2)}) collective-permute-start(f32[2,256,256]{2,1,0:T(8,128)} %copy-done.16), channel_id=1, source_target_pairs={{16,0},{17,1},{18,2},{19,3},{20,4},{21,5},{22,6},{23,7},{24,8},{25... | collective-permute-start | bytes 1572872 | tf_op jit(solution)/shard_map/ppermute | solution.py:315
  22.7 17.8 %collective-permute-start.2 = (f32[2,256,256]{2,1,0:T(8,128)}, f32[2,256,256]{2,1,0:T(8,128)}, u32[]{:S(2)}, u32[]{:S(2)}) collective-permute-start(f32[2,256,256]{2,1,0:T(8,128)} %shard_map.78), channel_id=1, source_target_pairs={{0,15},{1,0},{2,1},{3,2},{4,3},{5,4},{6,5},{7,6},{8,7},{9,8},{10,9... | collective-permute-start | bytes 1572872 | tf_op jit(solution)/shard_map/ppermute | solution.py:321
  36.3 14.5 %all-to-all-start.1 = ((f32[16,16,256]{2,1,0:T(8,128)}), f32[16,16,256]{2,1,0:T(8,128)}, u32[]{:S(2)}, u32[]{:S(2)}) async-start(f32[16,16,256]{2,1,0:T(8,128)} %copy-done.8), calls=%async_computation.1 | async-start | bytes 524288 | tf_op jit(solution)/shard_map/all_to_all | solution.py:325
  40.5 1.6 %copy-start.2 = (f32[4,2,256,256]{3,2,1,0:T(8,128)S(1)}, f32[4,2,256,256]{3,2,1,0:T(8,128)}, u32[]{:S(2)}) copy-start(f32[4,2,256,256]{3,2,1,0:T(8,128)} %probe.3) | copy-start | bytes 6291460
  47.9 1.3 copy-start.6
  50.8 1.6 %copy-start.3 = (f32[4,2,256,256]{3,2,1,0:T(8,128)S(1)}, f32[4,2,256,256]{3,2,1,0:T(8,128)}, u32[]{:S(2)}) copy-start(f32[4,2,256,256]{3,2,1,0:T(8,128)} %probe.3) | copy-start | bytes 6291460
  52.4 1.6 %copy-start.7 = (f32[4,2,256,256]{3,2,1,0:T(8,128)S(1)}, f32[4,2,256,256]{3,2,1,0:T(8,128)}, u32[]{:S(2)}) copy-start(f32[4,2,256,256]{3,2,1,0:T(8,128)} %copy-done.6) | copy-start | bytes 6291460
  61.8 3.2 %copy-start.11 = (f32[2,256,256]{2,1,0:T(8,128)}, f32[2,256,256]{2,1,0:T(8,128)S(1)}, u32[]{:S(2)}) copy-start(f32[2,256,256]{2,1,0:T(8,128)S(1)} %get-tuple-element.16.own) | copy-start | bytes 1572868
  61.8 3.0 %collective-permute-start.6 = (f32[2,2,256,256]{3,2,1,0:T(8,128)S(1)}, f32[2,2,256,256]{3,2,1,0:T(8,128)S(1)}, u32[]{:S(2)}, u32[]{:S(2)}) collective-permute-start(f32[2,2,256,256]{3,2,1,0:T(8,128)S(1)} %get-tuple-element.19), channel_id=1, source_target_pairs={{0,16},{1,17},{2,18},{3,19},{4,20},{5,21},{6,22},{7,23},{8,24},{9,... | collective-permute-start | bytes 3145736 | tf_op jit(solution)/shard_map/ppermute | solution.py:340
  92.4 8.4 %copy-start.12 = (f32[2,256,256]{2,1,0:T(8,128)S(1)}, f32[2,256,256]{2,1,0:T(8,128)}, u32[]{:S(2)}) copy-start(f32[2,256,256]{2,1,0:T(8,128)} %copy-done.11) | copy-start | bytes 1572868
  94.9 22.3 %all-to-all-start.3 = ((f32[64,16,256]{2,1,0:T(8,128)}), f32[64,16,256]{2,1,0:T(8,128)}, u32[]{:S(2)}, u32[]{:S(2)}) async-start(f32[64,16,256]{2,1,0:T(8,128)} %broadcast_in_dim.2), calls=%async_computation.3 | async-start | bytes 2097152 | tf_op jit(solution)/shard_map/all_to_all | solution.py:347
  100.8 21.5 %collective-permute-start.3 = (f32[2,256,256]{2,1,0:T(8,128)S(1)}, f32[2,256,256]{2,1,0:T(8,128)S(1)}, u32[]{:S(2)}, u32[]{:S(2)}) collective-permute-start(f32[2,256,256]{2,1,0:T(8,128)S(1)} %copy-done.12), channel_id=1, source_target_pairs={{15,0},{0,1},{1,2},{2,3},{3,4},{4,5},{5,6},{6,7},{7,8},{8,9},{9,10... | collective-permute-start | bytes 1572872 | tf_op jit(solution)/shard_map/ppermute | solution.py:341
  117.2 20.9 %collective-permute-start.7 = (f32[2,2,256,256]{3,2,1,0:T(8,128)}, f32[2,2,256,256]{3,2,1,0:T(8,128)}, u32[]{:S(2)}, u32[]{:S(2)}) collective-permute-start(f32[2,2,256,256]{3,2,1,0:T(8,128)} %bitcast.5), channel_id=1, source_target_pairs={{0,16},{1,17},{2,18},{3,19},{4,20},{5,21},{6,22},{7,23},{8,24},{9,... | collective-permute-start | bytes 3145736 | tf_op jit(solution)/shard_map/ppermute | solution.py:356
  120.3 8.0 %collective-permute-start.4 = (f32[2,256,256]{2,1,0:T(8,128)S(1)}, f32[2,256,256]{2,1,0:T(8,128)}, u32[]{:S(2)}, u32[]{:S(2)}) collective-permute-start(f32[2,256,256]{2,1,0:T(8,128)S(1)} %copy-done.12), channel_id=1, source_target_pairs={{0,16},{1,17},{2,18},{3,19},{4,20},{5,21},{6,22},{7,23},{8,24},{9,... | collective-permute-start | bytes 1572872 | tf_op jit(solution)/shard_map/ppermute | solution.py:342
  122.2 11.7 %collective-permute-start.5 = (f32[2,256,256]{2,1,0:T(8,128)S(1)}, f32[2,256,256]{2,1,0:T(8,128)}, u32[]{:S(2)}, u32[]{:S(2)}) collective-permute-start(f32[2,256,256]{2,1,0:T(8,128)S(1)} %collective-permute-done.3.got), channel_id=1, source_target_pairs={{0,16},{1,17},{2,18},{3,19},{4,20},{5,21},{6,22},{7,23},{8,24},{9,... | collective-permute-start | bytes 1572872 | tf_op jit(solution)/shard_map/ppermute | solution.py:345
  138.1 2.2 %copy-start.4 = (f32[4,2,256,256]{3,2,1,0:T(8,128)S(1)}, f32[4,2,256,256]{3,2,1,0:T(8,128)}, u32[]{:S(2)}) copy-start(f32[4,2,256,256]{3,2,1,0:T(8,128)} %probe.3) | copy-start | bytes 6291460
  (5 other events, 4.2 us)

commit v2 on v1

v2 whole, which is shorter than its diff:
```python
import functools
import math

import jax
import jax.numpy as jnp
import ml_dtypes
import numpy as np
from jax import lax
from jax.experimental import pallas as pl
from jax.experimental.pallas import tpu as pltpu
from jax.sharding import Mesh
from jax.sharding import PartitionSpec as P

W = 256
HALF = 128
TILE = 512
MODES = 4
CAP = 3
NR = 8
NC = 16
ALL = ("x", "core", "z", "y")
COL = ("z", "y")
CHIPS = ("x", "z", "y")
CHUNK = W // NC
BF = jnp.bfloat16
F32 = jnp.float32


def dft_tables():
    n = np.arange(HALF)[:, None]
    q = np.arange(HALF)[None, :]
    out = []
    for k in (2 * q, 2 * q + 1):
        angle = 2.0 * math.pi * ((n * k) % W) / W
        c = np.cos(angle) / math.sqrt(W)
        s = np.sin(angle) / math.sqrt(W)
        m = np.block([[c, -s], [s, c]])
        for t in (m, m.T):
            hi = t.astype(ml_dtypes.bfloat16)
            lo = (t - hi.astype(np.float64)).astype(ml_dtypes.bfloat16)
            out += [hi, lo]
    order = np.concatenate([np.arange(0, W, 2), np.arange(1, W, 2)])
    perm = np.zeros((W, W))
    perm[np.arange(W), order] = 1.0
    out += [perm.astype(ml_dtypes.bfloat16), perm.T.astype(ml_dtypes.bfloat16)]
    return np.stack(out)


def routes():
    up, side, slant, swap = [], [], [], []
    for r in range(NR):
        for c in range(NC):
            me = r * NC + c
            step = -1 if r % 2 == 0 else 1
            side.append((me, r * NC + (c + step) % NC))
            swap.append((me, (r ^ 1) * NC + c))
            if r > 0:
                up.append((me, me - NC))
                slant.append((me, (r - 1) * NC + (c - step) % NC))
    return up, side, slant, swap


def back(route):
    return [(b, a) for a, b in route]


UP, SIDE, SLANT, SWAP = routes()


def coords():
    core = lax.axis_index("core")
    row = lax.axis_index("x") * 2 + core
    col = lax.axis_index("z") * 4 + lax.axis_index("y")
    return row, col, core


def corner(offs, row, col):
    row = (row + NR) % NR
    col = (col + NC) % NC
    p = row * NC + col
    return offs[0, p] - row * TILE, offs[1, p] - col * TILE


def iota(shape, dim):
    return lax.broadcasted_iota(jnp.int32, shape, dim)


def fetch(pairs, sems):
    copies = []
    for n, (src, dst) in enumerate(pairs):
        copy = pltpu.make_async_copy(src, dst, sems.at[n])
        copy.start()
        copies.append(copy)
    return copies


def send_kernel(offs_hbm, tile, first, second, side, own, offs, t_buf, f_buf, s_buf, o_buf, w_buf, sems):
    row, col, core = coords()
    loads = fetch([(offs_hbm, offs), (tile.at[0], t_buf.at[0]), (tile.at[1], t_buf.at[1])], sems)
    loads[0].wait()
    even = core == 0
    _, c_up = corner(offs, row - 1, col)
    r_s, c_s = corner(offs, row, col)
    r_b, _ = corner(offs, row, col - 1)
    c1 = jnp.where(even, c_up, 0)
    c2 = jnp.where(even, 0, c_up)
    r_side, c_side = jnp.where(even, r_b, r_s), jnp.where(even, 0, c_s)
    r_own, c_own = jnp.where(even, r_s, r_b), jnp.where(even, c_s, 0)
    a = iota((W, W), 0)
    b = iota((W, W), 1)
    stores = []
    for i in range(2):
        loads[1 + i].wait()
        f_buf[i] = jnp.where(b >= c1, t_buf[i, :W, :W], t_buf[i, :W, W:])
        stores += fetch([(f_buf.at[i], first.at[i])], sems.at[pl.ds(3 + 4 * i, 1)])
        s_buf[i] = jnp.where(b >= c2, t_buf[i, :W, :W], t_buf[i, :W, W:])
        stores += fetch([(s_buf.at[i], second.at[i])], sems.at[pl.ds(4 + 4 * i, 1)])
        top = jnp.where(b >= c_side, t_buf[i, :W, :W], t_buf[i, :W, W:])
        low = jnp.where(b >= c_side, t_buf[i, W:, :W], t_buf[i, W:, W:])
        o_buf[i] = jnp.where(a >= r_side, top, low)
        stores += fetch([(o_buf.at[i], side.at[i])], sems.at[pl.ds(5 + 4 * i, 1)])
        top = jnp.where(b >= c_own, t_buf[i, :W, :W], t_buf[i, :W, W:])
        low = jnp.where(b >= c_own, t_buf[i, W:, :W], t_buf[i, W:, W:])
        w_buf[i] = jnp.where(a >= r_own, top, low)
        stores += fetch([(w_buf.at[i], own.at[i])], sems.at[pl.ds(6 + 4 * i, 1)])
    for copy in stores:
        copy.wait()


def split(x):
    hi = x.astype(BF)
    lo = (x - hi.astype(F32)).astype(BF)
    return hi, lo


def mm(a, b):
    return jnp.dot(a, b, preferred_element_type=F32)


def right(x, hi, lo):
    xh, xl = split(x)
    return mm(jnp.concatenate([xh, xh, xl], axis=1), jnp.concatenate([hi, lo, hi], axis=0))


def left(hi, lo, x):
    xh, xl = split(x)
    return mm(jnp.concatenate([hi, lo, hi], axis=1), jnp.concatenate([xh, xh, xl], axis=0))


def halves(x, axis):
    first = lax.slice_in_dim(x, 0, HALF, axis=axis)
    second = lax.slice_in_dim(x, HALF, W, axis=axis)
    return first, second


def work_kernel(
    offs_hbm, amp, own, below, side, slant, probe, tables, grad, give, keep, scale,
    offs, a_buf, o_buf, b_buf, s_buf, d_buf, p_buf, t_buf, f_buf, m_buf, x_buf, g_buf, q_buf, sems,
):
    row, col, core = coords()
    loads = fetch(
        [
            (offs_hbm, offs), (own, o_buf), (below, b_buf), (side, s_buf), (slant, d_buf),
            (tables, t_buf), (amp, a_buf),
        ],
        sems,
    )
    order = [(t + 2 * (1 - core)) % MODES for t in range(MODES)]
    p_loads = fetch([(probe.at[order[t]], p_buf.at[t]) for t in range(MODES)], sems.at[pl.ds(7, MODES)])
    loads[0].wait()
    r, c = corner(offs, row, jnp.where(core == 0, col, col - 1))
    a = iota((W, W), 0)
    b = iota((W, W), 1)
    beyond = jnp.where(c > b + W, 1, 0)
    use_side = beyond != core
    row_shift = (2 * W - r) % W
    col_shift = (2 * W - c) % W
    for n in range(1, 5):
        loads[n].wait()
    for i in range(2):
        whole = jnp.where(
            a + W >= r, jnp.where(use_side, s_buf[i], o_buf[i]), jnp.where(use_side, d_buf[i], b_buf[i])
        )
        x_buf[i] = pltpu.roll(pltpu.roll(whole, row_shift, 0), col_shift, 1)
    loads[5].wait()
    power = jnp.zeros((W, W), F32)
    for t in range(MODES):
        p_loads[t].wait()
        p_re = p_buf[t, 0]
        p_im = p_buf[t, 1]
        o_re = x_buf[0]
        o_im = x_buf[1]
        power += p_re * p_re + p_im * p_im
        e_re = p_re * o_re - p_im * o_im
        e_im = p_re * o_im + p_im * o_re
        r0, r1 = halves(e_re, 1)
        i0, i1 = halves(e_im, 1)
        even = right(jnp.concatenate([r0 + r1, i0 + i1], axis=1), t_buf[0], t_buf[1])
        odd = right(jnp.concatenate([r0 - r1, i0 - i1], axis=1), t_buf[4], t_buf[5])
        h_re = jnp.concatenate([even[:, :HALF], odd[:, :HALF]], axis=1)
        h_im = jnp.concatenate([even[:, HALF:], odd[:, HALF:]], axis=1)
        r0, r1 = halves(h_re, 0)
        i0, i1 = halves(h_im, 0)
        even = left(t_buf[2], t_buf[3], jnp.concatenate([r0 + r1, i0 + i1], axis=0))
        odd = left(t_buf[6], t_buf[7], jnp.concatenate([r0 - r1, i0 - i1], axis=0))
        f_buf[t, 0] = even
        f_buf[t, 1] = odd
        if t == 0:
            m_buf[:HALF] = even[:HALF] * even[:HALF] + even[HALF:] * even[HALF:]
            m_buf[HALF:] = odd[:HALF] * odd[:HALF] + odd[HALF:] * odd[HALF:]
        else:
            m_buf[:HALF] += even[:HALF] * even[:HALF] + even[HALF:] * even[HALF:]
            m_buf[HALF:] += odd[:HALF] * odd[:HALF] + odd[HALF:] * odd[HALF:]
    scale[...] = jnp.full(scale.shape, 1.0 / (jnp.max(power) + 1e-05), F32)
    loads[6].wait()
    x = a_buf[...]
    for turn in range(2):
        p1 = x.astype(BF)
        rest = x - p1.astype(F32)
        p2 = rest.astype(BF)
        p3 = (rest - p2.astype(F32)).astype(BF)
        if turn == 0:
            x = mm(t_buf[8], p1) + mm(t_buf[8], p2) + mm(t_buf[8], p3)
        else:
            x = mm(p1, t_buf[9]) + mm(p2, t_buf[9]) + mm(p3, t_buf[9])
    m_buf[...] = x / jnp.maximum(jnp.sqrt(m_buf[...]), 0.5) - 1.0
    stores = []
    for t in range(MODES):
        f_even = m_buf[:HALF]
        f_odd = m_buf[HALF:]
        even = f_buf[t, 0] * jnp.concatenate([f_even, f_even], axis=0)
        odd = f_buf[t, 1] * jnp.concatenate([f_odd, f_odd], axis=0)
        u = left(t_buf[0], t_buf[1], even)
        v = left(t_buf[4], t_buf[5], odd)
        h_re = jnp.concatenate([u[:HALF] + v[:HALF], u[:HALF] - v[:HALF]], axis=0)
        h_im = jnp.concatenate([u[HALF:] + v[HALF:], u[HALF:] - v[HALF:]], axis=0)
        u = right(jnp.concatenate([h_re[:, :HALF], h_im[:, :HALF]], axis=1), t_buf[2], t_buf[3])
        v = right(jnp.concatenate([h_re[:, HALF:], h_im[:, HALF:]], axis=1), t_buf[6], t_buf[7])
        b_re = jnp.concatenate([u[:, :HALF] + v[:, :HALF], u[:, :HALF] - v[:, :HALF]], axis=1)
        b_im = jnp.concatenate([u[:, HALF:] + v[:, HALF:], u[:, HALF:] - v[:, HALF:]], axis=1)
        p_re = p_buf[t, 0]
        p_im = p_buf[t, 1]
        o_re = x_buf[0]
        o_im = x_buf[1]
        g_re = p_re * b_re + p_im * b_im
        g_im = p_re * b_im - p_im * b_re
        if t == 0:
            g_buf[0] = g_re
            g_buf[1] = g_im
        else:
            g_buf[0] += g_re
            g_buf[1] += g_im
        q_buf[t, 0] = o_re * b_re + o_im * b_im
        q_buf[t, 1] = o_re * b_im - o_im * b_re
        target = give.at[t] if t < 2 else keep.at[t - 2]
        stores += fetch([(q_buf.at[t], target)], sems.at[pl.ds(11 + t, 1)])
    for i in range(2):
        g_buf[i] = pltpu.roll(pltpu.roll(g_buf[i], r % W, 0), c % W, 1)
        stores += fetch([(g_buf.at[i], grad.at[i])], sems.at[pl.ds(15 + i, 1)])
    for copy in stores:
        copy.wait()


def pick_kernel(owner_hbm, slots, out, owner, s_buf, o_buf, sems):
    row, col, core = coords()
    loads = fetch([(owner_hbm, owner), (slots, s_buf)], sems)
    loads[0].wait()
    base = row * NC
    owners = [owner[0, base + i] for i in range(NC)]
    index = []
    for i in range(NC):
        rank = jnp.int32(0)
        for q in range(i):
            rank = rank + jnp.where(owners[q] == owners[i], 1, 0)
        index.append(owners[i] * CAP + rank)
    loads[1].wait()
    for i in range(NC):
        device = jnp.where(core == 0, i, (i + 1) % NC)
        o_buf[device] = s_buf[index[i]]
    for copy in fetch([(o_buf, out)], sems.at[pl.ds(2, 1)]):
        copy.wait()


def sum_kernel(parts, out, p_buf, o_buf, sems):
    groups = 4
    per = 64 // groups
    loads = fetch(
        [(parts.at[pl.ds(g * per, per)], p_buf.at[pl.ds(g * per, per)]) for g in range(groups)], sems
    )
    total = jnp.zeros((16, W), F32)
    for g in range(groups):
        loads[g].wait()
        for n in range(per):
            total += p_buf[g * per + n]
    for n in range(8):
        o_buf[n] = total
    stores = fetch([(o_buf, out.at[pl.ds(8 * g, 8)]) for g in range(8)], sems.at[pl.ds(groups, 8)])
    for copy in stores:
        copy.wait()


def object_kernel(
    offs_hbm, scale, tile, own, got, above_first, above_second, out,
    offs, t_buf, w_buf, g_buf, f_buf, s_buf, o_buf, sems,
):
    row, col, core = coords()
    fetch([(offs_hbm, offs)], sems.at[pl.ds(12, 1)])[0].wait()
    loads = []
    for i in range(2):
        loads.append(
            fetch(
                [
                    (tile.at[i], t_buf.at[i]),
                    (own.at[i], w_buf.at[i]),
                    (got.at[i], g_buf.at[i]),
                    (above_first.at[i], f_buf.at[i]),
                    (above_second.at[i], s_buf.at[i]),
                ],
                sems.at[pl.ds(5 * i, 5)],
            )
        )
    a = iota((W, W), 0)
    b = iota((W, W), 1)
    s = scale[0, 0]
    r_s, c_s = corner(offs, row, col)
    r_b, c_b = corner(offs, row, col - 1)
    r_as, c_as = corner(offs, row - 1, col)
    r_ab, c_ab = corner(offs, row - 1, col - 1)

    def bands(at, v):
        return [v <= at, jnp.logical_and(v > at, v <= at + W)]

    even = core == 0
    rows_s, cols_s = bands(a, r_s), bands(b, c_s)
    rows_b = bands(a, r_b)
    in_b = c_b > b + W
    cols_as = bands(b, c_as)
    low_as = r_as > a + W
    low_ab = jnp.logical_and(r_ab > a + W, c_ab > b + W)
    stores = []
    for i in range(2):
        for copy in loads[i]:
            copy.wait()
        g_s = jnp.where(even, w_buf[i], g_buf[i])
        g_b = jnp.where(even, g_buf[i], w_buf[i])
        d_s = jnp.where(even, s_buf[i], f_buf[i])
        d_b = jnp.where(even, f_buf[i], s_buf[i])
        for p in range(2):
            for q in range(2):
                total = jnp.where(jnp.logical_and(rows_s[p], cols_s[q]), g_s, 0.0)
                if q == 0:
                    total += jnp.where(jnp.logical_and(rows_b[p], in_b), g_b, 0.0)
                if p == 0:
                    total += jnp.where(jnp.logical_and(low_as, cols_as[q]), d_s, 0.0)
                if p == 0 and q == 0:
                    total += jnp.where(low_ab, d_b, 0.0)
                at = (i, pl.ds(p * W, W), pl.ds(q * W, W))
                o_buf[at] = t_buf[at] + total * s
        stores += fetch([(o_buf.at[i], out.at[i])], sems.at[pl.ds(10 + i, 1)])
    for copy in stores:
        copy.wait()


def probe_kernel(probe, mine, theirs, out, p_buf, m_buf, o_buf, sems):
    core = lax.axis_index("core")
    order = [(m + 2 * core) % MODES for m in range(MODES)]
    loads = []
    for t in range(MODES):
        src = mine.at[t] if t < 2 else theirs.at[t - 2]
        loads.append(
            fetch([(probe.at[order[t]], p_buf.at[t]), (src, m_buf.at[t])], sems.at[pl.ds(2 * t, 2)])
        )
    stores = []
    for t in range(MODES):
        for copy in loads[t]:
            copy.wait()
        o_buf[t] = p_buf[t] + m_buf[t] * (1.0 / (NR * NC))
        stores += fetch([(o_buf.at[t], out.at[order[t]])], sems.at[pl.ds(8 + t, 1)])
    for copy in stores:
        copy.wait()


SMEM = pl.BlockSpec(memory_space=pltpu.SMEM)
VMEM = pl.BlockSpec(memory_space=pltpu.VMEM)
HBM = pl.BlockSpec(memory_space=pltpu.HBM)
PIECE = (2, W, W)
WORK_MB = 58


def call(kernel, outs, ins, scratch, sems, *args, flops=0, data=0, out_specs=None, mb=62):
    shapes = [jax.ShapeDtypeStruct(s, F32) for s in outs]
    buffers = [pltpu.VMEM(s, F32) if isinstance(s, tuple) else s for s in scratch]
    return pl.pallas_call(
        kernel,
        out_shape=shapes,
        in_specs=ins,
        out_specs=out_specs or [HBM] * len(outs),
        scratch_shapes=buffers + [pltpu.SemaphoreType.DMA((sems,))],
        compiler_params=pltpu.CompilerParams(vmem_limit_bytes=mb * 2**20),
        cost_estimate=pl.CostEstimate(flops=flops, bytes_accessed=data, transcendentals=0),
    )(*args)


def exchange(x):
    return lax.all_to_all(x, CHIPS, 0, 0, tiled=True)


def shards(tables, object_field, probe, measured, offsets, owner):
    offsets = offsets.T
    owner = owner.reshape(1, NR * NC)
    modes = (MODES, 2, W, W)
    half = (2, 2, W, W)
    table_buf = pltpu.VMEM(tables.shape, BF)
    offs_buf = pltpu.SMEM(offsets.shape, jnp.int32)
    owner_buf = pltpu.SMEM(owner.shape, jnp.int32)
    first, second, side, own = call(
        send_kernel, [PIECE] * 4, [HBM] * 2, [offs_buf, (2, TILE, TILE), PIECE, PIECE, PIECE, PIECE], 11,
        offsets, object_field, data=4 << 20,
    )
    side = lax.ppermute(side, ALL, SIDE)
    slant = lax.ppermute(first, ALL, SLANT)
    below = lax.ppermute(second, ALL, UP)
    spread = measured.reshape(CAP, NC, CHUNK, W).transpose(1, 0, 2, 3)
    spread = lax.all_to_all(spread, COL, 0, 0, tiled=True)
    slots = (NC * CAP, CHUNK, W)
    picked = call(
        pick_kernel, [(NC, CHUNK, W)], [HBM] * 2, [owner_buf, slots, (NC, CHUNK, W)], 3,
        owner, spread.reshape(slots), data=1 << 20, mb=50,
    )[0]
    amp = lax.all_to_all(picked, COL, 0, 0, tiled=True).reshape(W, W)
    grad, give, keep, scale = call(
        work_kernel, [PIECE, half, half, (8, 128)], [HBM] * 8,
        [offs_buf, (W, W), PIECE, PIECE, PIECE, PIECE, modes, table_buf, modes, (W, W), PIECE, PIECE, modes], 17,
        offsets, amp, own, below, side, slant, probe, tables,
        flops=2 * 96 * W**3, data=10 << 20, out_specs=[HBM, HBM, HBM, VMEM], mb=WORK_MB,
    )
    taken = lax.ppermute(give, ALL, SWAP)
    got = lax.ppermute(grad, ALL, back(SIDE))
    above_first = lax.ppermute(grad, ALL, back(UP))
    above_second = lax.ppermute(grad, ALL, back(SLANT))
    mine = (keep + taken).reshape(64, 16, W)
    inside = offsets[0, 0] >= 0
    parts = lax.cond(inside, exchange, jnp.zeros_like, mine)
    parts, got, above_first, above_second = lax.optimization_barrier((parts, got, above_first, above_second))
    copies = call(
        sum_kernel, [(64, 16, W)], [HBM], [(64, 16, W), (8, 16, W)], 12, parts, data=2 << 20, mb=50,
    )[0]
    mine = lax.all_to_all(copies, CHIPS, 0, 0, tiled=True)
    new_object = call(
        object_kernel, [(2, TILE, TILE)], [HBM, SMEM] + [HBM] * 5,
        [offs_buf, (2, TILE, TILE), PIECE, PIECE, PIECE, PIECE, (2, TILE, TILE)], 13,
        offsets, scale, object_field, grad, got, above_first, above_second, data=6 << 20,
    )[0]
    mine, new_object = lax.optimization_barrier((mine, new_object))
    mine = mine.reshape(half)
    theirs = lax.ppermute(mine, ALL, SWAP)
    new_probe = call(
        probe_kernel, [modes], [HBM] * 3, [modes, modes, modes], 12, probe, mine, theirs, data=6 << 20, mb=50,
    )[0]
    return (new_object, new_probe)


def solution(mesh):
    inner = Mesh(mesh.devices.reshape(4, 2, 4, 4), ALL)
    tables = dft_tables()
    placed = (P(None, ("x", "core"), COL), P(), P(ALL, None, None), P(), P())

    def whole(*args):
        return shards(jnp.asarray(tables), *args)

    return jax.shard_map(
        whole, mesh=inner, in_specs=placed, out_specs=(P(None, ("x", "core"), COL), P()), check_vma=False
    )
```

time: 143 us -> 123 us (0.86)
  local copies, waits for them, and re-layouts: 15.1 us -> 3.29 us
  starting transfers between devices: 39.3 us -> 48.4 us
  waiting for transfers between devices: 32.2 us -> 24.1 us
  blocking collectives: 27.4 us -> 21.5 us
  other arithmetic: 4.95 us -> 0.14 us
    unnamed x37 -> x12, local copies, waits for them, and re-layouts: 13 us -> 0.71 us
    all_to_all x1, waiting for transfers between devices: 10.2 us -> 0.57 us  [shards(): spread = lax.all_to_all(spread, COL, 0, 0, tiled=True)]
    ppermute x1, starting transfers between devices: 0.72 us -> 10.3 us  [shards(): taken = lax.ppermute(give, ALL, SWAP)]
    all_to_all x1, blocking collectives: 27.4 us -> 21.5 us  [exchange(): return lax.all_to_all(x, CHIPS, 0, 0, tiled=True)]
    ppermute x6, starting transfers between devices: 17.4 us -> 14.8 us  [the longest x1 5.35 us: shards(): slant = lax.ppermute(first, ALL, SLANT)]
    all_to_all x1, starting transfers between devices: 5.88 us -> 8.41 us  [shards(): mine = lax.all_to_all(copies, CHIPS, 0, 0, tiled=True)]
    ppermute x1, waiting for transfers between devices: 2.29 us -> 0.01 us  [shards(): taken = lax.ppermute(give, ALL, SWAP)]
    ppermute x1, waiting for transfers between devices: 0.01 us -> 2.29 us  [shards(): theirs = lax.ppermute(mine, ALL, SWAP)]
  transfers between devices with their start and end apart: 11 -> 11, of which waited for: 5 -> 6; matrix products, arithmetic and copies ran while one was open for 1% -> 1% of each run, Pallas kernels for 10% -> 7%
where the time goes in v2:
time: 123 us; the launch traced here: 122 us
  starting transfers between devices  48.4 us (39%)
  waiting for transfers between devices  24.1 us (20%)
  Pallas kernels  23.3 us (19%)
  blocking collectives  21.5 us (17%)
  local copies, waits for them, and re-layouts  3.29 us (3%)
  between operations  1.43 us (1%)
    pallas_call x6, Pallas kernels, call(): pl.pallas_call(kernel, out_shape=shapes, in_specs=ins, out_specs=out_spec...  23.3 us
    all_to_all x1, blocking collectives, exchange(): return lax.all_to_all(x, CHIPS, 0, 0, tiled=True)  21.5 us
    all_to_all x1, waiting for transfers between devices, shards(): mine = lax.all_to_all(copies, CHIPS, 0, 0, tiled=True)  12.2 us
    ppermute x1, starting transfers between devices, shards(): taken = lax.ppermute(give, ALL, SWAP)  10.3 us
    all_to_all x1, starting transfers between devices, shards(): spread = lax.all_to_all(spread, COL, 0, 0, tiled=True)  8.73 us
    all_to_all x1, starting transfers between devices, shards(): mine = lax.all_to_all(copies, CHIPS, 0, 0, tiled=True)  8.41 us
    ppermute x1, waiting for transfers between devices, shards(): side = lax.ppermute(side, ALL, SIDE)  7.36 us
    ppermute x1, starting transfers between devices, shards(): slant = lax.ppermute(first, ALL, SLANT)  5.35 us
  transfers between devices with their start and end apart: 11, of which 6 were waited for; matrix products, arithmetic and copies ran while one was open for 1% of the time, Pallas kernels for 7%

profile of v2, /device:TPU:1, one launch (start us, length us, event | category | flops | bytes accessed | tf_op | source)
XLA Modules:
  0.0 122.1 jit_solution(12245971117084404296)
XLA Ops:
  0.6 2.1 %copy.10 = f32[3,16,16,256]{3,2,0,1:T(8,128)} copy(f32[3,16,16,256]{3,2,1,0:T(8,128)} %bitcast.16) | data formatting | bytes 1572864 | tf_op jit(solution)/shard_map/reshape | solution.py:423
  2.7 8.7 %all-to-all-start.1 = ((f32[16,3,16,256]{3,2,1,0:T(8,128)}), f32[16,3,16,256]{3,2,1,0:T(8,128)S(1)}, u32[]{:S(2)}, u32[]{:S(2)}) async-start(f32[16,3,16,256]{3,2,1,0:T(8,128)} %bitcast.10), calls=%async_computation.1 | async-start | bytes 1572864 | tf_op jit(solution)/shard_map/all_to_all | solution.py:424
  11.4 2.7 %shard_map.78 = (f32[2,256,256]{2,1,0:T(8,128)}, f32[2,256,256]{2,1,0:T(8,128)}, f32[2,256,256]{2,1,0:T(8,128)}, f32[2,256,256]{2,1,0:T(8,128)}) custom-call(s32[2,128]{1,0:T(2,128)} %bitcast.18, f32[2,512,512]{2,1,0:T(8,128)} %tile.3), custom_call_target="tpu_custom_call" | custom-call | bytes 4194304 | tf_op jit(solution)/shard_map/pallas_call | solution.py:393
  14.1 2.9 %collective-permute-start = (f32[2,256,256]{2,1,0:T(8,128)}, f32[2,256,256]{2,1,0:T(8,128)S(1)}, u32[]{:S(2)}, u32[]{:S(2)}) collective-permute-start(f32[2,256,256]{2,1,0:T(8,128)} %get-tuple-element.28), channel_id=1, source_target_pairs={{16,0},{17,1},{18,2},{19,3},{20,4},{21,5},{22,6},{23,7},{24,8},{25... | collective-permute-start | bytes 1572872 | tf_op jit(solution)/shard_map/ppermute | solution.py:422
  17.0 1.7 %collective-permute-start.1 = (f32[2,256,256]{2,1,0:T(8,128)}, f32[2,256,256]{2,1,0:T(8,128)S(1)}, u32[]{:S(2)}, u32[]{:S(2)}) collective-permute-start(f32[2,256,256]{2,1,0:T(8,128)} %get-tuple-element.29), channel_id=1, source_target_pairs={{0,15},{1,0},{2,1},{3,2},{4,3},{5,4},{6,5},{7,6},{8,7},{9,8},{10,9... | collective-permute-start | bytes 1572872 | tf_op jit(solution)/shard_map/ppermute | solution.py:420
  18.7 5.3 %collective-permute-start.2 = (f32[2,256,256]{2,1,0:T(8,128)}, f32[2,256,256]{2,1,0:T(8,128)S(1)}, u32[]{:S(2)}, u32[]{:S(2)}) collective-permute-start(f32[2,256,256]{2,1,0:T(8,128)} %get-tuple-element.30), channel_id=1, source_target_pairs={{16,15},{17,0},{18,1},{19,2},{20,3},{21,4},{22,5},{23,6},{24,7},{2... | collective-permute-start | bytes 1572872 | tf_op jit(solution)/shard_map/ppermute | solution.py:421
  24.6 1.4 %shard_map.77 = f32[16,16,256]{2,1,0:T(8,128)} custom-call(s32[1,128]{1,0:T(1,128)S(1)} %bitcast.14, f32[48,16,256]{2,1,0:T(8,128)S(1)} %bitcast.13), custom_call_target="tpu_custom_call" | custom-call | bytes 1048576 | tf_op jit(solution)/shard_map/pallas_call | solution.py:393
  26.1 3.8 %all-to-all-start.2 = ((f32[16,16,256]{2,1,0:T(8,128)}), f32[16,16,256]{2,1,0:T(8,128)S(1)}, u32[]{:S(2)}, u32[]{:S(2)}) async-start(f32[16,16,256]{2,1,0:T(8,128)} %shard_map.77), calls=%async_computation.2 | async-start | bytes 524288 | tf_op jit(solution)/shard_map/all_to_all | solution.py:430
  29.9 7.4 %collective-permute-done.1.side = f32[2,256,256]{2,1,0:T(8,128)S(1)} collective-permute-done((f32[2,256,256]{2,1,0:T(8,128)}, f32[2,256,256]{2,1,0:T(8,128)S(1)}, u32[]{:S(2)}, u32[]{:S(2)}) %collective-permute-start.1) | collective-permute-done | bytes 524320 | tf_op jit(solution)/shard_map/ppermute | solution.py:420
  37.3 1.4 %all-to-all-done.2 = f32[16,16,256]{2,1,0:T(8,128)S(1)} async-done(((f32[16,16,256]{2,1,0:T(8,128)}), f32[16,16,256]{2,1,0:T(8,128)S(1)}, u32[]{:S(2)}, u32[]{:S(2)}) %all-to-all-start.2) | async-done | bytes 262176 | tf_op jit(solution)/shard_map/all_to_all | solution.py:430
  39.4 10.5 %shard_map.79 = (f32[2,256,256]{2,1,0:T(8,128)}, f32[2,2,256,256]{3,2,1,0:T(8,128)}, f32[2,2,256,256]{3,2,1,0:T(8,128)S(1)}, f32[8,128]{1,0:T(8,128)}) custom-call(s32[2,128]{1,0:T(2,128)} %bitcast.19, f32[256,256]{1,0:T(8,128)} %bitcast.17, f32[2,256,256]{2,1,0:T(8,128)} %get-tuple-element.27.own, f32[2,256,256]{2,1,0:T(8,128)} %copy-done.3, ...), custom_call_target="tpu_custom_call" | custom-call | flops 3221225472 | bytes 10485760 | tf_op jit(solution)/shard_map/pallas_call | solution.py:393
  49.9 10.3 %collective-permute-start.3 = (f32[2,2,256,256]{3,2,1,0:T(8,128)}, f32[2,2,256,256]{3,2,1,0:T(8,128)S(1)}, u32[]{:S(2)}, u32[]{:S(2)}) collective-permute-start(f32[2,2,256,256]{3,2,1,0:T(8,128)} %get-tuple-element.32), channel_id=1, source_target_pairs={{0,16},{1,17},{2,18},{3,19},{4,20},{5,21},{6,22},{7,23},{8,24},{9,... | collective-permute-start | bytes 3145736 | tf_op jit(solution)/shard_map/ppermute | solution.py:437
  60.2 1.0 collective-permute-start.4
  61.2 1.9 %collective-permute-start.5 = (f32[2,256,256]{2,1,0:T(8,128)}, f32[2,256,256]{2,1,0:T(8,128)}, u32[]{:S(2)}, u32[]{:S(2)}) collective-permute-start(f32[2,256,256]{2,1,0:T(8,128)} %get-tuple-element.33.own), channel_id=1, source_target_pairs={{0,16},{1,17},{2,18},{3,19},{4,20},{5,21},{6,22},{7,23},{8,24},{9,... | collective-permute-start | bytes 1572872 | tf_op jit(solution)/shard_map/ppermute | solution.py:439
  63.1 1.9 %collective-permute-start.6 = (f32[2,256,256]{2,1,0:T(8,128)}, f32[2,256,256]{2,1,0:T(8,128)}, u32[]{:S(2)}, u32[]{:S(2)}) collective-permute-start(f32[2,256,256]{2,1,0:T(8,128)} %get-tuple-element.33.own), channel_id=1, source_target_pairs={{15,16},{0,17},{1,18},{2,19},{3,20},{4,21},{5,22},{6,23},{7,24},{8... | collective-permute-start | bytes 1572872 | tf_op jit(solution)/shard_map/ppermute | solution.py:440
  66.2 21.6 %conditional.1 = (f32[64,16,256]{2,1,0:T(8,128)S(1)}) conditional(s32[]{:T(128)} %bitcast.2, () %tuple.17, (f32[2,2,256,256]{3,2,1,0:T(8,128)S(1)}, f32[2,2,256,256]{3,2,1,0:T(8,128)S(1)}) %tuple.18), branch_computations={%region_0.0_spmd, %region_1.0_spmd} | conditional | flops 262144 | bytes 5242888 | solution.py:443
  66.4 21.5 %all_to_all.19 = f32[64,16,256]{2,1,0:T(8,128)S(1)} all-to-all(f32[64,16,256]{2,1,0:T(8,128)S(1)} %bitcast.15), channel_id=1, replica_groups=mesh['x'=4,'core'=2,'z'=4,'y'=4] {'x','z','y'}, dimensions={0} | all-to-all | bytes 2097152 | tf_op jit(solution)/shard_map/cond/branch_1_fun/all_to_all | solution.py:405
  88.2 1.2 shard_map.80
  89.4 8.4 %all-to-all-start.3 = ((f32[64,16,256]{2,1,0:T(8,128)}), f32[64,16,256]{2,1,0:T(8,128)S(1)}, u32[]{:S(2)}, u32[]{:S(2)}) async-start(f32[64,16,256]{2,1,0:T(8,128)} %shard_map.80), calls=%async_computation.3 | async-start | bytes 2097152 | tf_op jit(solution)/shard_map/all_to_all | solution.py:448
  97.8 4.9 %shard_map.81 = f32[2,512,512]{2,1,0:T(8,128)} custom-call(s32[2,128]{1,0:T(2,128)} %bitcast.20, f32[8,128]{1,0:T(8,128)} %get-tuple-element.35.scale, f32[2,512,512]{2,1,0:T(8,128)} %tile.3, f32[2,256,256]{2,1,0:T(8,128)} %get-tuple-element.33.own, f32[2,256,256]{2,1,0:T(8,128)} %collective-permute-done.4.got, ...), custom_call_target="tpu_custom_call" | custom-call | bytes 6291456 | tf_op jit(solution)/shard_map/pallas_call | solution.py:393
  102.8 12.2 %all-to-all-done.3 = f32[64,16,256]{2,1,0:T(8,128)S(1)} async-done(((f32[64,16,256]{2,1,0:T(8,128)}), f32[64,16,256]{2,1,0:T(8,128)S(1)}, u32[]{:S(2)}, u32[]{:S(2)}) %all-to-all-start.3) | async-done | bytes 1048608 | tf_op jit(solution)/shard_map/all_to_all | solution.py:448
  114.9 2.4 %collective-permute-start.7 = (f32[2,2,256,256]{3,2,1,0:T(8,128)S(1)}, f32[2,2,256,256]{3,2,1,0:T(8,128)S(1)}, u32[]{:S(2)}, u32[]{:S(2)}) collective-permute-start(f32[2,2,256,256]{3,2,1,0:T(8,128)S(1)} %bitcast.11), channel_id=1, source_target_pairs={{0,16},{1,17},{2,18},{3,19},{4,20},{5,21},{6,22},{7,23},{8,24},{9,... | collective-permute-start | bytes 3145736 | tf_op jit(solution)/shard_map/ppermute | solution.py:456
  117.3 2.3 %collective-permute-done.7.theirs = f32[2,2,256,256]{3,2,1,0:T(8,128)S(1)} collective-permute-done((f32[2,2,256,256]{3,2,1,0:T(8,128)S(1)}, f32[2,2,256,256]{3,2,1,0:T(8,128)S(1)}, u32[]{:S(2)}, u32[]{:S(2)}) %collective-permute-start.7) | collective-permute-done | bytes 1048608 | tf_op jit(solution)/shard_map/ppermute | solution.py:456
  119.6 2.5 %shard_map.82 = f32[4,2,256,256]{3,2,1,0:T(8,128)} custom-call(f32[4,2,256,256]{3,2,1,0:T(8,128)} %probe.3, f32[2,2,256,256]{3,2,1,0:T(8,128)S(1)} %bitcast.12, f32[2,2,256,256]{3,2,1,0:T(8,128)S(1)} %collective-permute-done.7.theirs), custom_call_target="tpu_custom_call" | custom-call | bytes 6291456 | tf_op jit(solution)/shard_map/pallas_call | solution.py:393
  (21 shorter events, 2.3 us)
Async XLA Ops:
  2.7 21.9 %copy-start = (s32[128]{0:T(128)S(1)}, s32[128]{0:T(128)}, u32[]{:S(2)}) copy-start(s32[128]{0:T(128)} %param.12) | copy-start | bytes 1540
  2.7 21.9 %all-to-all-start.1 = ((f32[16,3,16,256]{3,2,1,0:T(8,128)}), f32[16,3,16,256]{3,2,1,0:T(8,128)S(1)}, u32[]{:S(2)}, u32[]{:S(2)}) async-start(f32[16,3,16,256]{3,2,1,0:T(8,128)} %bitcast.10), calls=%async_computation.1 | async-start | bytes 1572864 | tf_op jit(solution)/shard_map/all_to_all | solution.py:424
  14.1 15.8 %collective-permute-start = (f32[2,256,256]{2,1,0:T(8,128)}, f32[2,256,256]{2,1,0:T(8,128)S(1)}, u32[]{:S(2)}, u32[]{:S(2)}) collective-permute-start(f32[2,256,256]{2,1,0:T(8,128)} %get-tuple-element.28), channel_id=1, source_target_pairs={{16,0},{17,1},{18,2},{19,3},{20,4},{21,5},{22,6},{23,7},{24,8},{25... | collective-permute-start | bytes 1572872 | tf_op jit(solution)/shard_map/ppermute | solution.py:422
  17.0 20.3 %collective-permute-start.1 = (f32[2,256,256]{2,1,0:T(8,128)}, f32[2,256,256]{2,1,0:T(8,128)S(1)}, u32[]{:S(2)}, u32[]{:S(2)}) collective-permute-start(f32[2,256,256]{2,1,0:T(8,128)} %get-tuple-element.29), channel_id=1, source_target_pairs={{0,15},{1,0},{2,1},{3,2},{4,3},{5,4},{6,5},{7,6},{8,7},{9,8},{10,9... | collective-permute-start | bytes 1572872 | tf_op jit(solution)/shard_map/ppermute | solution.py:420
  18.7 18.6 %collective-permute-start.2 = (f32[2,256,256]{2,1,0:T(8,128)}, f32[2,256,256]{2,1,0:T(8,128)S(1)}, u32[]{:S(2)}, u32[]{:S(2)}) collective-permute-start(f32[2,256,256]{2,1,0:T(8,128)} %get-tuple-element.30), channel_id=1, source_target_pairs={{16,15},{17,0},{18,1},{19,2},{20,3},{21,4},{22,5},{23,6},{24,7},{2... | collective-permute-start | bytes 1572872 | tf_op jit(solution)/shard_map/ppermute | solution.py:421
  26.1 12.6 %all-to-all-start.2 = ((f32[16,16,256]{2,1,0:T(8,128)}), f32[16,16,256]{2,1,0:T(8,128)S(1)}, u32[]{:S(2)}, u32[]{:S(2)}) async-start(f32[16,16,256]{2,1,0:T(8,128)} %shard_map.77), calls=%async_computation.2 | async-start | bytes 524288 | tf_op jit(solution)/shard_map/all_to_all | solution.py:430
  29.9 8.8 %copy-start.3 = (f32[2,256,256]{2,1,0:T(8,128)}, f32[2,256,256]{2,1,0:T(8,128)S(1)}, u32[]{:S(2)}) copy-start(f32[2,256,256]{2,1,0:T(8,128)S(1)} %collective-permute-done.below) | copy-start | bytes 1572868
  37.3 1.4 %copy-start.4 = (f32[2,256,256]{2,1,0:T(8,128)}, f32[2,256,256]{2,1,0:T(8,128)S(1)}, u32[]{:S(2)}) copy-start(f32[2,256,256]{2,1,0:T(8,128)S(1)} %collective-permute-done.1.side) | copy-start | bytes 1572868
  37.3 1.4 %copy-start.5 = (f32[2,256,256]{2,1,0:T(8,128)}, f32[2,256,256]{2,1,0:T(8,128)S(1)}, u32[]{:S(2)}) copy-start(f32[2,256,256]{2,1,0:T(8,128)S(1)} %collective-permute-done.2.slant) | copy-start | bytes 1572868
  38.7 0.7 copy-start.1
  39.4 25.6 %copy-start.2 = (s32[128,2]{0,1:T(2,128)S(1)}, s32[128,2]{0,1:T(2,128)}, u32[]{:S(2)}) copy-start(s32[128,2]{0,1:T(2,128)} %param.11) | copy-start | bytes 3076
  49.9 16.3 %collective-permute-start.3 = (f32[2,2,256,256]{3,2,1,0:T(8,128)}, f32[2,2,256,256]{3,2,1,0:T(8,128)S(1)}, u32[]{:S(2)}, u32[]{:S(2)}) collective-permute-start(f32[2,2,256,256]{3,2,1,0:T(8,128)} %get-tuple-element.32), channel_id=1, source_target_pairs={{0,16},{1,17},{2,18},{3,19},{4,20},{5,21},{6,22},{7,23},{8,24},{9,... | collective-permute-start | bytes 3145736 | tf_op jit(solution)/shard_map/ppermute | solution.py:437
  60.2 27.7 %collective-permute-start.4 = (f32[2,256,256]{2,1,0:T(8,128)}, f32[2,256,256]{2,1,0:T(8,128)}, u32[]{:S(2)}, u32[]{:S(2)}) collective-permute-start(f32[2,256,256]{2,1,0:T(8,128)} %get-tuple-element.33.own), channel_id=1, source_target_pairs={{15,0},{0,1},{1,2},{2,3},{3,4},{4,5},{5,6},{6,7},{7,8},{8,9},{9,10... | collective-permute-start | bytes 1572872 | tf_op jit(solution)/shard_map/ppermute | solution.py:438
  61.2 26.7 %collective-permute-start.5 = (f32[2,256,256]{2,1,0:T(8,128)}, f32[2,256,256]{2,1,0:T(8,128)}, u32[]{:S(2)}, u32[]{:S(2)}) collective-permute-start(f32[2,256,256]{2,1,0:T(8,128)} %get-tuple-element.33.own), channel_id=1, source_target_pairs={{0,16},{1,17},{2,18},{3,19},{4,20},{5,21},{6,22},{7,23},{8,24},{9,... | collective-permute-start | bytes 1572872 | tf_op jit(solution)/shard_map/ppermute | solution.py:439
  63.1 25.1 %collective-permute-start.6 = (f32[2,256,256]{2,1,0:T(8,128)}, f32[2,256,256]{2,1,0:T(8,128)}, u32[]{:S(2)}, u32[]{:S(2)}) collective-permute-start(f32[2,256,256]{2,1,0:T(8,128)} %get-tuple-element.33.own), channel_id=1, source_target_pairs={{15,16},{0,17},{1,18},{2,19},{3,20},{4,21},{5,22},{6,23},{7,24},{8... | collective-permute-start | bytes 1572872 | tf_op jit(solution)/shard_map/ppermute | solution.py:440
  89.4 25.5 %all-to-all-start.3 = ((f32[64,16,256]{2,1,0:T(8,128)}), f32[64,16,256]{2,1,0:T(8,128)S(1)}, u32[]{:S(2)}, u32[]{:S(2)}) async-start(f32[64,16,256]{2,1,0:T(8,128)} %shard_map.80), calls=%async_computation.3 | async-start | bytes 2097152 | tf_op jit(solution)/shard_map/all_to_all | solution.py:448
  114.9 4.7 %collective-permute-start.7 = (f32[2,2,256,256]{3,2,1,0:T(8,128)S(1)}, f32[2,2,256,256]{3,2,1,0:T(8,128)S(1)}, u32[]{:S(2)}, u32[]{:S(2)}) collective-permute-start(f32[2,2,256,256]{3,2,1,0:T(8,128)S(1)} %bitcast.11), channel_id=1, source_target_pairs={{0,16},{1,17},{2,18},{3,19},{4,20},{5,21},{6,22},{7,23},{8,24},{9,... | collective-permute-start | bytes 3145736 | tf_op jit(solution)/shard_map/ppermute | solution.py:456

commit v3 on v2

--- a/solution.py
+++ b/solution.py
@@ -29,16 +29,17 @@
 def dft_tables():
     n = np.arange(HALF)[:, None]
     q = np.arange(HALF)[None, :]
-    out = []
+    plain, turned = [], []
     for k in (2 * q, 2 * q + 1):
         angle = 2.0 * math.pi * ((n * k) % W) / W
         c = np.cos(angle) / math.sqrt(W)
         s = np.sin(angle) / math.sqrt(W)
         m = np.block([[c, -s], [s, c]])
-        for t in (m, m.T):
+        for t, out in ((m, plain), (m.T, turned)):
             hi = t.astype(ml_dtypes.bfloat16)
             lo = (t - hi.astype(np.float64)).astype(ml_dtypes.bfloat16)
             out += [hi, lo]
+    out = plain + turned
     order = np.concatenate([np.arange(0, W, 2), np.arange(1, W, 2)])
     perm = np.zeros((W, W))
     perm[np.arange(W), order] = 1.0
@@ -94,35 +95,50 @@
     return copies
 
 
-def send_kernel(offs_hbm, tile, first, second, side, own, offs, t_buf, f_buf, s_buf, o_buf, w_buf, sems):
+def send_up_kernel(offs_hbm, tile, first, second, offs, t_buf, f_buf, s_buf, sems):
     row, col, core = coords()
-    loads = fetch([(offs_hbm, offs), (tile.at[0], t_buf.at[0]), (tile.at[1], t_buf.at[1])], sems)
+    loads = fetch([(offs_hbm, offs)] + [(tile.at[i, pl.ds(0, W)], t_buf.at[i]) for i in range(2)], sems)
+    loads[0].wait()
+    _, c = corner(offs, row - 1, col)
+    b = iota((W, W), 1)
+    c1 = jnp.where(core == 1, 0, c)
+    c2 = jnp.where(core == 1, c, 0)
+    stores = []
+    for i in range(2):
+        loads[1 + i].wait()
+        f_buf[i] = jnp.where(b >= c1, t_buf[i, :, :W], t_buf[i, :, W:])
+        stores += fetch([(f_buf.at[i], first.at[i])], sems.at[pl.ds(3 + 2 * i, 1)])
+        s_buf[i] = jnp.where(b >= c2, t_buf[i, :, :W], t_buf[i, :, W:])
+        stores += fetch([(s_buf.at[i], second.at[i])], sems.at[pl.ds(4 + 2 * i, 1)])
+    for copy in stores:
+        copy.wait()
+
+
+def send_side_kernel(offs_hbm, tile, below, side, own, offs, t_buf, b_buf, o_buf, w_buf, sems):
+    row, col, core = coords()
+    loads = fetch([(offs_hbm, offs)], sems)
+    for i in range(2):
+        loads += fetch([(tile.at[i], t_buf.at[i]), (below.at[i], b_buf.at[i])], sems.at[pl.ds(1 + 2 * i, 2)])
     loads[0].wait()
     even = core == 0
-    _, c_up = corner(offs, row - 1, col)
     r_s, c_s = corner(offs, row, col)
     r_b, _ = corner(offs, row, col - 1)
-    c1 = jnp.where(even, c_up, 0)
-    c2 = jnp.where(even, 0, c_up)
     r_side, c_side = jnp.where(even, r_b, r_s), jnp.where(even, 0, c_s)
     r_own, c_own = jnp.where(even, r_s, r_b), jnp.where(even, c_s, 0)
     a = iota((W, W), 0)
     b = iota((W, W), 1)
     stores = []
     for i in range(2):
-        loads[1 + i].wait()
-        f_buf[i] = jnp.where(b >= c1, t_buf[i, :W, :W], t_buf[i, :W, W:])
-        stores += fetch([(f_buf.at[i], first.at[i])], sems.at[pl.ds(3 + 4 * i, 1)])
-        s_buf[i] = jnp.where(b >= c2, t_buf[i, :W, :W], t_buf[i, :W, W:])
-        stores += fetch([(s_buf.at[i], second.at[i])], sems.at[pl.ds(4 + 4 * i, 1)])
+        loads[1 + 2 * i].wait()
+        loads[2 + 2 * i].wait()
         top = jnp.where(b >= c_side, t_buf[i, :W, :W], t_buf[i, :W, W:])
         low = jnp.where(b >= c_side, t_buf[i, W:, :W], t_buf[i, W:, W:])
-        o_buf[i] = jnp.where(a >= r_side, top, low)
-        stores += fetch([(o_buf.at[i], side.at[i])], sems.at[pl.ds(5 + 4 * i, 1)])
+        o_buf[i] = jnp.where(a >= r_side, top, jnp.where(a + W >= r_side, low, b_buf[i]))
+        stores += fetch([(o_buf.at[i], side.at[i])], sems.at[pl.ds(5 + 2 * i, 1)])
         top = jnp.where(b >= c_own, t_buf[i, :W, :W], t_buf[i, :W, W:])
         low = jnp.where(b >= c_own, t_buf[i, W:, :W], t_buf[i, W:, W:])
         w_buf[i] = jnp.where(a >= r_own, top, low)
-        stores += fetch([(w_buf.at[i], own.at[i])], sems.at[pl.ds(6 + 4 * i, 1)])
+        stores += fetch([(w_buf.at[i], own.at[i])], sems.at[pl.ds(6 + 2 * i, 1)])
     for copy in stores:
         copy.wait()
 
@@ -137,36 +153,39 @@
     return jnp.dot(a, b, preferred_element_type=F32)
 
 
+STRIP = 32
+
+
+def strips(rows):
+    return range(0, rows, STRIP)
+
+
+def put_split(ref, at, x):
+    hi, lo = split(x)
+    ref[0, pl.ds(at, STRIP)] = hi
+    ref[1, pl.ds(at, STRIP)] = lo
+
+
 def right(x, hi, lo):
-    xh, xl = split(x)
-    return mm(jnp.concatenate([xh, xh, xl], axis=1), jnp.concatenate([hi, lo, hi], axis=0))
+    return mm(jnp.concatenate([x[0], x[0], x[1]], axis=1), jnp.concatenate([hi, lo, hi], axis=0))
 
 
 def left(hi, lo, x):
-    xh, xl = split(x)
-    return mm(jnp.concatenate([hi, lo, hi], axis=1), jnp.concatenate([xh, xh, xl], axis=0))
-
-
-def halves(x, axis):
-    first = lax.slice_in_dim(x, 0, HALF, axis=axis)
-    second = lax.slice_in_dim(x, HALF, W, axis=axis)
-    return first, second
-
-
-def work_kernel(
-    offs_hbm, amp, own, below, side, slant, probe, tables, grad, give, keep, scale,
-    offs, a_buf, o_buf, b_buf, s_buf, d_buf, p_buf, t_buf, f_buf, m_buf, x_buf, g_buf, q_buf, sems,
+    return mm(jnp.concatenate([hi, lo, hi], axis=1), jnp.concatenate([x[0], x[0], x[1]], axis=0))
+
+
+def lanes(a, b):
+    return jnp.concatenate([a, b], axis=1)
+
+
+def forward_kernel(
+    offs_hbm, own, below, side, probe, tables, far, mag, patch, scale,
+    offs, o_buf, b_buf, s_buf, p_buf, t_buf, f_buf, m_buf, x_buf, g_buf, rows_in, cols_in, h_buf, sems,
 ):
     row, col, core = coords()
-    loads = fetch(
-        [
-            (offs_hbm, offs), (own, o_buf), (below, b_buf), (side, s_buf), (slant, d_buf),
-            (tables, t_buf), (amp, a_buf),
-        ],
-        sems,
-    )
-    order = [(t + 2 * (1 - core)) % MODES for t in range(MODES)]
-    p_loads = fetch([(probe.at[order[t]], p_buf.at[t]) for t in range(MODES)], sems.at[pl.ds(7, MODES)])
+    loads = fetch([(offs_hbm, offs), (own, o_buf), (below, b_buf), (side, s_buf)], sems)
+    p_loads = fetch([(probe.at[0], p_buf.at[0])], sems.at[pl.ds(4, 1)])
+    loads += fetch([(tables.at[pl.ds(0, 4)], t_buf.at[pl.ds(0, 4)])], sems.at[pl.ds(5, 1)])
     loads[0].wait()
     r, c = corner(offs, row, jnp.where(core == 0, col, col - 1))
     a = iota((W, W), 0)
@@ -175,44 +194,83 @@
     use_side = beyond != core
     row_shift = (2 * W - r) % W
     col_shift = (2 * W - c) % W
-    for n in range(1, 5):
+    for n in range(1, 4):
         loads[n].wait()
-    for i in range(2):
-        whole = jnp.where(
-            a + W >= r, jnp.where(use_side, s_buf[i], o_buf[i]), jnp.where(use_side, d_buf[i], b_buf[i])
-        )
+    loads += fetch([(tables.at[pl.ds(4, 4)], t_buf.at[pl.ds(4, 4)])], sems.at[pl.ds(15, 1)])
+    p_loads += fetch([(probe.at[m], p_buf.at[m]) for m in range(1, MODES)], sems.at[pl.ds(6, MODES - 1)])
+    for i in range(2):
+        whole = jnp.where(use_side, s_buf[i], jnp.where(a + W >= r, o_buf[i], b_buf[i]))
         x_buf[i] = pltpu.roll(pltpu.roll(whole, row_shift, 0), col_shift, 1)
+
+    stores = fetch([(x_buf, patch)], sems.at[pl.ds(9, 1)])
+
+    def enter(t):
+        p_loads[t].wait()
+        for k in strips(W):
+            at = pl.ds(k, STRIP)
+            p_re, p_im = p_buf[t, 0, at], p_buf[t, 1, at]
+            o_re, o_im = x_buf[0, at], x_buf[1, at]
+            e_re = p_re * o_re - p_im * o_im
+            e_im = p_re * o_im + p_im * o_re
+            power = p_re * p_re + p_im * p_im
+            g_buf[at] = power if t == 0 else g_buf[at] + power
+            r0, r1 = e_re[:, :HALF], e_re[:, HALF:]
+            i0, i1 = e_im[:, :HALF], e_im[:, HALF:]
+            put_split(rows_in.at[t, 0], k, lanes(r0 + r1, i0 + i1))
+            put_split(rows_in.at[t, 1], k, lanes(r0 - r1, i0 - i1))
+
+    def along_rows(t):
+        h_buf[t, 0] = right(rows_in[t, 0], t_buf[0], t_buf[1])
+        h_buf[t, 1] = right(rows_in[t, 1], t_buf[2], t_buf[3])
+        for k in strips(HALF):
+            near, away = pl.ds(k, STRIP), pl.ds(HALF + k, STRIP)
+            e0, e1 = h_buf[t, 0, near], h_buf[t, 0, away]
+            o0, o1 = h_buf[t, 1, near], h_buf[t, 1, away]
+            e_sum, e_dif, o_sum, o_dif = e0 + e1, e0 - e1, o0 + o1, o0 - o1
+            put_split(cols_in.at[t, 0], k, lanes(e_sum[:, :HALF], o_sum[:, :HALF]))
+            put_split(cols_in.at[t, 0], HALF + k, lanes(e_sum[:, HALF:], o_sum[:, HALF:]))
+            put_split(cols_in.at[t, 1], k, lanes(e_dif[:, :HALF], o_dif[:, :HALF]))
+            put_split(cols_in.at[t, 1], HALF + k, lanes(e_dif[:, HALF:], o_dif[:, HALF:]))
+
+    def along_cols(t):
+        f_buf[t, 0] = left(t_buf[4], t_buf[5], cols_in[t, 0])
+        f_buf[t, 1] = left(t_buf[6], t_buf[7], cols_in[t, 1])
+        stores.extend(fetch([(f_buf.at[t], far.at[t])], sems.at[pl.ds(10 + t, 1)]))
+        for k in strips(HALF):
+            near, away = pl.ds(k, STRIP), pl.ds(HALF + k, STRIP)
+            for p, at in ((0, near), (1, away)):
+                x, y = f_buf[t, p, near], f_buf[t, p, away]
+                z = x * x + y * y
+                m_buf[at] = z if t == 0 else m_buf[at] + z
+
+    enter(0)
+    loads[4].wait()
     loads[5].wait()
-    power = jnp.zeros((W, W), F32)
     for t in range(MODES):
-        p_loads[t].wait()
-        p_re = p_buf[t, 0]
-        p_im = p_buf[t, 1]
-        o_re = x_buf[0]
-        o_im = x_buf[1]
-        power += p_re * p_re + p_im * p_im
-        e_re = p_re * o_re - p_im * o_im
-        e_im = p_re * o_im + p_im * o_re
-        r0, r1 = halves(e_re, 1)
-        i0, i1 = halves(e_im, 1)
-        even = right(jnp.concatenate([r0 + r1, i0 + i1], axis=1), t_buf[0], t_buf[1])
-        odd = right(jnp.concatenate([r0 - r1, i0 - i1], axis=1), t_buf[4], t_buf[5])
-        h_re = jnp.concatenate([even[:, :HALF], odd[:, :HALF]], axis=1)
-        h_im = jnp.concatenate([even[:, HALF:], odd[:, HALF:]], axis=1)
-        r0, r1 = halves(h_re, 0)
-        i0, i1 = halves(h_im, 0)
-        even = left(t_buf[2], t_buf[3], jnp.concatenate([r0 + r1, i0 + i1], axis=0))
-        odd = left(t_buf[6], t_buf[7], jnp.concatenate([r0 - r1, i0 - i1], axis=0))
-        f_buf[t, 0] = even
-        f_buf[t, 1] = odd
-        if t == 0:
-            m_buf[:HALF] = even[:HALF] * even[:HALF] + even[HALF:] * even[HALF:]
-            m_buf[HALF:] = odd[:HALF] * odd[:HALF] + odd[HALF:] * odd[HALF:]
-        else:
-            m_buf[:HALF] += even[:HALF] * even[:HALF] + even[HALF:] * even[HALF:]
-            m_buf[HALF:] += odd[:HALF] * odd[:HALF] + odd[HALF:] * odd[HALF:]
-    scale[...] = jnp.full(scale.shape, 1.0 / (jnp.max(power) + 1e-05), F32)
-    loads[6].wait()
+        along_rows(t)
+        if t + 1 < MODES:
+            enter(t + 1)
+        along_cols(t)
+    for k in strips(W):
+        at = pl.ds(k, STRIP)
+        m_buf[at] = jnp.maximum(jnp.sqrt(m_buf[at]), 0.5)
+    stores += fetch([(m_buf, mag)], sems.at[pl.ds(14, 1)])
+    scale[...] = jnp.full(scale.shape, 1.0 / (jnp.max(g_buf[...]) + 1e-05), F32)
+    for copy in stores:
+        copy.wait()
+
+
+def backward_kernel(
+    offs_hbm, amp, far, mag, patch, probe, tables, grad, give, keep,
+    offs, a_buf, m_buf, t_buf, f_buf, x_buf, p_buf, g_buf, q_buf, rows_in, cols_in, h_buf, sems,
+):
+    row, col, core = coords()
+    order = [(t + 2 * (1 - core)) % MODES for t in range(MODES)]
+    loads = fetch([(amp, a_buf), (tables.at[pl.ds(8, 2)], t_buf.at[pl.ds(8, 2)]), (mag, m_buf)], sems)
+    t_loads = fetch([(tables.at[pl.ds(0, 4)], t_buf.at[pl.ds(0, 4)])], sems.at[pl.ds(19, 1)])
+    f_loads = fetch([(far.at[order[0]], f_buf.at[0])], sems.at[pl.ds(3, 1)])
+    loads[0].wait()
+    loads[1].wait()
     x = a_buf[...]
     for turn in range(2):
         p1 = x.astype(BF)
@@ -223,40 +281,76 @@
             x = mm(t_buf[8], p1) + mm(t_buf[8], p2) + mm(t_buf[8], p3)
         else:
             x = mm(p1, t_buf[9]) + mm(p2, t_buf[9]) + mm(p3, t_buf[9])
-    m_buf[...] = x / jnp.maximum(jnp.sqrt(m_buf[...]), 0.5) - 1.0
+    a_buf[...] = x
+    loads[2].wait()
+    f_loads[0].wait()
+    t_loads += fetch([(tables.at[pl.ds(4, 4)], t_buf.at[pl.ds(4, 4)])], sems.at[pl.ds(20, 1)])
+    loads += fetch([(patch, x_buf), (probe.at[order[0]], p_buf.at[0])], sems.at[pl.ds(4, 2)])
+    f_loads += fetch([(far.at[order[t]], f_buf.at[t]) for t in range(1, MODES)], sems.at[pl.ds(6, MODES - 1)])
+    p_loads = fetch([(probe.at[order[t]], p_buf.at[t]) for t in range(1, MODES)], sems.at[pl.ds(9, MODES - 1)])
+    loads += fetch([(offs_hbm, offs)], sems.at[pl.ds(12, 1)])
+    for k in strips(W):
+        at = pl.ds(k, STRIP)
+        m_buf[at] = a_buf[at] / m_buf[at] - 1.0
+
+    def weigh(t):
+        for k in strips(HALF):
+            near, away = pl.ds(k, STRIP), pl.ds(HALF + k, STRIP)
+            for p, at in ((0, near), (1, away)):
+                put_split(cols_in.at[t, p], k, f_buf[t, p, near] * m_buf[at])
+                put_split(cols_in.at[t, p], HALF + k, f_buf[t, p, away] * m_buf[at])
+
+    def back_cols(t):
+        h_buf[t, 0] = left(t_buf[0], t_buf[1], cols_in[t, 0])
+        h_buf[t, 1] = left(t_buf[2], t_buf[3], cols_in[t, 1])
+        for k in strips(HALF):
+            near, away = pl.ds(k, STRIP), pl.ds(HALF + k, STRIP)
+            u_re, v_re = h_buf[t, 0, near], h_buf[t, 1, near]
+            u_im, v_im = h_buf[t, 0, away], h_buf[t, 1, away]
+            for at, re, im in ((k, u_re + v_re, u_im + v_im), (HALF + k, u_re - v_re, u_im - v_im)):
+                put_split(rows_in.at[t, 0], at, lanes(re[:, :HALF], im[:, :HALF]))
+                put_split(rows_in.at[t, 1], at, lanes(re[:, HALF:], im[:, HALF:]))
+
     stores = []
+
+    def back_rows(t):
+        h_buf[t, 0] = right(rows_in[t, 0], t_buf[4], t_buf[5])
+        h_buf[t, 1] = right(rows_in[t, 1], t_buf[6], t_buf[7])
+        for k in strips(W):
+            at = pl.ds(k, STRIP)
+            u, v = h_buf[t, 0, at], h_buf[t, 1, at]
+            add, sub = u + v, u - v
+            b_re = lanes(add[:, :HALF], sub[:, :HALF])
+            b_im = lanes(add[:, HALF:], sub[:, HALF:])
+            p_re, p_im = p_buf[t, 0, at], p_buf[t, 1, at]
+            o_re, o_im = x_buf[0, at], x_buf[1, at]
+            g_re = p_re * b_re + p_im * b_im
+            g_im = p_re * b_im - p_im * b_re
+            g_buf[0, at] = g_re if t == 0 else g_buf[0, at] + g_re
+            g_buf[1, at] = g_im if t == 0 else g_buf[1, at] + g_im
+            q_buf[t, 0, at] = o_re * b_re + o_im * b_im
+            q_buf[t, 1, at] = o_re * b_im - o_im * b_re
+        target = give.at[t] if t < 2 else keep.at[t - 2]
+        stores.extend(fetch([(q_buf.at[t], target)], sems.at[pl.ds(13 + t, 1)]))
+
+    weigh(0)
+    t_loads[0].wait()
     for t in range(MODES):
-        f_even = m_buf[:HALF]
-        f_odd = m_buf[HALF:]
-        even = f_buf[t, 0] * jnp.concatenate([f_even, f_even], axis=0)
-        odd = f_buf[t, 1] * jnp.concatenate([f_odd, f_odd], axis=0)
-        u = left(t_buf[0], t_buf[1], even)
-        v = left(t_buf[4], t_buf[5], odd)
-        h_re = jnp.concatenate([u[:HALF] + v[:HALF], u[:HALF] - v[:HALF]], axis=0)
-        h_im = jnp.concatenate([u[HALF:] + v[HALF:], u[HALF:] - v[HALF:]], axis=0)
-        u = right(jnp.concatenate([h_re[:, :HALF], h_im[:, :HALF]], axis=1), t_buf[2], t_buf[3])
-        v = right(jnp.concatenate([h_re[:, HALF:], h_im[:, HALF:]], axis=1), t_buf[6], t_buf[7])
-        b_re = jnp.concatenate([u[:, :HALF] + v[:, :HALF], u[:, :HALF] - v[:, :HALF]], axis=1)
-        b_im = jnp.concatenate([u[:, HALF:] + v[:, HALF:], u[:, HALF:] - v[:, HALF:]], axis=1)
-        p_re = p_buf[t, 0]
-        p_im = p_buf[t, 1]
-        o_re = x_buf[0]
-        o_im = x_buf[1]
-        g_re = p_re * b_re + p_im * b_im
-        g_im = p_re * b_im - p_im * b_re
+        back_cols(t)
         if t == 0:
-            g_buf[0] = g_re
-            g_buf[1] = g_im
-        else:
-            g_buf[0] += g_re
-            g_buf[1] += g_im
-        q_buf[t, 0] = o_re * b_re + o_im * b_im
-        q_buf[t, 1] = o_re * b_im - o_im * b_re
-        target = give.at[t] if t < 2 else keep.at[t - 2]
-        stores += fetch([(q_buf.at[t], target)], sems.at[pl.ds(11 + t, 1)])
+            t_loads[1].wait()
+            loads[3].wait()
+            loads[4].wait()
+        if t + 1 < MODES:
+            f_loads[t + 1].wait()
+            weigh(t + 1)
+            p_loads[t].wait()
+        back_rows(t)
+    loads[5].wait()
+    r, c = corner(offs, row, jnp.where(core == 0, col, col - 1))
     for i in range(2):
         g_buf[i] = pltpu.roll(pltpu.roll(g_buf[i], r % W, 0), c % W, 1)
-        stores += fetch([(g_buf.at[i], grad.at[i])], sems.at[pl.ds(15 + i, 1)])
+        stores += fetch([(g_buf.at[i], grad.at[i])], sems.at[pl.ds(17 + i, 1)])
     for copy in stores:
         copy.wait()
 
@@ -361,21 +455,21 @@
         copy.wait()
 
 
-def probe_kernel(probe, mine, theirs, out, p_buf, m_buf, o_buf, sems):
+def probe_kernel(first, probe, total, *refs):
+    out, p_buf, m_buf, o_buf, sems = refs[-5:]
     core = lax.axis_index("core")
-    order = [(m + 2 * core) % MODES for m in range(MODES)]
+    base = 2 * jnp.where(first, core, 1 - core)
     loads = []
-    for t in range(MODES):
-        src = mine.at[t] if t < 2 else theirs.at[t - 2]
+    for t in range(2):
         loads.append(
-            fetch([(probe.at[order[t]], p_buf.at[t]), (src, m_buf.at[t])], sems.at[pl.ds(2 * t, 2)])
+            fetch([(probe.at[base + t], p_buf.at[t]), (total.at[t], m_buf.at[t])], sems.at[pl.ds(2 * t, 2)])
         )
     stores = []
-    for t in range(MODES):
+    for t in range(2):
         for copy in loads[t]:
             copy.wait()
         o_buf[t] = p_buf[t] + m_buf[t] * (1.0 / (NR * NC))
-        stores += fetch([(o_buf.at[t], out.at[order[t]])], sems.at[pl.ds(8 + t, 1)])
+        stores += fetch([(o_buf.at[t], out.at[base + t])], sems.at[pl.ds(4 + t, 1)])
     for copy in stores:
         copy.wait()
 
@@ -384,10 +478,10 @@
 VMEM = pl.BlockSpec(memory_space=pltpu.VMEM)
 HBM = pl.BlockSpec(memory_space=pltpu.HBM)
 PIECE = (2, W, W)
-WORK_MB = 58
-
-
-def call(kernel, outs, ins, scratch, sems, *args, flops=0, data=0, out_specs=None, mb=62):
+WORK_MB = 60
+
+
+def call(kernel, outs, ins, scratch, sems, *args, flops=0, data=0, out_specs=None, mb=62, alias=()):
     shapes = [jax.ShapeDtypeStruct(s, F32) for s in outs]
     buffers = [pltpu.VMEM(s, F32) if isinstance(s, tuple) else s for s in scratch]
     return pl.pallas_call(
@@ -395,6 +489,7 @@
         out_shape=shapes,
         in_specs=ins,
         out_specs=out_specs or [HBM] * len(outs),
+        input_output_aliases=dict(alias),
         scratch_shapes=buffers + [pltpu.SemaphoreType.DMA((sems,))],
         compiler_params=pltpu.CompilerParams(vmem_limit_bytes=mb * 2**20),
         cost_estimate=pl.CostEstimate(flops=flops, bytes_accessed=data, transcendentals=0),
@@ -410,16 +505,21 @@
     owner = owner.reshape(1, NR * NC)
     modes = (MODES, 2, W, W)
     half = (2, 2, W, W)
+    split_buf = pltpu.VMEM((MODES, 2, 2, W, W), BF)
     table_buf = pltpu.VMEM(tables.shape, BF)
     offs_buf = pltpu.SMEM(offsets.shape, jnp.int32)
     owner_buf = pltpu.SMEM(owner.shape, jnp.int32)
-    first, second, side, own = call(
-        send_kernel, [PIECE] * 4, [HBM] * 2, [offs_buf, (2, TILE, TILE), PIECE, PIECE, PIECE, PIECE], 11,
-        offsets, object_field, data=4 << 20,
+    first, second = call(
+        send_up_kernel, [PIECE] * 2, [HBM] * 2, [offs_buf, (2, W, TILE), PIECE, PIECE], 7,
+        offsets, object_field, data=3 << 20,
+    )
+    below_first = lax.ppermute(first, ALL, UP)
+    below = lax.ppermute(second, ALL, UP)
+    side, own = call(
+        send_side_kernel, [PIECE] * 2, [HBM] * 3, [offs_buf, (2, TILE, TILE), PIECE, PIECE, PIECE], 9,
+        offsets, object_field, below_first, data=4 << 20,
     )
     side = lax.ppermute(side, ALL, SIDE)
-    slant = lax.ppermute(first, ALL, SLANT)
-    below = lax.ppermute(second, ALL, UP)
     spread = measured.reshape(CAP, NC, CHUNK, W).transpose(1, 0, 2, 3)
     spread = lax.all_to_all(spread, COL, 0, 0, tiled=True)
     slots = (NC * CAP, CHUNK, W)
@@ -428,11 +528,19 @@
         owner, spread.reshape(slots), data=1 << 20, mb=50,
     )[0]
     amp = lax.all_to_all(picked, COL, 0, 0, tiled=True).reshape(W, W)
-    grad, give, keep, scale = call(
-        work_kernel, [PIECE, half, half, (8, 128)], [HBM] * 8,
-        [offs_buf, (W, W), PIECE, PIECE, PIECE, PIECE, modes, table_buf, modes, (W, W), PIECE, PIECE, modes], 17,
-        offsets, amp, own, below, side, slant, probe, tables,
-        flops=2 * 96 * W**3, data=10 << 20, out_specs=[HBM, HBM, HBM, VMEM], mb=WORK_MB,
+    far, mag, patch, scale = call(
+        forward_kernel, [modes, (W, W), PIECE, (8, 128)], [HBM] * 6,
+        [offs_buf, PIECE, PIECE, PIECE, modes, pltpu.VMEM((8, W, W), BF), modes, (W, W), PIECE, (W, W),
+         split_buf, split_buf, modes], 16,
+        offsets, own, below, side, probe, tables,
+        flops=2 * 48 * W**3, data=8 << 20, out_specs=[HBM, HBM, HBM, VMEM], mb=WORK_MB,
+    )
+    grad, give, keep = call(
+        backward_kernel, [PIECE, half, half], [HBM] * 7,
+        [offs_buf, (W, W), (W, W), table_buf, modes, PIECE, modes, PIECE, modes,
+         split_buf, split_buf, modes], 21,
+        offsets, amp, far, mag, patch, probe, tables,
+        flops=2 * 48 * W**3, data=8 << 20, mb=WORK_MB,
     )
     taken = lax.ppermute(give, ALL, SWAP)
     got = lax.ppermute(grad, ALL, back(SIDE))
@@ -455,7 +563,12 @@
     mine = mine.reshape(half)
     theirs = lax.ppermute(mine, ALL, SWAP)
     new_probe = call(
-        probe_kernel, [modes], [HBM] * 3, [modes, modes, modes], 12, probe, mine, theirs, data=6 << 20, mb=50,
+        functools.partial(probe_kernel, True), [modes], [HBM] * 2, [half, half, half], 6,
+        probe, mine, data=3 << 20, mb=50,
+    )[0]
+    new_probe = call(
+        functools.partial(probe_kernel, False), [modes], [HBM] * 3, [half, half, half], 6,
+        probe, theirs, new_probe, data=3 << 20, mb=50, alias=((2, 0),),
     )[0]
     return (new_object, new_probe)
 

time: 123 us -> 118 us (0.959)
  starting transfers between devices: 48.4 us -> 38.6 us
  Pallas kernels: 23.3 us -> 29.2 us
  waiting for transfers between devices: 24.1 us -> 21.3 us
  local copies, waits for them, and re-layouts: 3.29 us -> 5.32 us
    all_to_all x1, waiting for transfers between devices: 0.57 us -> 9.33 us  [shards(): spread = lax.all_to_all(spread, COL, 0, 0, tiled=True)]
    ppermute x1, starting transfers between devices: 10.3 us -> 1.6 us  [shards(): taken = lax.ppermute(give, ALL, SWAP)]
    ppermute x1, waiting for transfers between devices: 7.36 us -> 0.01 us  [shards(): side = lax.ppermute(side, ALL, SIDE)]
    pallas_call x6 -> x9, Pallas kernels: 23.3 us -> 29.2 us  [call(): pl.pallas_call(kernel, out_shape=shapes, in_specs=ins, out_specs=out_spec...]
    ppermute x1, starting transfers between devices: 1.92 us -> 5.54 us  [shards(): above_second = lax.ppermute(grad, ALL, back(SLANT))]
    unnamed x12 -> x16, local copies, waits for them, and re-layouts: 0.71 us -> 3.87 us
    ppermute x1, waiting for transfers between devices: 2.29 us -> 0.01 us  [shards(): theirs = lax.ppermute(mine, ALL, SWAP)]
    ppermute x1, starting transfers between devices: 5.35 us -> 3.46 us  [shards(): below_first = lax.ppermute(first, ALL, UP)]
  transfers between devices with their start and end apart: 11 -> 11, of which waited for: 6 -> 3; matrix products, arithmetic and copies ran while one was open for 1% -> 1% of each run, Pallas kernels for 7% -> 15%
where the time goes in v3:
time: 118 us; the launch traced here: 117 us
  starting transfers between devices  38.6 us (33%)
  Pallas kernels  29.2 us (25%)
  waiting for transfers between devices  21.3 us (18%)
  blocking collectives  20.8 us (18%)
  local copies, waits for them, and re-layouts  5.32 us (5%)
  between operations  1.5 us (1%)
    pallas_call x9, Pallas kernels, call(): pl.pallas_call(kernel, out_shape=shapes, in_specs=ins, out_specs=out_spec...  29.2 us
    all_to_all x1, blocking collectives, exchange(): return lax.all_to_all(x, CHIPS, 0, 0, tiled=True)  20.8 us
    all_to_all x1, waiting for transfers between devices, shards(): mine = lax.all_to_all(copies, CHIPS, 0, 0, tiled=True)  11.5 us
    all_to_all x1, waiting for transfers between devices, shards(): spread = lax.all_to_all(spread, COL, 0, 0, tiled=True)  9.33 us
    all_to_all x1, starting transfers between devices, shards(): spread = lax.all_to_all(spread, COL, 0, 0, tiled=True)  7.98 us
    all_to_all x1, starting transfers between devices, shards(): mine = lax.all_to_all(copies, CHIPS, 0, 0, tiled=True)  6.54 us
    ppermute x1, starting transfers between devices, shards(): above_second = lax.ppermute(grad, ALL, back(SLANT))  5.54 us
    unnamed x16, local copies, waits for them, and re-layouts  3.87 us
  transfers between devices with their start and end apart: 11, of which 3 were waited for; matrix products, arithmetic and copies ran while one was open for 1% of the time, Pallas kernels for 15%

profile of v3, /device:TPU:1, one launch (start us, length us, event | category | flops | bytes accessed | tf_op | source)
XLA Modules:
  0.0 116.9 jit_solution(4452706720819016431)
XLA Ops:
  0.6 2.2 %shard_map.78 = (f32[2,256,256]{2,1,0:T(8,128)}, f32[2,256,256]{2,1,0:T(8,128)}) custom-call(s32[2,128]{1,0:T(2,128)} %bitcast.18, f32[2,512,512]{2,1,0:T(8,128)} %tile.5), custom_call_target="tpu_custom_call" | custom-call | bytes 3145728 | tf_op jit(solution)/shard_map/pallas_call | solution.py:487
  2.8 3.5 %collective-permute-start = (f32[2,256,256]{2,1,0:T(8,128)}, f32[2,256,256]{2,1,0:T(8,128)S(1)}, u32[]{:S(2)}, u32[]{:S(2)}) collective-permute-start(f32[2,256,256]{2,1,0:T(8,128)} %get-tuple-element.30), channel_id=1, source_target_pairs={{16,0},{17,1},{18,2},{19,3},{20,4},{21,5},{22,6},{23,7},{24,8},{25... | collective-permute-start | bytes 1572872 | tf_op jit(solution)/shard_map/ppermute | solution.py:516
  7.2 8.0 %all-to-all-start.1 = ((f32[16,3,16,256]{3,2,1,0:T(8,128)}), f32[16,3,16,256]{3,2,1,0:T(8,128)S(1)}, u32[]{:S(2)}, u32[]{:S(2)}) async-start(f32[16,3,16,256]{3,2,1,0:T(8,128)} %bitcast.10), calls=%async_computation.1 | async-start | bytes 1572864 | tf_op jit(solution)/shard_map/all_to_all | solution.py:524
  15.2 1.9 %collective-permute-start.1 = (f32[2,256,256]{2,1,0:T(8,128)S(1)}, f32[2,256,256]{2,1,0:T(8,128)}, u32[]{:S(2)}, u32[]{:S(2)}) collective-permute-start(f32[2,256,256]{2,1,0:T(8,128)S(1)} %copy-done.6), channel_id=1, source_target_pairs={{16,0},{17,1},{18,2},{19,3},{20,4},{21,5},{22,6},{23,7},{24,8},{25... | collective-permute-start | bytes 1572872 | tf_op jit(solution)/shard_map/ppermute | solution.py:517
  18.0 2.6 %shard_map.79 = (f32[2,256,256]{2,1,0:T(8,128)}, f32[2,256,256]{2,1,0:T(8,128)}) custom-call(s32[2,128]{1,0:T(2,128)} %bitcast.19, f32[2,512,512]{2,1,0:T(8,128)} %tile.5, f32[2,256,256]{2,1,0:T(8,128)} %copy-done.4), custom_call_target="tpu_custom_call" | custom-call | bytes 4194304 | tf_op jit(solution)/shard_map/pallas_call | solution.py:487
  20.6 1.4 %collective-permute-start.2 = (f32[2,256,256]{2,1,0:T(8,128)}, f32[2,256,256]{2,1,0:T(8,128)S(1)}, u32[]{:S(2)}, u32[]{:S(2)}) collective-permute-start(f32[2,256,256]{2,1,0:T(8,128)} %get-tuple-element.33), channel_id=1, source_target_pairs={{0,15},{1,0},{2,1},{3,2},{4,3},{5,4},{6,5},{7,6},{8,7},{9,8},{10,9... | collective-permute-start | bytes 1572872 | tf_op jit(solution)/shard_map/ppermute | solution.py:522
  22.0 9.3 %all-to-all-done.1 = f32[16,3,16,256]{3,2,1,0:T(8,128)S(1)} async-done(((f32[16,3,16,256]{3,2,1,0:T(8,128)}), f32[16,3,16,256]{3,2,1,0:T(8,128)S(1)}, u32[]{:S(2)}, u32[]{:S(2)}) %all-to-all-start.1) | async-done | bytes 786464 | tf_op jit(solution)/shard_map/all_to_all | solution.py:524
  31.4 1.4 %shard_map.77 = f32[16,16,256]{2,1,0:T(8,128)} custom-call(s32[1,128]{1,0:T(1,128)S(1)} %bitcast.14, f32[48,16,256]{2,1,0:T(8,128)S(1)} %bitcast.13), custom_call_target="tpu_custom_call" | custom-call | bytes 1048576 | tf_op jit(solution)/shard_map/pallas_call | solution.py:487
  32.8 3.5 %all-to-all-start.2 = ((f32[16,16,256]{2,1,0:T(8,128)}), f32[16,16,256]{2,1,0:T(8,128)S(1)}, u32[]{:S(2)}, u32[]{:S(2)}) async-start(f32[16,16,256]{2,1,0:T(8,128)} %shard_map.77), calls=%async_computation.2 | async-start | bytes 524288 | tf_op jit(solution)/shard_map/all_to_all | solution.py:530
  37.2 6.8 %shard_map.80 = (f32[4,2,256,256]{3,2,1,0:T(8,128)}, f32[256,256]{1,0:T(8,128)}, f32[2,256,256]{2,1,0:T(8,128)}, f32[8,128]{1,0:T(8,128)}) custom-call(s32[2,128]{1,0:T(2,128)} %bitcast.20, f32[2,256,256]{2,1,0:T(8,128)} %get-tuple-element.31.own, f32[2,256,256]{2,1,0:T(8,128)} %collective-permute-done.1.below, f32[2,256,256]{2,1,0:T(8,128)} %copy-done.7, ...), custom_call_target="tpu_custom_call" | custom-call | flops 1610612736 | bytes 8388608 | tf_op jit(solution)/shard_map/pallas_call | solution.py:487
  45.1 7.6 %shard_map.81 = (f32[2,256,256]{2,1,0:T(8,128)}, f32[2,2,256,256]{3,2,1,0:T(8,128)}, f32[2,2,256,256]{3,2,1,0:T(8,128)S(1)}) custom-call(s32[2,128]{1,0:T(2,128)} %bitcast.21, f32[256,256]{1,0:T(8,128)} %bitcast.16, f32[4,2,256,256]{3,2,1,0:T(8,128)} %get-tuple-element.34.far, f32[256,256]{1,0:T(8,128)} %get-tuple-element.35.mag, ...), custom_call_target="tpu_custom_call" | custom-call | flops 1610612736 | bytes 8388608 | tf_op jit(solution)/shard_map/pallas_call | solution.py:487
  52.7 1.6 %collective-permute-start.3 = (f32[2,2,256,256]{3,2,1,0:T(8,128)}, f32[2,2,256,256]{3,2,1,0:T(8,128)S(1)}, u32[]{:S(2)}, u32[]{:S(2)}) collective-permute-start(f32[2,2,256,256]{3,2,1,0:T(8,128)} %get-tuple-element.38), channel_id=1, source_target_pairs={{0,16},{1,17},{2,18},{3,19},{4,20},{5,21},{6,22},{7,23},{8,24},{9,... | collective-permute-start | bytes 3145736 | tf_op jit(solution)/shard_map/ppermute | solution.py:545
  54.3 5.5 %collective-permute-start.6 = (f32[2,256,256]{2,1,0:T(8,128)}, f32[2,256,256]{2,1,0:T(8,128)}, u32[]{:S(2)}, u32[]{:S(2)}) collective-permute-start(f32[2,256,256]{2,1,0:T(8,128)} %get-tuple-element.39.own), channel_id=1, source_target_pairs={{15,16},{0,17},{1,18},{2,19},{3,20},{4,21},{5,22},{6,23},{7,24},{8... | collective-permute-start | bytes 1572872 | tf_op jit(solution)/shard_map/ppermute | solution.py:548
  59.8 1.9 %collective-permute-start.5 = (f32[2,256,256]{2,1,0:T(8,128)}, f32[2,256,256]{2,1,0:T(8,128)}, u32[]{:S(2)}, u32[]{:S(2)}) collective-permute-start(f32[2,256,256]{2,1,0:T(8,128)} %get-tuple-element.39.own), channel_id=1, source_target_pairs={{0,16},{1,17},{2,18},{3,19},{4,20},{5,21},{6,22},{7,23},{8,24},{9,... | collective-permute-start | bytes 1572872 | tf_op jit(solution)/shard_map/ppermute | solution.py:547
  61.8 1.6 %collective-permute-start.4 = (f32[2,256,256]{2,1,0:T(8,128)}, f32[2,256,256]{2,1,0:T(8,128)}, u32[]{:S(2)}, u32[]{:S(2)}) collective-permute-start(f32[2,256,256]{2,1,0:T(8,128)} %get-tuple-element.39.own), channel_id=1, source_target_pairs={{15,0},{0,1},{1,2},{2,3},{3,4},{4,5},{5,6},{6,7},{7,8},{8,9},{9,10... | collective-permute-start | bytes 1572872 | tf_op jit(solution)/shard_map/ppermute | solution.py:546
  64.6 21.0 %conditional.1 = (f32[64,16,256]{2,1,0:T(8,128)S(1)}) conditional(s32[]{:T(128)} %bitcast.2, () %tuple.17, (f32[2,2,256,256]{3,2,1,0:T(8,128)S(1)}, f32[2,2,256,256]{3,2,1,0:T(8,128)S(1)}) %tuple.18), branch_computations={%region_0.0_spmd, %region_1.0_spmd} | conditional | flops 262144 | bytes 5242888 | solution.py:551
  64.7 20.8 %all_to_all.19 = f32[64,16,256]{2,1,0:T(8,128)S(1)} all-to-all(f32[64,16,256]{2,1,0:T(8,128)S(1)} %bitcast.15), channel_id=1, replica_groups=mesh['x'=4,'core'=2,'z'=4,'y'=4] {'x','z','y'}, dimensions={0} | all-to-all | bytes 2097152 | tf_op jit(solution)/shard_map/cond/branch_1_fun/all_to_all | solution.py:500
  85.6 1.2 %shard_map.82 = f32[64,16,256]{2,1,0:T(8,128)} custom-call(f32[64,16,256]{2,1,0:T(8,128)S(1)} %get-tuple-element.47.parts), custom_call_target="tpu_custom_call" | custom-call | bytes 2097152 | tf_op jit(solution)/shard_map/pallas_call | solution.py:487
  86.8 6.5 %all-to-all-start.3 = ((f32[64,16,256]{2,1,0:T(8,128)}), f32[64,16,256]{2,1,0:T(8,128)S(1)}, u32[]{:S(2)}, u32[]{:S(2)}) async-start(f32[64,16,256]{2,1,0:T(8,128)} %shard_map.82), calls=%async_computation.3 | async-start | bytes 2097152 | tf_op jit(solution)/shard_map/all_to_all | solution.py:556
  93.3 4.9 %shard_map.83 = f32[2,512,512]{2,1,0:T(8,128)} custom-call(s32[2,128]{1,0:T(2,128)} %bitcast.22, f32[8,128]{1,0:T(8,128)} %get-tuple-element.41.scale, f32[2,512,512]{2,1,0:T(8,128)} %tile.5, f32[2,256,256]{2,1,0:T(8,128)} %get-tuple-element.39.own, f32[2,256,256]{2,1,0:T(8,128)} %collective-permute-done.4.got, ...), custom_call_target="tpu_custom_call" | custom-call | bytes 6291456 | tf_op jit(solution)/shard_map/pallas_call | solution.py:487
  98.3 11.5 %all-to-all-done.3 = f32[64,16,256]{2,1,0:T(8,128)S(1)} async-done(((f32[64,16,256]{2,1,0:T(8,128)}), f32[64,16,256]{2,1,0:T(8,128)S(1)}, u32[]{:S(2)}, u32[]{:S(2)}) %all-to-all-start.3) | async-done | bytes 1048608 | tf_op jit(solution)/shard_map/all_to_all | solution.py:556
  109.7 3.1 %collective-permute-start.7 = (f32[2,2,256,256]{3,2,1,0:T(8,128)S(1)}, f32[2,2,256,256]{3,2,1,0:T(8,128)S(1)}, u32[]{:S(2)}, u32[]{:S(2)}) collective-permute-start(f32[2,2,256,256]{3,2,1,0:T(8,128)S(1)} %bitcast.11), channel_id=1, source_target_pairs={{0,16},{1,17},{2,18},{3,19},{4,20},{5,21},{6,22},{7,23},{8,24},{9,... | collective-permute-start | bytes 3145736 | tf_op jit(solution)/shard_map/ppermute | solution.py:564
  112.8 1.6 %copy-done = f32[4,2,256,256]{3,2,1,0:T(8,128)S(1)} copy-done((f32[4,2,256,256]{3,2,1,0:T(8,128)S(1)}, f32[4,2,256,256]{3,2,1,0:T(8,128)}, u32[]{:S(2)}) %copy-start) | copy-done | bytes 2097176
  115.6 1.2 %shard_map.85 = f32[4,2,256,256]{3,2,1,0:T(8,128)} custom-call(f32[4,2,256,256]{3,2,1,0:T(8,128)S(1)} %copy-done, f32[2,2,256,256]{3,2,1,0:T(8,128)S(1)} %collective-permute-done.7.total, f32[4,2,256,256]{3,2,1,0:T(8,128)} %shard_map.84.refs_0_), custom_call_target="tpu_custom_call", output_to_operand_aliasing={{}: (2, {})} | custom-call | bytes 3145728 | tf_op jit(solution)/shard_map/pallas_call | solution.py:487
  (28 shorter events, 5.6 us)
Async XLA Ops:
  0.6 5.7 %copy-start.3 = (f32[3,256,256]{2,1,0:T(8,128)S(1)}, f32[3,256,256]{2,1,0:T(8,128)}, u32[]{:S(2)}) copy-start(f32[3,256,256]{2,1,0:T(8,128)} %param.10) | copy-start | bytes 2359300
  2.8 12.4 %copy-start.6 = (f32[2,256,256]{2,1,0:T(8,128)S(1)}, f32[2,256,256]{2,1,0:T(8,128)}, u32[]{:S(2)}) copy-start(f32[2,256,256]{2,1,0:T(8,128)} %get-tuple-element.32) | copy-start | bytes 1572868
  2.8 14.3 %collective-permute-start = (f32[2,256,256]{2,1,0:T(8,128)}, f32[2,256,256]{2,1,0:T(8,128)S(1)}, u32[]{:S(2)}, u32[]{:S(2)}) collective-permute-start(f32[2,256,256]{2,1,0:T(8,128)} %get-tuple-element.30), channel_id=1, source_target_pairs={{16,0},{17,1},{18,2},{19,3},{20,4},{21,5},{22,6},{23,7},{24,8},{25... | collective-permute-start | bytes 1572872 | tf_op jit(solution)/shard_map/ppermute | solution.py:516
  7.2 24.1 %copy-start.1 = (s32[128]{0:T(128)S(1)}, s32[128]{0:T(128)}, u32[]{:S(2)}) copy-start(s32[128]{0:T(128)} %param.12) | copy-start | bytes 1540
  7.2 24.1 %all-to-all-start.1 = ((f32[16,3,16,256]{3,2,1,0:T(8,128)}), f32[16,3,16,256]{3,2,1,0:T(8,128)S(1)}, u32[]{:S(2)}, u32[]{:S(2)}) async-start(f32[16,3,16,256]{3,2,1,0:T(8,128)} %bitcast.10), calls=%async_computation.1 | async-start | bytes 1572864 | tf_op jit(solution)/shard_map/all_to_all | solution.py:524
  15.2 21.1 %collective-permute-start.1 = (f32[2,256,256]{2,1,0:T(8,128)S(1)}, f32[2,256,256]{2,1,0:T(8,128)}, u32[]{:S(2)}, u32[]{:S(2)}) collective-permute-start(f32[2,256,256]{2,1,0:T(8,128)S(1)} %copy-done.6), channel_id=1, source_target_pairs={{16,0},{17,1},{18,2},{19,3},{20,4},{21,5},{22,6},{23,7},{24,8},{25... | collective-permute-start | bytes 1572872 | tf_op jit(solution)/shard_map/ppermute | solution.py:517
  17.2 0.8 copy-start.4
  20.6 15.8 %collective-permute-start.2 = (f32[2,256,256]{2,1,0:T(8,128)}, f32[2,256,256]{2,1,0:T(8,128)S(1)}, u32[]{:S(2)}, u32[]{:S(2)}) collective-permute-start(f32[2,256,256]{2,1,0:T(8,128)} %get-tuple-element.33), channel_id=1, source_target_pairs={{0,15},{1,0},{2,1},{3,2},{4,3},{5,4},{6,5},{7,6},{8,7},{9,8},{10,9... | collective-permute-start | bytes 1572872 | tf_op jit(solution)/shard_map/ppermute | solution.py:522
  32.8 11.6 %all-to-all-start.2 = ((f32[16,16,256]{2,1,0:T(8,128)}), f32[16,16,256]{2,1,0:T(8,128)S(1)}, u32[]{:S(2)}, u32[]{:S(2)}) async-start(f32[16,16,256]{2,1,0:T(8,128)} %shard_map.77), calls=%async_computation.2 | async-start | bytes 524288 | tf_op jit(solution)/shard_map/all_to_all | solution.py:530
  36.4 0.8 copy-start.7
  44.5 0.7 copy-start.2
  45.1 18.3 %copy-start.5 = (s32[128,2]{0,1:T(2,128)S(1)}, s32[128,2]{0,1:T(2,128)}, u32[]{:S(2)}) copy-start(s32[128,2]{0,1:T(2,128)} %param.11) | copy-start | bytes 3076
  52.7 11.9 %collective-permute-start.3 = (f32[2,2,256,256]{3,2,1,0:T(8,128)}, f32[2,2,256,256]{3,2,1,0:T(8,128)S(1)}, u32[]{:S(2)}, u32[]{:S(2)}) collective-permute-start(f32[2,2,256,256]{3,2,1,0:T(8,128)} %get-tuple-element.38), channel_id=1, source_target_pairs={{0,16},{1,17},{2,18},{3,19},{4,20},{5,21},{6,22},{7,23},{8,24},{9,... | collective-permute-start | bytes 3145736 | tf_op jit(solution)/shard_map/ppermute | solution.py:545
  54.3 31.2 %collective-permute-start.6 = (f32[2,256,256]{2,1,0:T(8,128)}, f32[2,256,256]{2,1,0:T(8,128)}, u32[]{:S(2)}, u32[]{:S(2)}) collective-permute-start(f32[2,256,256]{2,1,0:T(8,128)} %get-tuple-element.39.own), channel_id=1, source_target_pairs={{15,16},{0,17},{1,18},{2,19},{3,20},{4,21},{5,22},{6,23},{7,24},{8... | collective-permute-start | bytes 1572872 | tf_op jit(solution)/shard_map/ppermute | solution.py:548
  59.8 25.7 %collective-permute-start.5 = (f32[2,256,256]{2,1,0:T(8,128)}, f32[2,256,256]{2,1,0:T(8,128)}, u32[]{:S(2)}, u32[]{:S(2)}) collective-permute-start(f32[2,256,256]{2,1,0:T(8,128)} %get-tuple-element.39.own), channel_id=1, source_target_pairs={{0,16},{1,17},{2,18},{3,19},{4,20},{5,21},{6,22},{7,23},{8,24},{9,... | collective-permute-start | bytes 1572872 | tf_op jit(solution)/shard_map/ppermute | solution.py:547
  61.8 23.8 %collective-permute-start.4 = (f32[2,256,256]{2,1,0:T(8,128)}, f32[2,256,256]{2,1,0:T(8,128)}, u32[]{:S(2)}, u32[]{:S(2)}) collective-permute-start(f32[2,256,256]{2,1,0:T(8,128)} %get-tuple-element.39.own), channel_id=1, source_target_pairs={{15,0},{0,1},{1,2},{2,3},{3,4},{4,5},{5,6},{6,7},{7,8},{8,9},{9,10... | collective-permute-start | bytes 1572872 | tf_op jit(solution)/shard_map/ppermute | solution.py:546
  86.8 23.0 %all-to-all-start.3 = ((f32[64,16,256]{2,1,0:T(8,128)}), f32[64,16,256]{2,1,0:T(8,128)S(1)}, u32[]{:S(2)}, u32[]{:S(2)}) async-start(f32[64,16,256]{2,1,0:T(8,128)} %shard_map.82), calls=%async_computation.3 | async-start | bytes 2097152 | tf_op jit(solution)/shard_map/all_to_all | solution.py:556
  109.7 5.9 %collective-permute-start.7 = (f32[2,2,256,256]{3,2,1,0:T(8,128)S(1)}, f32[2,2,256,256]{3,2,1,0:T(8,128)S(1)}, u32[]{:S(2)}, u32[]{:S(2)}) collective-permute-start(f32[2,2,256,256]{3,2,1,0:T(8,128)S(1)} %bitcast.11), channel_id=1, source_target_pairs={{0,16},{1,17},{2,18},{3,19},{4,20},{5,21},{6,22},{7,23},{8,24},{9,... | collective-permute-start | bytes 3145736 | tf_op jit(solution)/shard_map/ppermute | solution.py:564
  112.8 1.6 %copy-start = (f32[4,2,256,256]{3,2,1,0:T(8,128)S(1)}, f32[4,2,256,256]{3,2,1,0:T(8,128)}, u32[]{:S(2)}) copy-start(f32[4,2,256,256]{3,2,1,0:T(8,128)} %probe.7) | copy-start | bytes 6291460

commit v4 on v3

--- a/solution.py
+++ b/solution.py
@@ -478,7 +478,6 @@
 VMEM = pl.BlockSpec(memory_space=pltpu.VMEM)
 HBM = pl.BlockSpec(memory_space=pltpu.HBM)
 PIECE = (2, W, W)
-WORK_MB = 60
 
 
 def call(kernel, outs, ins, scratch, sems, *args, flops=0, data=0, out_specs=None, mb=62, alias=()):
@@ -517,7 +516,7 @@
     below = lax.ppermute(second, ALL, UP)
     side, own = call(
         send_side_kernel, [PIECE] * 2, [HBM] * 3, [offs_buf, (2, TILE, TILE), PIECE, PIECE, PIECE], 9,
-        offsets, object_field, below_first, data=4 << 20,
+        offsets, object_field, below_first, data=4 << 20, mb=54,
     )
     side = lax.ppermute(side, ALL, SIDE)
     spread = measured.reshape(CAP, NC, CHUNK, W).transpose(1, 0, 2, 3)
@@ -533,14 +532,14 @@
         [offs_buf, PIECE, PIECE, PIECE, modes, pltpu.VMEM((8, W, W), BF), modes, (W, W), PIECE, (W, W),
          split_buf, split_buf, modes], 16,
         offsets, own, below, side, probe, tables,
-        flops=2 * 48 * W**3, data=8 << 20, out_specs=[HBM, HBM, HBM, VMEM], mb=WORK_MB,
+        flops=2 * 48 * W**3, data=8 << 20, out_specs=[HBM, HBM, HBM, VMEM], mb=50,
     )
     grad, give, keep = call(
         backward_kernel, [PIECE, half, half], [HBM] * 7,
         [offs_buf, (W, W), (W, W), table_buf, modes, PIECE, modes, PIECE, modes,
          split_buf, split_buf, modes], 21,
         offsets, amp, far, mag, patch, probe, tables,
-        flops=2 * 48 * W**3, data=8 << 20, mb=WORK_MB,
+        flops=2 * 48 * W**3, data=8 << 20, mb=49,
     )
     taken = lax.ppermute(give, ALL, SWAP)
     got = lax.ppermute(grad, ALL, back(SIDE))

time: 118 us -> 116 us (0.983)
  Pallas kernels: 29.2 us -> 27.2 us
  other arithmetic: 0.14 us -> 1.36 us
    pallas_call x9, Pallas kernels: 29.2 us -> 27.2 us  [call(): pl.pallas_call(kernel, out_shape=shapes, in_specs=ins, out_specs=out_spec...]
    ppermute x1, starting transfers between devices: 3.08 us -> 4.47 us  [shards(): theirs = lax.ppermute(mine, ALL, SWAP)]
    all_to_all x1, waiting for transfers between devices: 11.5 us -> 10.1 us  [shards(): mine = lax.all_to_all(copies, CHIPS, 0, 0, tiled=True)]
    all_to_all x1, starting transfers between devices: 6.54 us -> 5.17 us  [shards(): mine = lax.all_to_all(copies, CHIPS, 0, 0, tiled=True)]
    add x1, other arithmetic: 0.14 us -> 1.36 us  [shards(): mine = (keep + taken).reshape(64, 16, W)]
    unnamed x16 -> x20, local copies, waits for them, and re-layouts: 3.87 us -> 4.01 us
  transfers between devices with their start and end apart: 11 -> 11, of which waited for: 3 -> 3; matrix products, arithmetic and copies ran while one was open for 1% -> 2% of each run, Pallas kernels for 15% -> 14%
where the time goes in v4:
time: 116 us; the launch traced here: 115 us
  starting transfers between devices  38.7 us (33%)
  Pallas kernels  27.2 us (23%)
  blocking collectives  20.8 us (18%)
  waiting for transfers between devices  20.2 us (17%)
  local copies, waits for them, and re-layouts  5.45 us (5%)
  between operations  1.56 us (1%)
  other arithmetic  1.36 us (1%)
    pallas_call x9, Pallas kernels, call(): pl.pallas_call(kernel, out_shape=shapes, in_specs=ins, out_specs=out_spec...  27.2 us
    all_to_all x1, blocking collectives, exchange(): return lax.all_to_all(x, CHIPS, 0, 0, tiled=True)  20.8 us
    all_to_all x1, waiting for transfers between devices, shards(): mine = lax.all_to_all(copies, CHIPS, 0, 0, tiled=True)  10.1 us
    all_to_all x1, waiting for transfers between devices, shards(): spread = lax.all_to_all(spread, COL, 0, 0, tiled=True)  9.17 us
    all_to_all x1, starting transfers between devices, shards(): spread = lax.all_to_all(spread, COL, 0, 0, tiled=True)  7.98 us
    all_to_all x1, starting transfers between devices, shards(): mine = lax.all_to_all(copies, CHIPS, 0, 0, tiled=True)  5.17 us
    ppermute x1, starting transfers between devices, shards(): above_second = lax.ppermute(grad, ALL, back(SLANT))  5.08 us
    ppermute x1, starting transfers between devices, shards(): theirs = lax.ppermute(mine, ALL, SWAP)  4.47 us
  transfers between devices with their start and end apart: 11, of which 3 were waited for; matrix products, arithmetic and copies ran while one was open for 2% of the time, Pallas kernels for 14%

profile of v4, /device:TPU:1, one launch (start us, length us, event | category | flops | bytes accessed | tf_op | source)
XLA Modules:
  0.0 115.3 jit_solution(15748487598429997471)
XLA Ops:
  0.6 2.2 %shard_map.78 = (f32[2,256,256]{2,1,0:T(8,128)}, f32[2,256,256]{2,1,0:T(8,128)}) custom-call(s32[2,128]{1,0:T(2,128)} %bitcast.15, f32[2,512,512]{2,1,0:T(8,128)} %tile.5), custom_call_target="tpu_custom_call" | custom-call | bytes 3145728 | tf_op jit(solution)/shard_map/pallas_call | solution.py:486
  2.8 3.3 %collective-permute-start = (f32[2,256,256]{2,1,0:T(8,128)}, f32[2,256,256]{2,1,0:T(8,128)S(1)}, u32[]{:S(2)}, u32[]{:S(2)}) collective-permute-start(f32[2,256,256]{2,1,0:T(8,128)} %get-tuple-element.30), channel_id=1, source_target_pairs={{16,0},{17,1},{18,2},{19,3},{20,4},{21,5},{22,6},{23,7},{24,8},{25... | collective-permute-start | bytes 1572872 | tf_op jit(solution)/shard_map/ppermute | solution.py:515
  7.1 8.0 %all-to-all-start.1 = ((f32[16,3,16,256]{3,2,1,0:T(8,128)}), f32[16,3,16,256]{3,2,1,0:T(8,128)S(1)}, u32[]{:S(2)}, u32[]{:S(2)}) async-start(f32[16,3,16,256]{3,2,1,0:T(8,128)} %bitcast.10), calls=%async_computation.1 | async-start | bytes 1572864 | tf_op jit(solution)/shard_map/all_to_all | solution.py:523
  15.1 2.1 %collective-permute-start.1 = (f32[2,256,256]{2,1,0:T(8,128)}, f32[2,256,256]{2,1,0:T(8,128)S(1)}, u32[]{:S(2)}, u32[]{:S(2)}) collective-permute-start(f32[2,256,256]{2,1,0:T(8,128)} %get-tuple-element.32), channel_id=1, source_target_pairs={{16,0},{17,1},{18,2},{19,3},{20,4},{21,5},{22,6},{23,7},{24,8},{25... | collective-permute-start | bytes 1572872 | tf_op jit(solution)/shard_map/ppermute | solution.py:516
  18.0 2.6 %shard_map.79 = (f32[2,256,256]{2,1,0:T(8,128)}, f32[2,256,256]{2,1,0:T(8,128)}) custom-call(s32[2,128]{1,0:T(2,128)} %bitcast.16, f32[2,512,512]{2,1,0:T(8,128)} %tile.5, f32[2,256,256]{2,1,0:T(8,128)} %copy-done.9), custom_call_target="tpu_custom_call" | custom-call | bytes 4194304 | tf_op jit(solution)/shard_map/pallas_call | solution.py:486
  20.6 1.4 %collective-permute-start.2 = (f32[2,256,256]{2,1,0:T(8,128)}, f32[2,256,256]{2,1,0:T(8,128)}, u32[]{:S(2)}, u32[]{:S(2)}) collective-permute-start(f32[2,256,256]{2,1,0:T(8,128)} %get-tuple-element.33), channel_id=1, source_target_pairs={{0,15},{1,0},{2,1},{3,2},{4,3},{5,4},{6,5},{7,6},{8,7},{9,8},{10,9... | collective-permute-start | bytes 1572872 | tf_op jit(solution)/shard_map/ppermute | solution.py:521
  22.1 9.2 %all-to-all-done.1 = f32[16,3,16,256]{3,2,1,0:T(8,128)S(1)} async-done(((f32[16,3,16,256]{3,2,1,0:T(8,128)}), f32[16,3,16,256]{3,2,1,0:T(8,128)S(1)}, u32[]{:S(2)}, u32[]{:S(2)}) %all-to-all-start.1) | async-done | bytes 786464 | tf_op jit(solution)/shard_map/all_to_all | solution.py:523
  31.2 1.4 %shard_map.77 = f32[16,16,256]{2,1,0:T(8,128)} custom-call(s32[1,128]{1,0:T(1,128)S(1)} %bitcast.21, f32[48,16,256]{2,1,0:T(8,128)S(1)} %bitcast.13), custom_call_target="tpu_custom_call" | custom-call | bytes 1048576 | tf_op jit(solution)/shard_map/pallas_call | solution.py:486
  32.7 3.5 %all-to-all-start.2 = ((f32[16,16,256]{2,1,0:T(8,128)}), f32[16,16,256]{2,1,0:T(8,128)S(1)}, u32[]{:S(2)}, u32[]{:S(2)}) async-start(f32[16,16,256]{2,1,0:T(8,128)} %shard_map.77), calls=%async_computation.2 | async-start | bytes 524288 | tf_op jit(solution)/shard_map/all_to_all | solution.py:529
  37.3 5.5 %shard_map.80 = (f32[4,2,256,256]{3,2,1,0:T(8,128)}, f32[256,256]{1,0:T(8,128)S(1)}, f32[2,256,256]{2,1,0:T(8,128)S(1)}, f32[8,128]{1,0:T(8,128)S(1)}) custom-call(s32[2,128]{1,0:T(2,128)S(1)} %bitcast.18, f32[2,256,256]{2,1,0:T(8,128)S(1)} %copy-done.6, f32[2,256,256]{2,1,0:T(8,128)S(1)} %collective-permute-done.1.below, ...), custom_call_target="tpu_custom_call" | custom-call | flops 1610612736 | bytes 8388608 | tf_op jit(solution)/shard_map/pallas_call | solution.py:486
  44.3 6.8 %shard_map.81 = (f32[2,256,256]{2,1,0:T(8,128)S(1)}, f32[2,2,256,256]{3,2,1,0:T(8,128)S(1)}, f32[2,2,256,256]{3,2,1,0:T(8,128)}) custom-call(s32[2,128]{1,0:T(2,128)S(1)} %bitcast.19, f32[256,256]{1,0:T(8,128)S(1)} %bitcast.14, f32[4,2,256,256]{3,2,1,0:T(8,128)} %get-tuple-element.34.far, f32[256,256]{1,0:T(8,128)S(1)} %get-tuple-element.35.mag, ...), custom_call_target="tpu_custom_call" | custom-call | flops 1610612736 | bytes 8388608 | tf_op jit(solution)/shard_map/pallas_call | solution.py:486
  51.1 1.6 %collective-permute-start.3 = (f32[2,2,256,256]{3,2,1,0:T(8,128)S(1)}, f32[2,2,256,256]{3,2,1,0:T(8,128)S(1)}, u32[]{:S(2)}, u32[]{:S(2)}) collective-permute-start(f32[2,2,256,256]{3,2,1,0:T(8,128)S(1)} %get-tuple-element.38), channel_id=1, source_target_pairs={{0,16},{1,17},{2,18},{3,19},{4,20},{5,21},{6,22},{7,23},{8,24},{9,... | collective-permute-start | bytes 3145736 | tf_op jit(solution)/shard_map/ppermute | solution.py:544
  52.7 5.1 %collective-permute-start.6 = (f32[2,256,256]{2,1,0:T(8,128)S(1)}, f32[2,256,256]{2,1,0:T(8,128)S(1)}, u32[]{:S(2)}, u32[]{:S(2)}) collective-permute-start(f32[2,256,256]{2,1,0:T(8,128)S(1)} %get-tuple-element.39.own), channel_id=1, source_target_pairs={{15,16},{0,17},{1,18},{2,19},{3,20},{4,21},{5,22},{6,23},{7,24},{8... | collective-permute-start | bytes 1572872 | tf_op jit(solution)/shard_map/ppermute | solution.py:547
  57.8 1.9 %collective-permute-start.5 = (f32[2,256,256]{2,1,0:T(8,128)S(1)}, f32[2,256,256]{2,1,0:T(8,128)}, u32[]{:S(2)}, u32[]{:S(2)}) collective-permute-start(f32[2,256,256]{2,1,0:T(8,128)S(1)} %get-tuple-element.39.own), channel_id=1, source_target_pairs={{0,16},{1,17},{2,18},{3,19},{4,20},{5,21},{6,22},{7,23},{8,24},{9,... | collective-permute-start | bytes 1572872 | tf_op jit(solution)/shard_map/ppermute | solution.py:546
  59.7 2.1 %collective-permute-start.4 = (f32[2,256,256]{2,1,0:T(8,128)S(1)}, f32[2,256,256]{2,1,0:T(8,128)}, u32[]{:S(2)}, u32[]{:S(2)}) collective-permute-start(f32[2,256,256]{2,1,0:T(8,128)S(1)} %get-tuple-element.39.own), channel_id=1, source_target_pairs={{15,0},{0,1},{1,2},{2,3},{3,4},{4,5},{5,6},{6,7},{7,8},{8,9},{9,10... | collective-permute-start | bytes 1572872 | tf_op jit(solution)/shard_map/ppermute | solution.py:545
  63.0 22.2 %conditional.1 = (f32[64,16,256]{2,1,0:T(8,128)S(1)}) conditional(s32[]{:T(128)} %bitcast.2, () %tuple.17, (f32[2,2,256,256]{3,2,1,0:T(8,128)}, f32[2,2,256,256]{3,2,1,0:T(8,128)S(1)}) %tuple.18), branch_computations={%region_0.0_spmd, %region_1.0_spmd} | conditional | flops 262144 | bytes 5242888 | solution.py:550
  63.0 1.4 %add.3 = f32[2,2,256,256]{3,2,1,0:T(8,128)S(1)} add(f32[2,2,256,256]{3,2,1,0:T(8,128)} %get-tuple-element.9, f32[2,2,256,256]{3,2,1,0:T(8,128)S(1)} %get-tuple-element.10) | non-fusion elementwise | flops 262144 | bytes 3145728 | tf_op jit(solution)/shard_map/add | solution.py:548
  64.4 20.8 %all_to_all.19 = f32[64,16,256]{2,1,0:T(8,128)S(1)} all-to-all(f32[64,16,256]{2,1,0:T(8,128)S(1)} %bitcast.22), channel_id=1, replica_groups=mesh['x'=4,'core'=2,'z'=4,'y'=4] {'x','z','y'}, dimensions={0} | all-to-all | bytes 2097152 | tf_op jit(solution)/shard_map/cond/branch_1_fun/all_to_all | solution.py:499
  85.2 1.3 %shard_map.82 = f32[64,16,256]{2,1,0:T(8,128)} custom-call(f32[64,16,256]{2,1,0:T(8,128)S(1)} %get-tuple-element.47.parts), custom_call_target="tpu_custom_call" | custom-call | bytes 2097152 | tf_op jit(solution)/shard_map/pallas_call | solution.py:486
  86.5 5.2 %all-to-all-start.3 = ((f32[64,16,256]{2,1,0:T(8,128)}), f32[64,16,256]{2,1,0:T(8,128)S(1)}, u32[]{:S(2)}, u32[]{:S(2)}) async-start(f32[64,16,256]{2,1,0:T(8,128)} %shard_map.82), calls=%async_computation.3 | async-start | bytes 2097152 | tf_op jit(solution)/shard_map/all_to_all | solution.py:555
  91.7 4.9 %shard_map.83 = f32[2,512,512]{2,1,0:T(8,128)} custom-call(s32[2,128]{1,0:T(2,128)} %bitcast.17, f32[8,128]{1,0:T(8,128)} %copy-done.4, f32[2,512,512]{2,1,0:T(8,128)} %tile.5, f32[2,256,256]{2,1,0:T(8,128)} %copy-done.2, f32[2,256,256]{2,1,0:T(8,128)} %collective-permute-done.4.got, f32[2,256,256]{2,1,0:T(8,128)} %collective-permute-done.5.above_first, ...), custom_call_target="tpu_custom_call" | custom-call | bytes 6291456 | tf_op jit(solution)/shard_map/pallas_call | solution.py:486
  96.7 10.1 %all-to-all-done.3 = f32[64,16,256]{2,1,0:T(8,128)S(1)} async-done(((f32[64,16,256]{2,1,0:T(8,128)}), f32[64,16,256]{2,1,0:T(8,128)S(1)}, u32[]{:S(2)}, u32[]{:S(2)}) %all-to-all-start.3) | async-done | bytes 1048608 | tf_op jit(solution)/shard_map/all_to_all | solution.py:555
  106.7 4.5 %collective-permute-start.7 = (f32[2,2,256,256]{3,2,1,0:T(8,128)S(1)}, f32[2,2,256,256]{3,2,1,0:T(8,128)S(1)}, u32[]{:S(2)}, u32[]{:S(2)}) collective-permute-start(f32[2,2,256,256]{3,2,1,0:T(8,128)S(1)} %bitcast.11), channel_id=1, source_target_pairs={{0,16},{1,17},{2,18},{3,19},{4,20},{5,21},{6,22},{7,23},{8,24},{9,... | collective-permute-start | bytes 3145736 | tf_op jit(solution)/shard_map/ppermute | solution.py:563
  111.2 1.6 %copy-done = f32[4,2,256,256]{3,2,1,0:T(8,128)S(1)} copy-done((f32[4,2,256,256]{3,2,1,0:T(8,128)S(1)}, f32[4,2,256,256]{3,2,1,0:T(8,128)}, u32[]{:S(2)}) %copy-start) | copy-done | bytes 2097176
  (32 shorter events, 7.3 us)
Async XLA Ops:
  0.6 5.5 %copy-start.7 = (f32[3,256,256]{2,1,0:T(8,128)S(1)}, f32[3,256,256]{2,1,0:T(8,128)}, u32[]{:S(2)}) copy-start(f32[3,256,256]{2,1,0:T(8,128)} %param.10) | copy-start | bytes 2359300
  2.8 14.4 %collective-permute-start = (f32[2,256,256]{2,1,0:T(8,128)}, f32[2,256,256]{2,1,0:T(8,128)S(1)}, u32[]{:S(2)}, u32[]{:S(2)}) collective-permute-start(f32[2,256,256]{2,1,0:T(8,128)} %get-tuple-element.30), channel_id=1, source_target_pairs={{16,0},{17,1},{18,2},{19,3},{20,4},{21,5},{22,6},{23,7},{24,8},{25... | collective-permute-start | bytes 1572872 | tf_op jit(solution)/shard_map/ppermute | solution.py:515
  7.1 24.1 %copy-start.5 = (s32[128]{0:T(128)S(1)}, s32[128]{0:T(128)}, u32[]{:S(2)}) copy-start(s32[128]{0:T(128)} %param.12) | copy-start | bytes 1540
  7.1 24.1 %all-to-all-start.1 = ((f32[16,3,16,256]{3,2,1,0:T(8,128)}), f32[16,3,16,256]{3,2,1,0:T(8,128)S(1)}, u32[]{:S(2)}, u32[]{:S(2)}) async-start(f32[16,3,16,256]{3,2,1,0:T(8,128)} %bitcast.10), calls=%async_computation.1 | async-start | bytes 1572864 | tf_op jit(solution)/shard_map/all_to_all | solution.py:523
  15.1 21.2 %copy-start.1 = (bf16[10,256,256]{2,1,0:T(8,128)(2,1)S(1)}, bf16[10,256,256]{2,1,0:T(8,128)(2,1)}, u32[]{:S(2)}) copy-start(bf16[10,256,256]{2,1,0:T(8,128)(2,1)} %constant.7.clone.tables) | copy-start | bytes 3932164
  15.1 21.2 %copy-start.3 = (s32[128,2]{0,1:T(2,128)S(1)}, s32[128,2]{0,1:T(2,128)}, u32[]{:S(2)}) copy-start(s32[128,2]{0,1:T(2,128)} %param.11) | copy-start | bytes 3076
  15.1 21.1 %collective-permute-start.1 = (f32[2,256,256]{2,1,0:T(8,128)}, f32[2,256,256]{2,1,0:T(8,128)S(1)}, u32[]{:S(2)}, u32[]{:S(2)}) collective-permute-start(f32[2,256,256]{2,1,0:T(8,128)} %get-tuple-element.32), channel_id=1, source_target_pairs={{16,0},{17,1},{18,2},{19,3},{20,4},{21,5},{22,6},{23,7},{24,8},{25... | collective-permute-start | bytes 1572872 | tf_op jit(solution)/shard_map/ppermute | solution.py:516
  17.2 0.8 copy-start.9
  20.6 15.6 %collective-permute-start.2 = (f32[2,256,256]{2,1,0:T(8,128)}, f32[2,256,256]{2,1,0:T(8,128)}, u32[]{:S(2)}, u32[]{:S(2)}) collective-permute-start(f32[2,256,256]{2,1,0:T(8,128)} %get-tuple-element.33), channel_id=1, source_target_pairs={{0,15},{1,0},{2,1},{3,2},{4,3},{5,4},{6,5},{7,6},{8,7},{9,8},{10,9... | collective-permute-start | bytes 1572872 | tf_op jit(solution)/shard_map/ppermute | solution.py:521
  32.7 11.6 %all-to-all-start.2 = ((f32[16,16,256]{2,1,0:T(8,128)}), f32[16,16,256]{2,1,0:T(8,128)S(1)}, u32[]{:S(2)}, u32[]{:S(2)}) async-start(f32[16,16,256]{2,1,0:T(8,128)} %shard_map.77), calls=%async_computation.2 | async-start | bytes 524288 | tf_op jit(solution)/shard_map/all_to_all | solution.py:529
  36.3 1.0 copy-start.6
  42.8 0.6 copy-start.4
  51.1 11.9 %copy-start.2 = (f32[2,256,256]{2,1,0:T(8,128)}, f32[2,256,256]{2,1,0:T(8,128)S(1)}, u32[]{:S(2)}) copy-start(f32[2,256,256]{2,1,0:T(8,128)S(1)} %get-tuple-element.39.own) | copy-start | bytes 1572868
  51.1 11.9 %collective-permute-start.3 = (f32[2,2,256,256]{3,2,1,0:T(8,128)S(1)}, f32[2,2,256,256]{3,2,1,0:T(8,128)S(1)}, u32[]{:S(2)}, u32[]{:S(2)}) collective-permute-start(f32[2,2,256,256]{3,2,1,0:T(8,128)S(1)} %get-tuple-element.38), channel_id=1, source_target_pairs={{0,16},{1,17},{2,18},{3,19},{4,20},{5,21},{6,22},{7,23},{8,24},{9,... | collective-permute-start | bytes 3145736 | tf_op jit(solution)/shard_map/ppermute | solution.py:544
  52.7 32.5 %collective-permute-start.6 = (f32[2,256,256]{2,1,0:T(8,128)S(1)}, f32[2,256,256]{2,1,0:T(8,128)S(1)}, u32[]{:S(2)}, u32[]{:S(2)}) collective-permute-start(f32[2,256,256]{2,1,0:T(8,128)S(1)} %get-tuple-element.39.own), channel_id=1, source_target_pairs={{15,16},{0,17},{1,18},{2,19},{3,20},{4,21},{5,22},{6,23},{7,24},{8... | collective-permute-start | bytes 1572872 | tf_op jit(solution)/shard_map/ppermute | solution.py:547
  57.8 27.4 %collective-permute-start.5 = (f32[2,256,256]{2,1,0:T(8,128)S(1)}, f32[2,256,256]{2,1,0:T(8,128)}, u32[]{:S(2)}, u32[]{:S(2)}) collective-permute-start(f32[2,256,256]{2,1,0:T(8,128)S(1)} %get-tuple-element.39.own), channel_id=1, source_target_pairs={{0,16},{1,17},{2,18},{3,19},{4,20},{5,21},{6,22},{7,23},{8,24},{9,... | collective-permute-start | bytes 1572872 | tf_op jit(solution)/shard_map/ppermute | solution.py:546
  59.7 25.5 %collective-permute-start.4 = (f32[2,256,256]{2,1,0:T(8,128)S(1)}, f32[2,256,256]{2,1,0:T(8,128)}, u32[]{:S(2)}, u32[]{:S(2)}) collective-permute-start(f32[2,256,256]{2,1,0:T(8,128)S(1)} %get-tuple-element.39.own), channel_id=1, source_target_pairs={{15,0},{0,1},{1,2},{2,3},{3,4},{4,5},{5,6},{6,7},{7,8},{8,9},{9,10... | collective-permute-start | bytes 1572872 | tf_op jit(solution)/shard_map/ppermute | solution.py:545
  85.2 1.3 %copy-start.8 = (f32[2,256,256]{2,1,0:T(8,128)}, f32[2,256,256]{2,1,0:T(8,128)S(1)}, u32[]{:S(2)}) copy-start(f32[2,256,256]{2,1,0:T(8,128)S(1)} %collective-permute-done.6.above_second) | copy-start | bytes 1572868
  86.5 20.2 %all-to-all-start.3 = ((f32[64,16,256]{2,1,0:T(8,128)}), f32[64,16,256]{2,1,0:T(8,128)S(1)}, u32[]{:S(2)}, u32[]{:S(2)}) async-start(f32[64,16,256]{2,1,0:T(8,128)} %shard_map.82), calls=%async_computation.3 | async-start | bytes 2097152 | tf_op jit(solution)/shard_map/all_to_all | solution.py:555
  106.7 7.3 %collective-permute-start.7 = (f32[2,2,256,256]{3,2,1,0:T(8,128)S(1)}, f32[2,2,256,256]{3,2,1,0:T(8,128)S(1)}, u32[]{:S(2)}, u32[]{:S(2)}) collective-permute-start(f32[2,2,256,256]{3,2,1,0:T(8,128)S(1)} %bitcast.11), channel_id=1, source_target_pairs={{0,16},{1,17},{2,18},{3,19},{4,20},{5,21},{6,22},{7,23},{8,24},{9,... | collective-permute-start | bytes 3145736 | tf_op jit(solution)/shard_map/ppermute | solution.py:563
  111.2 1.6 %copy-start = (f32[4,2,256,256]{3,2,1,0:T(8,128)S(1)}, f32[4,2,256,256]{3,2,1,0:T(8,128)}, u32[]{:S(2)}) copy-start(f32[4,2,256,256]{3,2,1,0:T(8,128)} %probe.7) | copy-start | bytes 6291460

commit v5 on v4

--- a/solution.py
+++ b/solution.py
@@ -55,9 +55,9 @@
             step = -1 if r % 2 == 0 else 1
             side.append((me, r * NC + (c + step) % NC))
             swap.append((me, (r ^ 1) * NC + c))
-            if r > 0:
-                up.append((me, me - NC))
-                slant.append((me, (r - 1) * NC + (c - step) % NC))
+            above = (r - 1) % NR
+            up.append((me, above * NC + c))
+            slant.append((me, above * NC + (c - step) % NC))
     return up, side, slant, swap
 
 

time: 116 us -> 113 us (0.974)
  starting transfers between devices: 38.7 us -> 36.7 us
  waiting for transfers between devices: 20.2 us -> 18.8 us
    all_to_all x1, waiting for transfers between devices: 9.17 us -> 4.35 us  [shards(): spread = lax.all_to_all(spread, COL, 0, 0, tiled=True)]
    ppermute x1, waiting for transfers between devices: 0.01 us -> 2.97 us  [shards(): side = lax.ppermute(side, ALL, SIDE)]
    all_to_all x1, starting transfers between devices: 5.17 us -> 7.48 us  [shards(): mine = lax.all_to_all(copies, CHIPS, 0, 0, tiled=True)]
    ppermute x1, starting transfers between devices: 1.92 us -> 0.01 us  [shards(): above_first = lax.ppermute(grad, ALL, back(UP))]
    ppermute x1, starting transfers between devices: 3.33 us -> 1.43 us  [shards(): below_first = lax.ppermute(first, ALL, UP)]
    ppermute x1, starting transfers between devices: 1.59 us -> 3.25 us  [shards(): taken = lax.ppermute(give, ALL, SWAP)]
    ppermute x1, starting transfers between devices: 4.47 us -> 3.1 us  [shards(): theirs = lax.ppermute(mine, ALL, SWAP)]
    all_to_all x1, waiting for transfers between devices: 10.1 us -> 11.4 us  [shards(): mine = lax.all_to_all(copies, CHIPS, 0, 0, tiled=True)]
  transfers between devices with their start and end apart: 11 -> 11, of which waited for: 3 -> 3; matrix products, arithmetic and copies ran while one was open for 2% -> 3% of each run, Pallas kernels for 14% -> 14%
where the time goes in v5:
time: 113 us; the launch traced here: 112 us
  starting transfers between devices  36.7 us (32%)
  Pallas kernels  27.2 us (24%)
  blocking collectives  20.8 us (18%)
  waiting for transfers between devices  18.8 us (17%)
  local copies, waits for them, and re-layouts  5.46 us (5%)
  between operations  1.48 us (1%)
  other arithmetic  1.36 us (1%)
    pallas_call x9, Pallas kernels, call(): pl.pallas_call(kernel, out_shape=shapes, in_specs=ins, out_specs=out_spec...  27.2 us
    all_to_all x1, blocking collectives, exchange(): return lax.all_to_all(x, CHIPS, 0, 0, tiled=True)  20.8 us
    all_to_all x1, waiting for transfers between devices, shards(): mine = lax.all_to_all(copies, CHIPS, 0, 0, tiled=True)  11.4 us
    all_to_all x1, starting transfers between devices, shards(): spread = lax.all_to_all(spread, COL, 0, 0, tiled=True)  7.98 us
    all_to_all x1, starting transfers between devices, shards(): mine = lax.all_to_all(copies, CHIPS, 0, 0, tiled=True)  7.48 us
    all_to_all x1, waiting for transfers between devices, shards(): spread = lax.all_to_all(spread, COL, 0, 0, tiled=True)  4.35 us
    unnamed x20, local copies, waits for them, and re-layouts  4.02 us
    ppermute x1, starting transfers between devices, shards(): above_second = lax.ppermute(grad, ALL, back(SLANT))  3.72 us
  transfers between devices with their start and end apart: 11, of which 3 were waited for; matrix products, arithmetic and copies ran while one was open for 3% of the time, Pallas kernels for 14%

profile of v5, /device:TPU:1, one launch (start us, length us, event | category | flops | bytes accessed | tf_op | source)
XLA Modules:
  0.0 111.7 jit_solution(2332382771882616622)
XLA Ops:
  0.6 2.2 %shard_map.78 = (f32[2,256,256]{2,1,0:T(8,128)}, f32[2,256,256]{2,1,0:T(8,128)}) custom-call(s32[2,128]{1,0:T(2,128)} %bitcast.15, f32[2,512,512]{2,1,0:T(8,128)} %tile.5), custom_call_target="tpu_custom_call" | custom-call | bytes 3145728 | tf_op jit(solution)/shard_map/pallas_call | solution.py:486
  2.8 1.4 %collective-permute-start = (f32[2,256,256]{2,1,0:T(8,128)}, f32[2,256,256]{2,1,0:T(8,128)S(1)}, u32[]{:S(2)}, u32[]{:S(2)}) collective-permute-start(f32[2,256,256]{2,1,0:T(8,128)} %get-tuple-element.30), channel_id=1, source_target_pairs={{0,112},{1,113},{2,114},{3,115},{4,116},{5,117},{6,118},{7,119},{8... | collective-permute-start | bytes 1572872 | tf_op jit(solution)/shard_map/ppermute | solution.py:515
  5.2 8.0 %all-to-all-start.1 = ((f32[16,3,16,256]{3,2,1,0:T(8,128)}), f32[16,3,16,256]{3,2,1,0:T(8,128)S(1)}, u32[]{:S(2)}, u32[]{:S(2)}) async-start(f32[16,3,16,256]{3,2,1,0:T(8,128)} %bitcast.10), calls=%async_computation.1 | async-start | bytes 1572864 | tf_op jit(solution)/shard_map/all_to_all | solution.py:523
  13.2 2.5 %collective-permute-start.1 = (f32[2,256,256]{2,1,0:T(8,128)}, f32[2,256,256]{2,1,0:T(8,128)S(1)}, u32[]{:S(2)}, u32[]{:S(2)}) collective-permute-start(f32[2,256,256]{2,1,0:T(8,128)} %get-tuple-element.32), channel_id=1, source_target_pairs={{0,112},{1,113},{2,114},{3,115},{4,116},{5,117},{6,118},{7,119},{8... | collective-permute-start | bytes 1572872 | tf_op jit(solution)/shard_map/ppermute | solution.py:516
  16.5 2.6 %shard_map.79 = (f32[2,256,256]{2,1,0:T(8,128)}, f32[2,256,256]{2,1,0:T(8,128)}) custom-call(s32[2,128]{1,0:T(2,128)} %bitcast.16, f32[2,512,512]{2,1,0:T(8,128)} %tile.5, f32[2,256,256]{2,1,0:T(8,128)} %copy-done.9), custom_call_target="tpu_custom_call" | custom-call | bytes 4194304 | tf_op jit(solution)/shard_map/pallas_call | solution.py:486
  19.1 1.7 %collective-permute-start.2 = (f32[2,256,256]{2,1,0:T(8,128)}, f32[2,256,256]{2,1,0:T(8,128)}, u32[]{:S(2)}, u32[]{:S(2)}) collective-permute-start(f32[2,256,256]{2,1,0:T(8,128)} %get-tuple-element.33), channel_id=1, source_target_pairs={{0,15},{1,0},{2,1},{3,2},{4,3},{5,4},{6,5},{7,6},{8,7},{9,8},{10,9... | collective-permute-start | bytes 1572872 | tf_op jit(solution)/shard_map/ppermute | solution.py:521
  20.8 4.3 %all-to-all-done.1 = f32[16,3,16,256]{3,2,1,0:T(8,128)S(1)} async-done(((f32[16,3,16,256]{3,2,1,0:T(8,128)}), f32[16,3,16,256]{3,2,1,0:T(8,128)S(1)}, u32[]{:S(2)}, u32[]{:S(2)}) %all-to-all-start.1) | async-done | bytes 786464 | tf_op jit(solution)/shard_map/all_to_all | solution.py:523
  25.2 1.4 %shard_map.77 = f32[16,16,256]{2,1,0:T(8,128)} custom-call(s32[1,128]{1,0:T(1,128)S(1)} %bitcast.21, f32[48,16,256]{2,1,0:T(8,128)S(1)} %bitcast.13), custom_call_target="tpu_custom_call" | custom-call | bytes 1048576 | tf_op jit(solution)/shard_map/pallas_call | solution.py:486
  26.6 3.5 %all-to-all-start.2 = ((f32[16,16,256]{2,1,0:T(8,128)}), f32[16,16,256]{2,1,0:T(8,128)S(1)}, u32[]{:S(2)}, u32[]{:S(2)}) async-start(f32[16,16,256]{2,1,0:T(8,128)} %shard_map.77), calls=%async_computation.2 | async-start | bytes 524288 | tf_op jit(solution)/shard_map/all_to_all | solution.py:529
  30.2 3.0 %collective-permute-done.2.side = f32[2,256,256]{2,1,0:T(8,128)} collective-permute-done((f32[2,256,256]{2,1,0:T(8,128)}, f32[2,256,256]{2,1,0:T(8,128)}, u32[]{:S(2)}, u32[]{:S(2)}) %collective-permute-start.2) | collective-permute-done | bytes 524320 | tf_op jit(solution)/shard_map/ppermute | solution.py:521
  34.2 5.4 %shard_map.80 = (f32[4,2,256,256]{3,2,1,0:T(8,128)}, f32[256,256]{1,0:T(8,128)S(1)}, f32[2,256,256]{2,1,0:T(8,128)S(1)}, f32[8,128]{1,0:T(8,128)S(1)}) custom-call(s32[2,128]{1,0:T(2,128)S(1)} %bitcast.18, f32[2,256,256]{2,1,0:T(8,128)S(1)} %copy-done.6, f32[2,256,256]{2,1,0:T(8,128)S(1)} %collective-permute-done.1.below, ...), custom_call_target="tpu_custom_call" | custom-call | flops 1610612736 | bytes 8388608 | tf_op jit(solution)/shard_map/pallas_call | solution.py:486
  40.3 6.8 %shard_map.81 = (f32[2,256,256]{2,1,0:T(8,128)S(1)}, f32[2,2,256,256]{3,2,1,0:T(8,128)S(1)}, f32[2,2,256,256]{3,2,1,0:T(8,128)}) custom-call(s32[2,128]{1,0:T(2,128)S(1)} %bitcast.19, f32[256,256]{1,0:T(8,128)S(1)} %bitcast.14, f32[4,2,256,256]{3,2,1,0:T(8,128)} %get-tuple-element.34.far, f32[256,256]{1,0:T(8,128)S(1)} %get-tuple-element.35.mag, ...), custom_call_target="tpu_custom_call" | custom-call | flops 1610612736 | bytes 8388608 | tf_op jit(solution)/shard_map/pallas_call | solution.py:486
  47.1 3.3 %collective-permute-start.3 = (f32[2,2,256,256]{3,2,1,0:T(8,128)S(1)}, f32[2,2,256,256]{3,2,1,0:T(8,128)S(1)}, u32[]{:S(2)}, u32[]{:S(2)}) collective-permute-start(f32[2,2,256,256]{3,2,1,0:T(8,128)S(1)} %get-tuple-element.38), channel_id=1, source_target_pairs={{0,16},{1,17},{2,18},{3,19},{4,20},{5,21},{6,22},{7,23},{8,24},{9,... | collective-permute-start | bytes 3145736 | tf_op jit(solution)/shard_map/ppermute | solution.py:544
  50.3 3.7 %collective-permute-start.6 = (f32[2,256,256]{2,1,0:T(8,128)S(1)}, f32[2,256,256]{2,1,0:T(8,128)S(1)}, u32[]{:S(2)}, u32[]{:S(2)}) collective-permute-start(f32[2,256,256]{2,1,0:T(8,128)S(1)} %get-tuple-element.39.own), channel_id=1, source_target_pairs={{113,0},{114,1},{115,2},{116,3},{117,4},{118,5},{119,6},{120,7},{1... | collective-permute-start | bytes 1572872 | tf_op jit(solution)/shard_map/ppermute | solution.py:547
  54.1 2.0 %collective-permute-start.4 = (f32[2,256,256]{2,1,0:T(8,128)S(1)}, f32[2,256,256]{2,1,0:T(8,128)}, u32[]{:S(2)}, u32[]{:S(2)}) collective-permute-start(f32[2,256,256]{2,1,0:T(8,128)S(1)} %get-tuple-element.39.own), channel_id=1, source_target_pairs={{15,0},{0,1},{1,2},{2,3},{3,4},{4,5},{5,6},{6,7},{7,8},{8,9},{9,10... | collective-permute-start | bytes 1572872 | tf_op jit(solution)/shard_map/ppermute | solution.py:545
  57.2 22.2 %conditional.1 = (f32[64,16,256]{2,1,0:T(8,128)S(1)}) conditional(s32[]{:T(128)} %bitcast.2, () %tuple.17, (f32[2,2,256,256]{3,2,1,0:T(8,128)}, f32[2,2,256,256]{3,2,1,0:T(8,128)S(1)}) %tuple.18), branch_computations={%region_0.0_spmd, %region_1.0_spmd} | conditional | flops 262144 | bytes 5242888 | solution.py:550
  57.2 1.4 %add.3 = f32[2,2,256,256]{3,2,1,0:T(8,128)S(1)} add(f32[2,2,256,256]{3,2,1,0:T(8,128)} %get-tuple-element.9, f32[2,2,256,256]{3,2,1,0:T(8,128)S(1)} %get-tuple-element.10) | non-fusion elementwise | flops 262144 | bytes 3145728 | tf_op jit(solution)/shard_map/add | solution.py:548
  58.6 20.8 %all_to_all.19 = f32[64,16,256]{2,1,0:T(8,128)S(1)} all-to-all(f32[64,16,256]{2,1,0:T(8,128)S(1)} %bitcast.22), channel_id=1, replica_groups=mesh['x'=4,'core'=2,'z'=4,'y'=4] {'x','z','y'}, dimensions={0} | all-to-all | bytes 2097152 | tf_op jit(solution)/shard_map/cond/branch_1_fun/all_to_all | solution.py:499
  79.4 1.3 %shard_map.82 = f32[64,16,256]{2,1,0:T(8,128)} custom-call(f32[64,16,256]{2,1,0:T(8,128)S(1)} %get-tuple-element.47.parts), custom_call_target="tpu_custom_call" | custom-call | bytes 2097152 | tf_op jit(solution)/shard_map/pallas_call | solution.py:486
  80.7 7.5 %all-to-all-start.3 = ((f32[64,16,256]{2,1,0:T(8,128)}), f32[64,16,256]{2,1,0:T(8,128)S(1)}, u32[]{:S(2)}, u32[]{:S(2)}) async-start(f32[64,16,256]{2,1,0:T(8,128)} %shard_map.82), calls=%async_computation.3 | async-start | bytes 2097152 | tf_op jit(solution)/shard_map/all_to_all | solution.py:555
  88.2 4.9 %shard_map.83 = f32[2,512,512]{2,1,0:T(8,128)} custom-call(s32[2,128]{1,0:T(2,128)} %bitcast.17, f32[8,128]{1,0:T(8,128)} %copy-done.4, f32[2,512,512]{2,1,0:T(8,128)} %tile.5, f32[2,256,256]{2,1,0:T(8,128)} %copy-done.2, f32[2,256,256]{2,1,0:T(8,128)} %collective-permute-done.4.got, f32[2,256,256]{2,1,0:T(8,128)} %collective-permute-done.5.above_first, ...), custom_call_target="tpu_custom_call" | custom-call | bytes 6291456 | tf_op jit(solution)/shard_map/pallas_call | solution.py:486
  93.1 11.4 %all-to-all-done.3 = f32[64,16,256]{2,1,0:T(8,128)S(1)} async-done(((f32[64,16,256]{2,1,0:T(8,128)}), f32[64,16,256]{2,1,0:T(8,128)S(1)}, u32[]{:S(2)}, u32[]{:S(2)}) %all-to-all-start.3) | async-done | bytes 1048608 | tf_op jit(solution)/shard_map/all_to_all | solution.py:555
  104.6 3.1 %collective-permute-start.7 = (f32[2,2,256,256]{3,2,1,0:T(8,128)S(1)}, f32[2,2,256,256]{3,2,1,0:T(8,128)S(1)}, u32[]{:S(2)}, u32[]{:S(2)}) collective-permute-start(f32[2,2,256,256]{3,2,1,0:T(8,128)S(1)} %bitcast.11), channel_id=1, source_target_pairs={{0,16},{1,17},{2,18},{3,19},{4,20},{5,21},{6,22},{7,23},{8,24},{9,... | collective-permute-start | bytes 3145736 | tf_op jit(solution)/shard_map/ppermute | solution.py:563
  107.7 1.6 %copy-done = f32[4,2,256,256]{3,2,1,0:T(8,128)S(1)} copy-done((f32[4,2,256,256]{3,2,1,0:T(8,128)S(1)}, f32[4,2,256,256]{3,2,1,0:T(8,128)}, u32[]{:S(2)}) %copy-start) | copy-done | bytes 2097176
  (32 shorter events, 6.3 us)
Async XLA Ops:
  0.6 3.6 %copy-start.7 = (f32[3,256,256]{2,1,0:T(8,128)S(1)}, f32[3,256,256]{2,1,0:T(8,128)}, u32[]{:S(2)}) copy-start(f32[3,256,256]{2,1,0:T(8,128)} %param.10) | copy-start | bytes 2359300
  2.8 12.9 %collective-permute-start = (f32[2,256,256]{2,1,0:T(8,128)}, f32[2,256,256]{2,1,0:T(8,128)S(1)}, u32[]{:S(2)}, u32[]{:S(2)}) collective-permute-start(f32[2,256,256]{2,1,0:T(8,128)} %get-tuple-element.30), channel_id=1, source_target_pairs={{0,112},{1,113},{2,114},{3,115},{4,116},{5,117},{6,118},{7,119},{8... | collective-permute-start | bytes 1572872 | tf_op jit(solution)/shard_map/ppermute | solution.py:515
  5.2 20.0 %copy-start.5 = (s32[128]{0:T(128)S(1)}, s32[128]{0:T(128)}, u32[]{:S(2)}) copy-start(s32[128]{0:T(128)} %param.12) | copy-start | bytes 1540
  5.2 20.0 %all-to-all-start.1 = ((f32[16,3,16,256]{3,2,1,0:T(8,128)}), f32[16,3,16,256]{3,2,1,0:T(8,128)S(1)}, u32[]{:S(2)}, u32[]{:S(2)}) async-start(f32[16,3,16,256]{3,2,1,0:T(8,128)} %bitcast.10), calls=%async_computation.1 | async-start | bytes 1572864 | tf_op jit(solution)/shard_map/all_to_all | solution.py:523
  13.2 20.0 %copy-start.1 = (bf16[10,256,256]{2,1,0:T(8,128)(2,1)S(1)}, bf16[10,256,256]{2,1,0:T(8,128)(2,1)}, u32[]{:S(2)}) copy-start(bf16[10,256,256]{2,1,0:T(8,128)(2,1)} %constant.7.clone.tables) | copy-start | bytes 3932164
  13.2 20.0 %copy-start.3 = (s32[128,2]{0,1:T(2,128)S(1)}, s32[128,2]{0,1:T(2,128)}, u32[]{:S(2)}) copy-start(s32[128,2]{0,1:T(2,128)} %param.11) | copy-start | bytes 3076
  13.2 17.0 %collective-permute-start.1 = (f32[2,256,256]{2,1,0:T(8,128)}, f32[2,256,256]{2,1,0:T(8,128)S(1)}, u32[]{:S(2)}, u32[]{:S(2)}) collective-permute-start(f32[2,256,256]{2,1,0:T(8,128)} %get-tuple-element.32), channel_id=1, source_target_pairs={{0,112},{1,113},{2,114},{3,115},{4,116},{5,117},{6,118},{7,119},{8... | collective-permute-start | bytes 1572872 | tf_op jit(solution)/shard_map/ppermute | solution.py:516
  15.7 0.8 copy-start.9
  19.1 14.0 %collective-permute-start.2 = (f32[2,256,256]{2,1,0:T(8,128)}, f32[2,256,256]{2,1,0:T(8,128)}, u32[]{:S(2)}, u32[]{:S(2)}) collective-permute-start(f32[2,256,256]{2,1,0:T(8,128)} %get-tuple-element.33), channel_id=1, source_target_pairs={{0,15},{1,0},{2,1},{3,2},{4,3},{5,4},{6,5},{7,6},{8,7},{9,8},{10,9... | collective-permute-start | bytes 1572872 | tf_op jit(solution)/shard_map/ppermute | solution.py:521
  26.6 13.6 %all-to-all-start.2 = ((f32[16,16,256]{2,1,0:T(8,128)}), f32[16,16,256]{2,1,0:T(8,128)S(1)}, u32[]{:S(2)}, u32[]{:S(2)}) async-start(f32[16,16,256]{2,1,0:T(8,128)} %shard_map.77), calls=%async_computation.2 | async-start | bytes 524288 | tf_op jit(solution)/shard_map/all_to_all | solution.py:529
  33.2 1.0 copy-start.6
  39.7 0.6 copy-start.4
  47.1 10.1 %copy-start.2 = (f32[2,256,256]{2,1,0:T(8,128)}, f32[2,256,256]{2,1,0:T(8,128)S(1)}, u32[]{:S(2)}) copy-start(f32[2,256,256]{2,1,0:T(8,128)S(1)} %get-tuple-element.39.own) | copy-start | bytes 1572868
  47.1 10.1 %collective-permute-start.3 = (f32[2,2,256,256]{3,2,1,0:T(8,128)S(1)}, f32[2,2,256,256]{3,2,1,0:T(8,128)S(1)}, u32[]{:S(2)}, u32[]{:S(2)}) collective-permute-start(f32[2,2,256,256]{3,2,1,0:T(8,128)S(1)} %get-tuple-element.38), channel_id=1, source_target_pairs={{0,16},{1,17},{2,18},{3,19},{4,20},{5,21},{6,22},{7,23},{8,24},{9,... | collective-permute-start | bytes 3145736 | tf_op jit(solution)/shard_map/ppermute | solution.py:544
  50.3 29.0 %collective-permute-start.6 = (f32[2,256,256]{2,1,0:T(8,128)S(1)}, f32[2,256,256]{2,1,0:T(8,128)S(1)}, u32[]{:S(2)}, u32[]{:S(2)}) collective-permute-start(f32[2,256,256]{2,1,0:T(8,128)S(1)} %get-tuple-element.39.own), channel_id=1, source_target_pairs={{113,0},{114,1},{115,2},{116,3},{117,4},{118,5},{119,6},{120,7},{1... | collective-permute-start | bytes 1572872 | tf_op jit(solution)/shard_map/ppermute | solution.py:547
  54.1 25.3 %collective-permute-start.5 = (f32[2,256,256]{2,1,0:T(8,128)S(1)}, f32[2,256,256]{2,1,0:T(8,128)}, u32[]{:S(2)}, u32[]{:S(2)}) collective-permute-start(f32[2,256,256]{2,1,0:T(8,128)S(1)} %get-tuple-element.39.own), channel_id=1, source_target_pairs={{112,0},{113,1},{114,2},{115,3},{116,4},{117,5},{118,6},{119,7},{1... | collective-permute-start | bytes 1572872 | tf_op jit(solution)/shard_map/ppermute | solution.py:546
  54.1 25.3 %collective-permute-start.4 = (f32[2,256,256]{2,1,0:T(8,128)S(1)}, f32[2,256,256]{2,1,0:T(8,128)}, u32[]{:S(2)}, u32[]{:S(2)}) collective-permute-start(f32[2,256,256]{2,1,0:T(8,128)S(1)} %get-tuple-element.39.own), channel_id=1, source_target_pairs={{15,0},{0,1},{1,2},{2,3},{3,4},{4,5},{5,6},{6,7},{7,8},{8,9},{9,10... | collective-permute-start | bytes 1572872 | tf_op jit(solution)/shard_map/ppermute | solution.py:545
  79.4 1.3 %copy-start.8 = (f32[2,256,256]{2,1,0:T(8,128)}, f32[2,256,256]{2,1,0:T(8,128)S(1)}, u32[]{:S(2)}) copy-start(f32[2,256,256]{2,1,0:T(8,128)S(1)} %collective-permute-done.6.above_second) | copy-start | bytes 1572868
  80.7 23.9 %all-to-all-start.3 = ((f32[64,16,256]{2,1,0:T(8,128)}), f32[64,16,256]{2,1,0:T(8,128)S(1)}, u32[]{:S(2)}, u32[]{:S(2)}) async-start(f32[64,16,256]{2,1,0:T(8,128)} %shard_map.82), calls=%async_computation.3 | async-start | bytes 2097152 | tf_op jit(solution)/shard_map/all_to_all | solution.py:555
  104.6 5.9 %collective-permute-start.7 = (f32[2,2,256,256]{3,2,1,0:T(8,128)S(1)}, f32[2,2,256,256]{3,2,1,0:T(8,128)S(1)}, u32[]{:S(2)}, u32[]{:S(2)}) collective-permute-start(f32[2,2,256,256]{3,2,1,0:T(8,128)S(1)} %bitcast.11), channel_id=1, source_target_pairs={{0,16},{1,17},{2,18},{3,19},{4,20},{5,21},{6,22},{7,23},{8,24},{9,... | collective-permute-start | bytes 3145736 | tf_op jit(solution)/shard_map/ppermute | solution.py:563
  107.7 1.6 %copy-start = (f32[4,2,256,256]{3,2,1,0:T(8,128)S(1)}, f32[4,2,256,256]{3,2,1,0:T(8,128)}, u32[]{:S(2)}) copy-start(f32[4,2,256,256]{3,2,1,0:T(8,128)} %probe.7) | copy-start | bytes 6291460

commit v6 on v5

--- a/solution.py
+++ b/solution.py
@@ -95,26 +95,23 @@
     return copies
 
 
-def send_up_kernel(offs_hbm, tile, first, second, offs, t_buf, f_buf, s_buf, sems):
+def send_up_kernel(offs_hbm, tile, first, offs, t_buf, f_buf, sems):
     row, col, core = coords()
     loads = fetch([(offs_hbm, offs)] + [(tile.at[i, pl.ds(0, W)], t_buf.at[i]) for i in range(2)], sems)
     loads[0].wait()
     _, c = corner(offs, row - 1, col)
     b = iota((W, W), 1)
     c1 = jnp.where(core == 1, 0, c)
-    c2 = jnp.where(core == 1, c, 0)
     stores = []
     for i in range(2):
         loads[1 + i].wait()
         f_buf[i] = jnp.where(b >= c1, t_buf[i, :, :W], t_buf[i, :, W:])
-        stores += fetch([(f_buf.at[i], first.at[i])], sems.at[pl.ds(3 + 2 * i, 1)])
-        s_buf[i] = jnp.where(b >= c2, t_buf[i, :, :W], t_buf[i, :, W:])
-        stores += fetch([(s_buf.at[i], second.at[i])], sems.at[pl.ds(4 + 2 * i, 1)])
-    for copy in stores:
-        copy.wait()
-
-
-def send_side_kernel(offs_hbm, tile, below, side, own, offs, t_buf, b_buf, o_buf, w_buf, sems):
+        stores += fetch([(f_buf.at[i], first.at[i])], sems.at[pl.ds(3 + i, 1)])
+    for copy in stores:
+        copy.wait()
+
+
+def send_side_kernel(offs_hbm, tile, below, side, own, second, offs, t_buf, b_buf, o_buf, w_buf, u_buf, sems):
     row, col, core = coords()
     loads = fetch([(offs_hbm, offs)], sems)
     for i in range(2):
@@ -123,6 +120,8 @@
     even = core == 0
     r_s, c_s = corner(offs, row, col)
     r_b, _ = corner(offs, row, col - 1)
+    _, c_up = corner(offs, row - 1, col)
+    c_up = jnp.where(even, 0, c_up)
     r_side, c_side = jnp.where(even, r_b, r_s), jnp.where(even, 0, c_s)
     r_own, c_own = jnp.where(even, r_s, r_b), jnp.where(even, c_s, 0)
     a = iota((W, W), 0)
@@ -139,6 +138,8 @@
         low = jnp.where(b >= c_own, t_buf[i, W:, :W], t_buf[i, W:, W:])
         w_buf[i] = jnp.where(a >= r_own, top, low)
         stores += fetch([(w_buf.at[i], own.at[i])], sems.at[pl.ds(6 + 2 * i, 1)])
+        u_buf[i] = jnp.where(b >= c_up, t_buf[i, :W, :W], t_buf[i, :W, W:])
+        stores += fetch([(u_buf.at[i], second.at[i])], sems.at[pl.ds(9 + i, 1)])
     for copy in stores:
         copy.wait()
 
@@ -508,17 +509,17 @@
     table_buf = pltpu.VMEM(tables.shape, BF)
     offs_buf = pltpu.SMEM(offsets.shape, jnp.int32)
     owner_buf = pltpu.SMEM(owner.shape, jnp.int32)
-    first, second = call(
-        send_up_kernel, [PIECE] * 2, [HBM] * 2, [offs_buf, (2, W, TILE), PIECE, PIECE], 7,
+    first = call(
+        send_up_kernel, [PIECE], [HBM] * 2, [offs_buf, (2, W, TILE), PIECE], 5,
         offsets, object_field, data=3 << 20,
-    )
+    )[0]
     below_first = lax.ppermute(first, ALL, UP)
-    below = lax.ppermute(second, ALL, UP)
-    side, own = call(
-        send_side_kernel, [PIECE] * 2, [HBM] * 3, [offs_buf, (2, TILE, TILE), PIECE, PIECE, PIECE], 9,
+    side, own, second = call(
+        send_side_kernel, [PIECE] * 3, [HBM] * 3, [offs_buf, (2, TILE, TILE), PIECE, PIECE, PIECE, PIECE], 11,
         offsets, object_field, below_first, data=4 << 20, mb=54,
     )
     side = lax.ppermute(side, ALL, SIDE)
+    below = lax.ppermute(second, ALL, UP)
     spread = measured.reshape(CAP, NC, CHUNK, W).transpose(1, 0, 2, 3)
     spread = lax.all_to_all(spread, COL, 0, 0, tiled=True)
     slots = (NC * CAP, CHUNK, W)

time: 113 us -> 112 us (level)
  starting transfers between devices: 36.7 us -> 37.9 us
where the time goes in v6:
time: 112 us
  starting transfers between devices  37.9 us (34%)
  Pallas kernels  27.2 us (24%)
  blocking collectives  19.9 us (18%)
  waiting for transfers between devices  18.4 us (16%)
  local copies, waits for them, and re-layouts  5.48 us (5%)
  between operations  1.49 us (1%)
  other arithmetic  1.41 us (1%)
    pallas_call x9, Pallas kernels, call(): pl.pallas_call(kernel, out_shape=shapes, in_specs=ins, out_specs=out_spec...  27.2 us
    all_to_all x1, blocking collectives, exchange(): return lax.all_to_all(x, CHIPS, 0, 0, tiled=True)  19.9 us
    all_to_all x1, waiting for transfers between devices, shards(): mine = lax.all_to_all(copies, CHIPS, 0, 0, tiled=True)  11.1 us
    all_to_all x1, starting transfers between devices, shards(): mine = lax.all_to_all(copies, CHIPS, 0, 0, tiled=True)  8.36 us
    all_to_all x1, starting transfers between devices, shards(): spread = lax.all_to_all(spread, COL, 0, 0, tiled=True)  7.98 us
    all_to_all x1, waiting for transfers between devices, shards(): spread = lax.all_to_all(spread, COL, 0, 0, tiled=True)  4.29 us
    unnamed x20, local copies, waits for them, and re-layouts  4.03 us
    ppermute x1, starting transfers between devices, shards(): above_second = lax.ppermute(grad, ALL, back(SLANT))  3.8 us
  transfers between devices with their start and end apart: 11, of which 3 were waited for; matrix products, arithmetic and copies ran while one was open for 3% of the time, Pallas kernels for 14%

profile of v6, /device:TPU:1, one launch (start us, length us, event | category | flops | bytes accessed | tf_op | source)
XLA Modules:
  0.0 111.6 jit_solution(677791841352476418)
XLA Ops:
  0.6 2.0 %shard_map.78 = f32[2,256,256]{2,1,0:T(8,128)} custom-call(s32[2,128]{1,0:T(2,128)} %bitcast.15, f32[2,512,512]{2,1,0:T(8,128)} %tile.5), custom_call_target="tpu_custom_call" | custom-call | bytes 3145728 | tf_op jit(solution)/shard_map/pallas_call | solution.py:487
  2.7 1.4 %collective-permute-start = (f32[2,256,256]{2,1,0:T(8,128)}, f32[2,256,256]{2,1,0:T(8,128)S(1)}, u32[]{:S(2)}, u32[]{:S(2)}) collective-permute-start(f32[2,256,256]{2,1,0:T(8,128)} %shard_map.78), channel_id=1, source_target_pairs={{0,112},{1,113},{2,114},{3,115},{4,116},{5,117},{6,118},{7,119},{8... | collective-permute-start | bytes 1572872 | tf_op jit(solution)/shard_map/ppermute | solution.py:516
  5.1 8.0 %all-to-all-start.1 = ((f32[16,3,16,256]{3,2,1,0:T(8,128)}), f32[16,3,16,256]{3,2,1,0:T(8,128)S(1)}, u32[]{:S(2)}, u32[]{:S(2)}) async-start(f32[16,3,16,256]{3,2,1,0:T(8,128)} %bitcast.10), calls=%async_computation.1 | async-start | bytes 1572864 | tf_op jit(solution)/shard_map/all_to_all | solution.py:524
  13.9 2.8 %shard_map.79 = (f32[2,256,256]{2,1,0:T(8,128)}, f32[2,256,256]{2,1,0:T(8,128)}, f32[2,256,256]{2,1,0:T(8,128)}) custom-call(s32[2,128]{1,0:T(2,128)} %bitcast.16, f32[2,512,512]{2,1,0:T(8,128)} %tile.5, f32[2,256,256]{2,1,0:T(8,128)} %copy-done.9), custom_call_target="tpu_custom_call" | custom-call | bytes 4194304 | tf_op jit(solution)/shard_map/pallas_call | solution.py:487
  16.6 2.5 %collective-permute-start.1 = (f32[2,256,256]{2,1,0:T(8,128)}, f32[2,256,256]{2,1,0:T(8,128)S(1)}, u32[]{:S(2)}, u32[]{:S(2)}) collective-permute-start(f32[2,256,256]{2,1,0:T(8,128)} %get-tuple-element.30), channel_id=1, source_target_pairs={{0,112},{1,113},{2,114},{3,115},{4,116},{5,117},{6,118},{7,119},{8... | collective-permute-start | bytes 1572872 | tf_op jit(solution)/shard_map/ppermute | solution.py:522
  19.1 1.6 %collective-permute-start.2 = (f32[2,256,256]{2,1,0:T(8,128)}, f32[2,256,256]{2,1,0:T(8,128)}, u32[]{:S(2)}, u32[]{:S(2)}) collective-permute-start(f32[2,256,256]{2,1,0:T(8,128)} %get-tuple-element.31), channel_id=1, source_target_pairs={{0,15},{1,0},{2,1},{3,2},{4,3},{5,4},{6,5},{7,6},{8,7},{9,8},{10,9... | collective-permute-start | bytes 1572872 | tf_op jit(solution)/shard_map/ppermute | solution.py:521
  20.8 4.3 %all-to-all-done.1 = f32[16,3,16,256]{3,2,1,0:T(8,128)S(1)} async-done(((f32[16,3,16,256]{3,2,1,0:T(8,128)}), f32[16,3,16,256]{3,2,1,0:T(8,128)S(1)}, u32[]{:S(2)}, u32[]{:S(2)}) %all-to-all-start.1) | async-done | bytes 786464 | tf_op jit(solution)/shard_map/all_to_all | solution.py:524
  25.1 1.4 %shard_map.77 = f32[16,16,256]{2,1,0:T(8,128)} custom-call(s32[1,128]{1,0:T(1,128)S(1)} %bitcast.21, f32[48,16,256]{2,1,0:T(8,128)S(1)} %bitcast.13), custom_call_target="tpu_custom_call" | custom-call | bytes 1048576 | tf_op jit(solution)/shard_map/pallas_call | solution.py:487
  26.5 3.5 %all-to-all-start.2 = ((f32[16,16,256]{2,1,0:T(8,128)}), f32[16,16,256]{2,1,0:T(8,128)S(1)}, u32[]{:S(2)}, u32[]{:S(2)}) async-start(f32[16,16,256]{2,1,0:T(8,128)} %shard_map.77), calls=%async_computation.2 | async-start | bytes 524288 | tf_op jit(solution)/shard_map/all_to_all | solution.py:530
  30.1 3.0 %collective-permute-done.2.side = f32[2,256,256]{2,1,0:T(8,128)} collective-permute-done((f32[2,256,256]{2,1,0:T(8,128)}, f32[2,256,256]{2,1,0:T(8,128)}, u32[]{:S(2)}, u32[]{:S(2)}) %collective-permute-start.2) | collective-permute-done | bytes 524320 | tf_op jit(solution)/shard_map/ppermute | solution.py:521
  34.1 5.4 %shard_map.80 = (f32[4,2,256,256]{3,2,1,0:T(8,128)}, f32[256,256]{1,0:T(8,128)S(1)}, f32[2,256,256]{2,1,0:T(8,128)S(1)}, f32[8,128]{1,0:T(8,128)S(1)}) custom-call(s32[2,128]{1,0:T(2,128)S(1)} %bitcast.18, f32[2,256,256]{2,1,0:T(8,128)S(1)} %copy-done.6, f32[2,256,256]{2,1,0:T(8,128)S(1)} %collective-permute-done.1.below, ...), custom_call_target="tpu_custom_call" | custom-call | flops 1610612736 | bytes 8388608 | tf_op jit(solution)/shard_map/pallas_call | solution.py:487
  40.1 6.8 %shard_map.81 = (f32[2,256,256]{2,1,0:T(8,128)S(1)}, f32[2,2,256,256]{3,2,1,0:T(8,128)S(1)}, f32[2,2,256,256]{3,2,1,0:T(8,128)}) custom-call(s32[2,128]{1,0:T(2,128)S(1)} %bitcast.19, f32[256,256]{1,0:T(8,128)S(1)} %bitcast.14, f32[4,2,256,256]{3,2,1,0:T(8,128)} %get-tuple-element.32.far, f32[256,256]{1,0:T(8,128)S(1)} %get-tuple-element.33.mag, ...), custom_call_target="tpu_custom_call" | custom-call | flops 1610612736 | bytes 8388608 | tf_op jit(solution)/shard_map/pallas_call | solution.py:487
  47.0 3.2 %collective-permute-start.3 = (f32[2,2,256,256]{3,2,1,0:T(8,128)S(1)}, f32[2,2,256,256]{3,2,1,0:T(8,128)S(1)}, u32[]{:S(2)}, u32[]{:S(2)}) collective-permute-start(f32[2,2,256,256]{3,2,1,0:T(8,128)S(1)} %get-tuple-element.36), channel_id=1, source_target_pairs={{0,16},{1,17},{2,18},{3,19},{4,20},{5,21},{6,22},{7,23},{8,24},{9,... | collective-permute-start | bytes 3145736 | tf_op jit(solution)/shard_map/ppermute | solution.py:545
  50.2 3.8 %collective-permute-start.6 = (f32[2,256,256]{2,1,0:T(8,128)S(1)}, f32[2,256,256]{2,1,0:T(8,128)S(1)}, u32[]{:S(2)}, u32[]{:S(2)}) collective-permute-start(f32[2,256,256]{2,1,0:T(8,128)S(1)} %get-tuple-element.37.own), channel_id=1, source_target_pairs={{113,0},{114,1},{115,2},{116,3},{117,4},{118,5},{119,6},{120,7},{1... | collective-permute-start | bytes 1572872 | tf_op jit(solution)/shard_map/ppermute | solution.py:548
  54.0 2.0 %collective-permute-start.4 = (f32[2,256,256]{2,1,0:T(8,128)S(1)}, f32[2,256,256]{2,1,0:T(8,128)}, u32[]{:S(2)}, u32[]{:S(2)}) collective-permute-start(f32[2,256,256]{2,1,0:T(8,128)S(1)} %get-tuple-element.37.own), channel_id=1, source_target_pairs={{15,0},{0,1},{1,2},{2,3},{3,4},{4,5},{5,6},{6,7},{7,8},{8,9},{9,10... | collective-permute-start | bytes 1572872 | tf_op jit(solution)/shard_map/ppermute | solution.py:546
  57.1 21.3 %conditional.1 = (f32[64,16,256]{2,1,0:T(8,128)S(1)}) conditional(s32[]{:T(128)} %bitcast.2, () %tuple.17, (f32[2,2,256,256]{3,2,1,0:T(8,128)}, f32[2,2,256,256]{3,2,1,0:T(8,128)S(1)}) %tuple.18), branch_computations={%region_0.0_spmd, %region_1.0_spmd} | conditional | flops 262144 | bytes 5242888 | solution.py:551
  57.1 1.4 %add.3 = f32[2,2,256,256]{3,2,1,0:T(8,128)S(1)} add(f32[2,2,256,256]{3,2,1,0:T(8,128)} %get-tuple-element.9, f32[2,2,256,256]{3,2,1,0:T(8,128)S(1)} %get-tuple-element.10) | non-fusion elementwise | flops 262144 | bytes 3145728 | tf_op jit(solution)/shard_map/add | solution.py:549
  58.5 19.9 %all_to_all.19 = f32[64,16,256]{2,1,0:T(8,128)S(1)} all-to-all(f32[64,16,256]{2,1,0:T(8,128)S(1)} %bitcast.22), channel_id=1, replica_groups=mesh['x'=4,'core'=2,'z'=4,'y'=4] {'x','z','y'}, dimensions={0} | all-to-all | bytes 2097152 | tf_op jit(solution)/shard_map/cond/branch_1_fun/all_to_all | solution.py:500
  78.4 1.3 %shard_map.82 = f32[64,16,256]{2,1,0:T(8,128)} custom-call(f32[64,16,256]{2,1,0:T(8,128)S(1)} %get-tuple-element.45.parts), custom_call_target="tpu_custom_call" | custom-call | bytes 2097152 | tf_op jit(solution)/shard_map/pallas_call | solution.py:487
  79.7 8.4 %all-to-all-start.3 = ((f32[64,16,256]{2,1,0:T(8,128)}), f32[64,16,256]{2,1,0:T(8,128)S(1)}, u32[]{:S(2)}, u32[]{:S(2)}) async-start(f32[64,16,256]{2,1,0:T(8,128)} %shard_map.82), calls=%async_computation.3 | async-start | bytes 2097152 | tf_op jit(solution)/shard_map/all_to_all | solution.py:556
  88.1 4.9 %shard_map.83 = f32[2,512,512]{2,1,0:T(8,128)} custom-call(s32[2,128]{1,0:T(2,128)} %bitcast.17, f32[8,128]{1,0:T(8,128)} %copy-done.4, f32[2,512,512]{2,1,0:T(8,128)} %tile.5, f32[2,256,256]{2,1,0:T(8,128)} %copy-done.2, f32[2,256,256]{2,1,0:T(8,128)} %collective-permute-done.4.got, f32[2,256,256]{2,1,0:T(8,128)} %collective-permute-done.5.above_first, ...), custom_call_target="tpu_custom_call" | custom-call | bytes 6291456 | tf_op jit(solution)/shard_map/pallas_call | solution.py:487
  93.0 11.1 %all-to-all-done.3 = f32[64,16,256]{2,1,0:T(8,128)S(1)} async-done(((f32[64,16,256]{2,1,0:T(8,128)}), f32[64,16,256]{2,1,0:T(8,128)S(1)}, u32[]{:S(2)}, u32[]{:S(2)}) %all-to-all-start.3) | async-done | bytes 1048608 | tf_op jit(solution)/shard_map/all_to_all | solution.py:556
  104.1 3.5 %collective-permute-start.7 = (f32[2,2,256,256]{3,2,1,0:T(8,128)S(1)}, f32[2,2,256,256]{3,2,1,0:T(8,128)S(1)}, u32[]{:S(2)}, u32[]{:S(2)}) collective-permute-start(f32[2,2,256,256]{3,2,1,0:T(8,128)S(1)} %bitcast.11), channel_id=1, source_target_pairs={{0,16},{1,17},{2,18},{3,19},{4,20},{5,21},{6,22},{7,23},{8,24},{9,... | collective-permute-start | bytes 3145736 | tf_op jit(solution)/shard_map/ppermute | solution.py:564
  107.6 1.6 %copy-done = f32[4,2,256,256]{3,2,1,0:T(8,128)S(1)} copy-done((f32[4,2,256,256]{3,2,1,0:T(8,128)S(1)}, f32[4,2,256,256]{3,2,1,0:T(8,128)}, u32[]{:S(2)}) %copy-start) | copy-done | bytes 2097176
  (32 shorter events, 6.4 us)
Async XLA Ops:
  0.6 3.5 %copy-start.7 = (f32[3,256,256]{2,1,0:T(8,128)S(1)}, f32[3,256,256]{2,1,0:T(8,128)}, u32[]{:S(2)}) copy-start(f32[3,256,256]{2,1,0:T(8,128)} %param.10) | copy-start | bytes 2359300
  2.7 10.4 %collective-permute-start = (f32[2,256,256]{2,1,0:T(8,128)}, f32[2,256,256]{2,1,0:T(8,128)S(1)}, u32[]{:S(2)}, u32[]{:S(2)}) collective-permute-start(f32[2,256,256]{2,1,0:T(8,128)} %shard_map.78), channel_id=1, source_target_pairs={{0,112},{1,113},{2,114},{3,115},{4,116},{5,117},{6,118},{7,119},{8... | collective-permute-start | bytes 1572872 | tf_op jit(solution)/shard_map/ppermute | solution.py:516
  5.1 20.0 %copy-start.5 = (s32[128]{0:T(128)S(1)}, s32[128]{0:T(128)}, u32[]{:S(2)}) copy-start(s32[128]{0:T(128)} %param.12) | copy-start | bytes 1540
  5.1 20.0 %all-to-all-start.1 = ((f32[16,3,16,256]{3,2,1,0:T(8,128)}), f32[16,3,16,256]{3,2,1,0:T(8,128)S(1)}, u32[]{:S(2)}, u32[]{:S(2)}) async-start(f32[16,3,16,256]{3,2,1,0:T(8,128)} %bitcast.10), calls=%async_computation.1 | async-start | bytes 1572864 | tf_op jit(solution)/shard_map/all_to_all | solution.py:524
  13.1 20.0 %copy-start.1 = (bf16[10,256,256]{2,1,0:T(8,128)(2,1)S(1)}, bf16[10,256,256]{2,1,0:T(8,128)(2,1)}, u32[]{:S(2)}) copy-start(bf16[10,256,256]{2,1,0:T(8,128)(2,1)} %constant.7.clone.tables) | copy-start | bytes 3932164
  13.1 20.0 %copy-start.3 = (s32[128,2]{0,1:T(2,128)S(1)}, s32[128,2]{0,1:T(2,128)}, u32[]{:S(2)}) copy-start(s32[128,2]{0,1:T(2,128)} %param.11) | copy-start | bytes 3076
  13.1 0.8 copy-start.9
  16.6 13.4 %collective-permute-start.1 = (f32[2,256,256]{2,1,0:T(8,128)}, f32[2,256,256]{2,1,0:T(8,128)S(1)}, u32[]{:S(2)}, u32[]{:S(2)}) collective-permute-start(f32[2,256,256]{2,1,0:T(8,128)} %get-tuple-element.30), channel_id=1, source_target_pairs={{0,112},{1,113},{2,114},{3,115},{4,116},{5,117},{6,118},{7,119},{8... | collective-permute-start | bytes 1572872 | tf_op jit(solution)/shard_map/ppermute | solution.py:522
  19.1 13.9 %collective-permute-start.2 = (f32[2,256,256]{2,1,0:T(8,128)}, f32[2,256,256]{2,1,0:T(8,128)}, u32[]{:S(2)}, u32[]{:S(2)}) collective-permute-start(f32[2,256,256]{2,1,0:T(8,128)} %get-tuple-element.31), channel_id=1, source_target_pairs={{0,15},{1,0},{2,1},{3,2},{4,3},{5,4},{6,5},{7,6},{8,7},{9,8},{10,9... | collective-permute-start | bytes 1572872 | tf_op jit(solution)/shard_map/ppermute | solution.py:521
  26.5 13.6 %all-to-all-start.2 = ((f32[16,16,256]{2,1,0:T(8,128)}), f32[16,16,256]{2,1,0:T(8,128)S(1)}, u32[]{:S(2)}, u32[]{:S(2)}) async-start(f32[16,16,256]{2,1,0:T(8,128)} %shard_map.77), calls=%async_computation.2 | async-start | bytes 524288 | tf_op jit(solution)/shard_map/all_to_all | solution.py:530
  33.1 1.0 copy-start.6
  39.6 0.6 copy-start.4
  47.0 10.1 %copy-start.2 = (f32[2,256,256]{2,1,0:T(8,128)}, f32[2,256,256]{2,1,0:T(8,128)S(1)}, u32[]{:S(2)}) copy-start(f32[2,256,256]{2,1,0:T(8,128)S(1)} %get-tuple-element.37.own) | copy-start | bytes 1572868
  47.0 10.1 %collective-permute-start.3 = (f32[2,2,256,256]{3,2,1,0:T(8,128)S(1)}, f32[2,2,256,256]{3,2,1,0:T(8,128)S(1)}, u32[]{:S(2)}, u32[]{:S(2)}) collective-permute-start(f32[2,2,256,256]{3,2,1,0:T(8,128)S(1)} %get-tuple-element.36), channel_id=1, source_target_pairs={{0,16},{1,17},{2,18},{3,19},{4,20},{5,21},{6,22},{7,23},{8,24},{9,... | collective-permute-start | bytes 3145736 | tf_op jit(solution)/shard_map/ppermute | solution.py:545
  50.2 28.2 %collective-permute-start.6 = (f32[2,256,256]{2,1,0:T(8,128)S(1)}, f32[2,256,256]{2,1,0:T(8,128)S(1)}, u32[]{:S(2)}, u32[]{:S(2)}) collective-permute-start(f32[2,256,256]{2,1,0:T(8,128)S(1)} %get-tuple-element.37.own), channel_id=1, source_target_pairs={{113,0},{114,1},{115,2},{116,3},{117,4},{118,5},{119,6},{120,7},{1... | collective-permute-start | bytes 1572872 | tf_op jit(solution)/shard_map/ppermute | solution.py:548
  54.0 24.4 %collective-permute-start.5 = (f32[2,256,256]{2,1,0:T(8,128)S(1)}, f32[2,256,256]{2,1,0:T(8,128)}, u32[]{:S(2)}, u32[]{:S(2)}) collective-permute-start(f32[2,256,256]{2,1,0:T(8,128)S(1)} %get-tuple-element.37.own), channel_id=1, source_target_pairs={{112,0},{113,1},{114,2},{115,3},{116,4},{117,5},{118,6},{119,7},{1... | collective-permute-start | bytes 1572872 | tf_op jit(solution)/shard_map/ppermute | solution.py:547
  54.0 24.4 %collective-permute-start.4 = (f32[2,256,256]{2,1,0:T(8,128)S(1)}, f32[2,256,256]{2,1,0:T(8,128)}, u32[]{:S(2)}, u32[]{:S(2)}) collective-permute-start(f32[2,256,256]{2,1,0:T(8,128)S(1)} %get-tuple-element.37.own), channel_id=1, source_target_pairs={{15,0},{0,1},{1,2},{2,3},{3,4},{4,5},{5,6},{6,7},{7,8},{8,9},{9,10... | collective-permute-start | bytes 1572872 | tf_op jit(solution)/shard_map/ppermute | solution.py:546
  78.4 1.3 %copy-start.8 = (f32[2,256,256]{2,1,0:T(8,128)}, f32[2,256,256]{2,1,0:T(8,128)S(1)}, u32[]{:S(2)}) copy-start(f32[2,256,256]{2,1,0:T(8,128)S(1)} %collective-permute-done.6.above_second) | copy-start | bytes 1572868
  79.7 24.4 %all-to-all-start.3 = ((f32[64,16,256]{2,1,0:T(8,128)}), f32[64,16,256]{2,1,0:T(8,128)S(1)}, u32[]{:S(2)}, u32[]{:S(2)}) async-start(f32[64,16,256]{2,1,0:T(8,128)} %shard_map.82), calls=%async_computation.3 | async-start | bytes 2097152 | tf_op jit(solution)/shard_map/all_to_all | solution.py:556
  104.1 6.3 %collective-permute-start.7 = (f32[2,2,256,256]{3,2,1,0:T(8,128)S(1)}, f32[2,2,256,256]{3,2,1,0:T(8,128)S(1)}, u32[]{:S(2)}, u32[]{:S(2)}) collective-permute-start(f32[2,2,256,256]{3,2,1,0:T(8,128)S(1)} %bitcast.11), channel_id=1, source_target_pairs={{0,16},{1,17},{2,18},{3,19},{4,20},{5,21},{6,22},{7,23},{8,24},{9,... | collective-permute-start | bytes 3145736 | tf_op jit(solution)/shard_map/ppermute | solution.py:564
  107.6 1.6 %copy-start = (f32[4,2,256,256]{3,2,1,0:T(8,128)S(1)}, f32[4,2,256,256]{3,2,1,0:T(8,128)}, u32[]{:S(2)}) copy-start(f32[4,2,256,256]{3,2,1,0:T(8,128)} %probe.7) | copy-start | bytes 6291460
